TPU v7x, 512 devices: a whole 4x8x8 slice. The times are simulated.
512 devices in a mesh: replica: 8 (over x, core), mp: 64 (over z, y).
Axes of the slice: x: 4, y: 8, z: 8, core: 2. Of those that a mesh axis runs over, the one named last changes fastest.
Arguments:
- gradient: bfloat16 [8, 4096, 8192], P('replica', 'mp'), may hold values from -6 to 6
- error: bfloat16 [8, 4096, 8192], P('replica', 'mp'), may hold values from -6 to 6
- q_prev: float32 [8192, 64], P('mp'), may hold values from -0.0625 to 0.0625
Outputs:
- new_error: bfloat16 [8, 4096, 8192], P('replica', 'mp')
- q_factor: float32 [8192, 64], P('mp')
- p_factor: float32 [4096, 64], P('mp')
All inputs are finite; a program needn't handle non-finite values.
Results may differ from a plain program's by a relative error of at most 0.001.
Values sent between devices are 32-bit elements; how exact they have to be, the bound alone decides.
No kernel may reach another device: no remote copies, remote signals or barrier semaphores. Data moves between devices by JAX's collectives and lax.ppermute only.
A program may use at most 64 MiB of HBM per device.

v0:
```python
import jax
import jax.numpy as jnp
from jax import lax
from jax.sharding import PartitionSpec as P


def partner(value, axis, apart):
    mask = 2**apart
    pairs = [(source, source ^ mask) for source in range(lax.axis_size(axis))]
    return lax.ppermute(value, axis, pairs)


def body(gradient, error, q_prev):
    highest = lax.Precision.HIGHEST
    replicas = lax.axis_size("replica")
    moment = gradient[0].astype(jnp.float32) + error[0].astype(jnp.float32)
    q_whole = lax.all_gather(q_prev, "mp", axis=0, tiled=True)
    p_local = jnp.dot(moment, q_whole, precision=highest)
    p_mean = lax.psum(p_local, "replica") / replicas
    gram_part = jnp.dot(p_mean.T, p_mean, precision=highest)
    levels = lax.axis_size("mp").bit_length() - 1
    for level in range(levels):
        gram_part = gram_part + partner(gram_part, "mp", level)
    lower_factor = jnp.linalg.cholesky(gram_part)
    p_factor = lax.linalg.triangular_solve(
        lower_factor, p_mean, left_side=False, lower=True, transpose_a=True
    )
    cols_dev = q_prev.shape[0]
    q_term = lax.dot_general(moment, p_factor, (((0,), (0,)), ((), ())), precision=highest)
    q_full = lax.psum(q_term, ("replica", "mp")) / replicas
    start = lax.axis_index("mp") * cols_dev
    q_factor = lax.dynamic_slice_in_dim(q_full, start, cols_dev, 0)
    update = jnp.dot(p_factor, q_full.T, precision=highest)
    new_error = (moment - update).astype(jnp.bfloat16)[None]
    return (new_error, q_factor, p_factor)


def solution(mesh):
    return jax.shard_map(
        body,
        mesh=mesh,
        in_specs=(P("replica", "mp", None), P("replica", "mp", None), P("mp", None)),
        out_specs=(P("replica", "mp", None), P("mp", None), P("mp", None)),
        check_vma=False,
    )
```

profile of v0, /device:TPU:1, one launch (start us, length us, event | category | flops | bytes accessed | tf_op | source)
XLA Modules:
  0.0 474.4 jit_solution(16538198692860800793)
XLA Ops:
  7.2 0.0 all-gather.2.cloned.1.call-start
  7.2 0.7 all-gather.2.cloned.1.call-update
  7.9 0.0 copy-start
  7.9 0.0 copy-start.1
  7.9 0.0 all-reduce.2.cloned.1.call-start
  8.0 88.4 %all-gather.2.cloned.1.call-done = f32[8192,64]{0,1:T(8,128)} async-done(((f32[128,64]{0,1:T(8,128)}), f32[8192,64]{0,1:T(8,128)}) %all-gather.2.cloned.1.call-update) | async-done | bytes 2097168 | tf_op jit(solution)/shard_map/all_gather | solution.py:17
  96.4 4.2 fusion.4
  100.6 24.4 %psum.14 = f32[64,64]{1,0:T(8,128)S(1)} all-reduce(f32[64,64]{1,0:T(8,128)S(1)} %fusion.4), channel_id=1, replica_groups=mesh['replica'=8,'mp'=64] {'replica'}, use_global_device_ids=true, to_apply=%region_0.0 | all-reduce | flops 4096 | bytes 32768 | tf_op jit(solution)/shard_map/psum | solution.py:19
  125.0 0.2 fusion.11
  125.3 3.1 collective-permute-start
  128.4 1.6 collective-permute-done
  130.0 3.2 collective-permute-start.1
  133.1 2.4 collective-permute-done.1
  135.5 4.1 collective-permute-start.2
  139.6 4.5 collective-permute-done.2
  144.1 2.6 collective-permute-start.3
  146.7 2.3 collective-permute-done.3
  149.0 3.4 collective-permute-start.4
  152.5 2.1 collective-permute-done.4
  154.6 4.1 collective-permute-start.5
  158.7 4.4 collective-permute-done.5
  163.1 0.1 copy.8
  163.2 5.8 %cholesky.16 = f32[64,64]{1,0:T(8,128)S(1)} custom-call(f32[64,64]{1,0:T(8,128)S(1)} %fusion.9), custom_call_target="Cholesky" | custom-call | tf_op jit(solution)/shard_map/jit(cholesky)/cholesky | solution.py:24
  169.1 0.6 compare_reduce_fusion
  169.8 0.7 fusion.6
  170.4 4.9 %custom-call.6 = f32[1,64,64]{1,2,0:T(8,128)S(1)} custom-call(f32[1,64,64]{2,1,0:T(8,128)S(1)} %fusion.6), custom_call_target="InvertDiagBlocksLowerTriangular" | custom-call | tf_op jit(solution)/shard_map/triangular_solve | solution.py:25
  175.3 0.2 fusion.7
  175.5 0.0 copy-done
  175.5 0.0 copy-done.1
  175.5 0.0 copy-start.3
  175.5 3.6 fusion.2
  179.1 0.0 all-reduce.2.cloned.1.call-update
  179.1 283.1 %all-reduce.2.cloned.1.call-done = f32[8192,64]{0,1:T(8,128)} async-done(((f32[8192,64]{0,1:T(8,128)}), f32[8192,64]{0,1:T(8,128)}) %all-reduce.2.cloned.1.call-update) | async-done | bytes 2097168 | tf_op jit(solution)/shard_map/psum | solution.py:30
  462.2 0.0 copy-start.2
  462.2 1.9 broadcast_multiply_fusion
  464.1 0.6 constant_dynamic-slice_fusion
  464.7 0.0 copy-done.3
  464.7 0.0 copy-done.2
  464.7 2.9 fusion.1
  (8 shorter events, 0.1 us)
Async XLA Ops:
  7.2 89.2 %all-gather.2.cloned.1.call-start = ((), (), s32[]{:S(2)}) async-start(), calls=%async_computation | async-start | bytes 2129920 | tf_op jit(solution)/shard_map/all_gather | solution.py:17
  7.9 167.6 %copy-start = (bf16[1,64,8192]{2,1,0:T(8,128)(2,1)S(1)}, bf16[1,64,8192]{2,1,0:T(8,128)(2,1)}, u32[]{:S(2)}) copy-start(bf16[1,64,8192]{2,1,0:T(8,128)(2,1)} %param.4) | copy-start | bytes 3145732
  7.9 167.6 %copy-start.1 = (bf16[1,64,8192]{2,1,0:T(8,128)(2,1)S(1)}, bf16[1,64,8192]{2,1,0:T(8,128)(2,1)}, u32[]{:S(2)}) copy-start(bf16[1,64,8192]{2,1,0:T(8,128)(2,1)} %param.3) | copy-start | bytes 3145732
  7.9 454.3 %all-reduce.2.cloned.1.call-start = ((), (), s32[]{:S(2)}) async-start(), calls=%async_computation.1 | async-start | bytes 4194304 | tf_op jit(solution)/shard_map/psum | solution.py:30
  125.3 4.7 collective-permute-start
  130.0 5.5 %collective-permute-start.1 = (f32[64,64]{0,1:T(8,128)S(1)}, f32[64,64]{0,1:T(8,128)S(1)}, u32[]{:S(2)}, u32[]{:S(2)}) collective-permute-start(f32[64,64]{0,1:T(8,128)S(1)} %add.44), channel_id=1, source_target_pairs={{0,2},{1,3},{2,0},{3,1},{4,6},{5,7},{6,4},{7,5},{8,10},{9,11},{10,... | collective-permute-start | bytes 49160 | tf_op jit(solution)/shard_map/ppermute | solution.py:10
  135.5 8.6 %collective-permute-start.2 = (f32[64,64]{0,1:T(8,128)S(1)}, f32[64,64]{0,1:T(8,128)S(1)}, u32[]{:S(2)}, u32[]{:S(2)}) collective-permute-start(f32[64,64]{0,1:T(8,128)S(1)} %add.45), channel_id=1, source_target_pairs={{0,4},{1,5},{2,6},{3,7},{4,0},{5,1},{6,2},{7,3},{8,12},{9,13},{10,... | collective-permute-start | bytes 49160 | tf_op jit(solution)/shard_map/ppermute | solution.py:10
  144.1 4.9 %collective-permute-start.3 = (f32[64,64]{0,1:T(8,128)S(1)}, f32[64,64]{0,1:T(8,128)S(1)}, u32[]{:S(2)}, u32[]{:S(2)}) collective-permute-start(f32[64,64]{0,1:T(8,128)S(1)} %add.46), channel_id=1, source_target_pairs={{0,8},{1,9},{2,10},{3,11},{4,12},{5,13},{6,14},{7,15},{8,0},{9,1},... | collective-permute-start | bytes 49160 | tf_op jit(solution)/shard_map/ppermute | solution.py:10
  149.0 5.5 %collective-permute-start.4 = (f32[64,64]{0,1:T(8,128)S(1)}, f32[64,64]{0,1:T(8,128)S(1)}, u32[]{:S(2)}, u32[]{:S(2)}) collective-permute-start(f32[64,64]{0,1:T(8,128)S(1)} %add.47), channel_id=1, source_target_pairs={{0,16},{1,17},{2,18},{3,19},{4,20},{5,21},{6,22},{7,23},{8,24},{9,... | collective-permute-start | bytes 49160 | tf_op jit(solution)/shard_map/ppermute | solution.py:10
  154.6 8.6 %collective-permute-start.5 = (f32[64,64]{0,1:T(8,128)S(1)}, f32[64,64]{0,1:T(8,128)S(1)}, u32[]{:S(2)}, u32[]{:S(2)}) collective-permute-start(f32[64,64]{0,1:T(8,128)S(1)} %add.48), channel_id=1, source_target_pairs={{0,32},{1,33},{2,34},{3,35},{4,36},{5,37},{6,38},{7,39},{8,40},{9,... | collective-permute-start | bytes 49160 | tf_op jit(solution)/shard_map/ppermute | solution.py:10
  175.5 289.2 %copy-start.3 = (f32[64,64]{1,0:T(8,128)}, f32[64,64]{1,0:T(8,128)S(1)}, u32[]{:S(2)}) copy-start(f32[64,64]{1,0:T(8,128)S(1)} %fusion.7) | copy-start | bytes 49156
  462.2 2.5 copy-start.2
Sparse Core Ops, SparseCore 0:
  11.0 85.3 all-gather.1
  179.2 282.8 all-reduce.1
where the time goes:
time: 475 us; the launch traced here: 474 us
  waiting for transfers between devices  389 us (82%)
  blocking collectives  24.4 us (5%)
  starting transfers between devices  20.6 us (4%)
  between operations  14.2 us (3%)
  other arithmetic  14 us (3%)
  matrix products  11.1 us (2%)
    psum x1, waiting for transfers between devices, body(): q_full = lax.psum(q_term, ('replica', 'mp')) / replicas  283 us
    all_gather x1, waiting for transfers between devices, body(): q_whole = lax.all_gather(q_prev, 'mp', axis=0, tiled=True)  88.4 us
    psum x1, blocking collectives, body(): p_mean = lax.psum(p_local, 'replica') / replicas  24.4 us
    ppermute x6, starting transfers between devices, partner(): return lax.ppermute(value, axis, pairs)  20.5 us
    ppermute x6, waiting for transfers between devices, partner(): return lax.ppermute(value, axis, pairs)  17.3 us
  transfers between devices with their start and end apart: 8, of which 8 were waited for; matrix products, arithmetic and copies ran while one was open for 0% of the time, Pallas kernels for 0%

commit v1 on v0

v1 whole, which is shorter than its diff:
```python
import functools

import jax
import jax.numpy as jnp
from jax import lax
from jax.experimental import pallas as pl
from jax.experimental.pallas import tpu as pltpu
from jax.sharding import PartitionSpec as P

HIGHEST = lax.Precision.HIGHEST
BLOCK = 128
CORES = 2


def exchange(value, axis, groups=None):
    return lax.all_to_all(value, axis, 0, 0, axis_index_groups=groups)


def spread(value, axis, groups=None):
    count = len(groups[0]) if groups else lax.axis_size(axis)
    return exchange(jnp.broadcast_to(value[None], (count,) + value.shape), axis, groups)


def swap_cores(value, replicas):
    return lax.ppermute(value, "replica", [(r, r ^ 1) for r in range(replicas)])


def fold(square):
    half = square.shape[0] // 2
    return jnp.concatenate([square[:half], square[half:]], axis=1)


def unfold(folded):
    half = folded.shape[1] // 2
    return jnp.concatenate([folded[:, :half], folded[:, half:]], axis=0)


def split_kernel(core_ref, g_keep, e_keep, g_give, e_give, keep, give):
    keep[0] = g_keep[0].astype(jnp.float32) + e_keep[0].astype(jnp.float32)
    give[0] = g_give[0].astype(jnp.float32) + e_give[0].astype(jnp.float32)


def split_moment(core, gradient, error, own):
    _, rows, cols = gradient.shape
    chips = cols // own // CORES
    keep = pl.BlockSpec((1, rows, own), lambda x, core: (0, 0, CORES * x + core[0]))
    give = pl.BlockSpec((1, rows, own), lambda x, core: (0, 0, CORES * x + 1 - core[0]))
    out = pl.BlockSpec((1, rows, own), lambda x, core: (x, 0, 0))
    shape = jax.ShapeDtypeStruct((chips, rows, own), jnp.float32)
    return pl.pallas_call(
        split_kernel,
        grid_spec=pltpu.PrefetchScalarGridSpec(
            num_scalar_prefetch=1, grid=(chips,),
            in_specs=[keep, keep, give, give], out_specs=[out, out]),
        out_shape=[shape, shape],
        cost_estimate=pl.CostEstimate(flops=rows * cols, bytes_accessed=8 * rows * cols, transcendentals=0),
        name="split_moment",
    )(core, gradient, error, gradient, error)


def update_kernel(core_ref, weights, mine, theirs, gradient, error, out):
    core = core_ref[0]
    groups = mine.shape[1]
    own = groups * BLOCK
    factor = weights[...]
    for c in range(CORES):
        for a in range(0, groups, 2):
            right = jnp.concatenate(
                [jnp.where(core == c, mine[0, k], theirs[0, k]) for k in (a, a + 1)], axis=1)
            change = jnp.dot(factor, right, precision=HIGHEST, preferred_element_type=jnp.float32)
            columns = slice(c * own + a * BLOCK, c * own + (a + 2) * BLOCK)
            moment = gradient[0, :, columns].astype(jnp.float32) + error[0, :, columns].astype(jnp.float32)
            out[0, :, columns] = (moment - change).astype(out.dtype)


def update_error(core, weights, mine, theirs, gradient, error):
    _, rows, cols = gradient.shape
    chips, groups, rank, _ = mine.shape
    wide = cols // chips
    whole = pl.BlockSpec(weights.shape, lambda x, core: (0, 0))
    chunk = pl.BlockSpec((1, groups, rank, BLOCK), lambda x, core: (x, 0, 0, 0))
    band = pl.BlockSpec((1, rows, wide), lambda x, core: (0, 0, x))
    return pl.pallas_call(
        update_kernel,
        grid_spec=pltpu.PrefetchScalarGridSpec(
            num_scalar_prefetch=1, grid=(chips,),
            in_specs=[whole, chunk, chunk, band, band], out_specs=band),
        out_shape=jax.ShapeDtypeStruct(gradient.shape, gradient.dtype),
        cost_estimate=pl.CostEstimate(
            flops=2 * rows * cols * rank, bytes_accessed=6 * rows * cols + 4 * rank * cols, transcendentals=0),
        name="update_error",
    )(core, weights, mine, theirs, gradient, error)


def body(gradient, error, q_prev):
    replicas = lax.axis_size("replica")
    shards = lax.axis_size("mp")
    rows, cols = gradient.shape[1:]
    rank = q_prev.shape[1]
    own = cols // replicas
    groups = own // BLOCK
    slab = rank // replicas
    replica = lax.axis_index("replica")
    shard = lax.axis_index("mp")
    core = lax.rem(replica, CORES)
    core_arg = core.astype(jnp.int32).reshape(1)
    chip_groups = [[c + CORES * x for x in range(replicas // CORES)] for c in range(CORES)]
    inner_groups = [[o * replicas + i for i in range(replicas)] for o in range(groups)]
    outer_groups = [[o * replicas + i for o in range(groups)] for i in range(replicas)]

    pairs = [
        (b * shards + r * groups + a, r * shards + a * replicas + b)
        for r in range(replicas) for a in range(groups) for b in range(replicas)
    ]
    tile = lax.dynamic_slice_in_dim(q_prev.T, replica * slab, slab, 0)
    tile = lax.ppermute(tile, ("replica", "mp"), pairs)
    q_block = spread(tile, "mp", inner_groups).reshape(rank, BLOCK)
    q_blocks = spread(q_block, "mp", outer_groups)
    q_own = q_blocks.transpose(1, 0, 2).reshape(rank, own)

    keep, give = split_moment(core_arg, gradient, error, own)
    pair_sum = keep + swap_cores(give, replicas)
    mean = exchange(pair_sum, "replica", chip_groups).sum(0) / replicas

    p_part = lax.dot_general(mean, q_own, (((1,), (1,)), ((), ())), precision=HIGHEST)
    p_mean = unfold(spread(fold(p_part), "replica").sum(0))

    s_part = lax.dot_general(p_mean, mean, (((0,), (0,)), ((), ())), precision=HIGHEST)
    s_part = s_part.reshape(replicas, slab, groups, BLOCK).transpose(2, 0, 1, 3)
    s_tile = exchange(s_part.reshape(shards, slab, BLOCK), "mp").sum(0)
    s_blocks = spread(s_tile, "mp").reshape(groups, rank, BLOCK)
    s_own = s_blocks.transpose(1, 0, 2).reshape(rank, own)
    gram_part = lax.dot_general(s_own, q_own, (((1,), (1,)), ((), ())), precision=HIGHEST)
    gram = unfold(spread(fold(gram_part), "replica").sum(0))
    mine = spread(s_blocks, "replica", chip_groups)
    theirs = swap_cores(mine, replicas)

    lower = jnp.linalg.cholesky(gram)
    p_factor = lax.linalg.triangular_solve(
        lower, p_mean, left_side=False, lower=True, transpose_a=True
    )
    weights = lax.linalg.triangular_solve(lower, p_factor, left_side=False, lower=True)
    owner, block = shard // groups, lax.rem(shard, groups)
    start = (owner // CORES, block, 0, 0)
    sizes = (1, 1, rank, BLOCK)
    s_block = jnp.where(
        lax.rem(owner, CORES) == core,
        lax.dynamic_slice(mine, start, sizes), lax.dynamic_slice(theirs, start, sizes))[0, 0]
    q_factor = lax.linalg.triangular_solve(lower, s_block, left_side=True, lower=True).T
    new_error = update_error(core_arg, weights, mine, theirs, gradient, error)
    return (new_error, q_factor, p_factor)


def solution(mesh):
    return jax.shard_map(
        body,
        mesh=mesh,
        in_specs=(P("replica", "mp", None), P("replica", "mp", None), P("mp", None)),
        out_specs=(P("replica", "mp", None), P("mp", None), P("mp", None)),
        check_vma=False,
    )
```

time: 475 us -> 174 us (0.37)
  waiting for transfers between devices: 389 us -> 31.7 us
  blocking collectives: 24.4 us -> 73.2 us
  starting transfers between devices: 20.6 us -> 36.6 us
  between operations: 14.2 us -> 0.87 us
  Pallas kernels: 0 us -> 8.91 us
  matrix products: 11.1 us -> 3.73 us
    psum x1 -> x0, waiting for transfers between devices: 283 us -> none  [body(): q_full = lax.psum(q_term, ('replica', 'mp')) / replicas]
    all_gather x1 -> x0, waiting for transfers between devices: 88.4 us -> none  [body(): q_whole = lax.all_gather(q_prev, 'mp', axis=0, tiled=True)]
    all_to_all x0 -> x5, blocking collectives: none -> 73.2 us  [exchange(): return lax.all_to_all(value, axis, 0, 0, axis_index_groups=groups)]
    all_to_all x0 -> x3, waiting for transfers between devices: none -> 28.6 us  [exchange(): return lax.all_to_all(value, axis, 0, 0, axis_index_groups=groups)]
    psum x1 -> x0, blocking collectives: 24.4 us -> none  [body(): p_mean = lax.psum(p_local, 'replica') / replicas]
    all_to_all x0 -> x3, starting transfers between devices: none -> 22.3 us  [exchange(): return lax.all_to_all(value, axis, 0, 0, axis_index_groups=groups)]
    ppermute x6 -> x3, waiting for transfers between devices: 17.3 us -> 3 us  [the longest x1 3 us: body(): tile = lax.ppermute(tile, ('replica', 'mp'), pairs)]
    dot_general x4 -> x3, matrix products: 10.9 us -> 1.13 us  [the longest x1 0.42 us: body(): lax.dot_general(p_mean, mean, (((0,), (0,)), ((), ())), precision=HIGHEST)]
  transfers between devices with their start and end apart: 8 -> 6, of which waited for: 8 -> 4; matrix products, arithmetic and copies ran while one was open for 0% -> 9% of each run, Pallas kernels for 0% -> 0%
where the time goes in v1:
time: 174 us; the launch traced here: 173 us
  blocking collectives  73.2 us (42%)
  starting transfers between devices  36.6 us (21%)
  waiting for transfers between devices  31.7 us (18%)
  other arithmetic  13.9 us (8%)
  Pallas kernels  8.91 us (5%)
  local copies, waits for them, and re-layouts  3.94 us (2%)
  matrix products  3.73 us (2%)
    all_to_all x5, blocking collectives, exchange(): return lax.all_to_all(value, axis, 0, 0, axis_index_groups=groups)  73.2 us
    all_to_all x3, waiting for transfers between devices, exchange(): return lax.all_to_all(value, axis, 0, 0, axis_index_groups=groups)  28.6 us
    all_to_all x3, starting transfers between devices, exchange(): return lax.all_to_all(value, axis, 0, 0, axis_index_groups=groups)  22.3 us
    ppermute x2, starting transfers between devices, swap_cores(): return lax.ppermute(value, 'replica', [(r, r ^ 1) for r in range(replicas)])  12.4 us
    another operation x3, other arithmetic, body(): lower = jnp.linalg.cholesky(gram)  6.52 us
    another operation x2, other arithmetic, body(): lax.linalg.triangular_solve(lower, p_mean, left_side=False, lower=True, t...  5.55 us
    pallas_call x1, Pallas kernels, update_error(): pl.pallas_call(update_kernel, grid_spec=pltpu.PrefetchScalarGridSpec(num_...  5.08 us
    pallas_call x1, Pallas kernels, split_moment(): pl.pallas_call(split_kernel, grid_spec=pltpu.PrefetchScalarGridSpec(num_s...  3.83 us
  transfers between devices with their start and end apart: 6, of which 4 were waited for; matrix products, arithmetic and copies ran while one was open for 9% of the time, Pallas kernels for 0%

profile of v1, /device:TPU:1, one launch (start us, length us, event | category | flops | bytes accessed | tf_op | source)
XLA Modules:
  0.0 172.8 jit_solution(13566430916836882330)
XLA Ops:
  0.6 0.0 copy-start
  0.7 3.8 %split_moment.1 = (f32[4,64,1024]{2,1,0:T(8,128)}, f32[4,64,1024]{2,1,0:T(8,128)}) custom-call(s32[1]{0:T(128)} %bitcast.core_ref, bf16[1,64,8192]{2,1,0:T(8,128)(2,1)} %gradient.1, bf16[1,64,8192]{2,1,0:T(8,128)(2,1)} %error.1, bf16[1,64,8192]{2,1,0:T(8,128)(2,1)} %gradient.1, bf16[1,64,8192]{2,1,0:T(8,128)(2,1)} %error.1), custom_call_target="tpu_custom_call" | custom-call | flops 524288 | bytes 4194304 | tf_op jit(solution)/shard_map/split_moment/pallas_call | solution.py:50
  4.5 8.8 %collective-permute-start = (f32[4,64,1024]{2,1,0:T(8,128)}, f32[4,64,1024]{2,1,0:T(8,128)S(1)}, u32[]{:S(2)}, u32[]{:S(2)}) collective-permute-start(f32[4,64,1024]{2,1,0:T(8,128)} %get-tuple-element.6), channel_id=1, source_target_pairs={{0,64},{64,0},{128,192},{192,128},{256,320},{320,256},{384,448},{4... | collective-permute-start | bytes 3145736 | tf_op jit(solution)/shard_map/ppermute | solution.py:25
  13.3 0.0 copy-done
  13.3 1.9 %collective-permute-start.1 = (f32[8,128]{1,0:T(8,128)S(1)}, f32[8,128]{1,0:T(8,128)S(1)}, u32[]{:S(2)}, u32[]{:S(2)}) collective-permute-start(f32[8,128]{1,0:T(8,128)S(1)} %dynamic-slice_bitcast_fusion), channel_id=1, source_target_pairs={{0,0},{64,1},{128,2},{192,3},{256,4},{320,5},{384,6},{448,7},{1,8}... | collective-permute-start | bytes 12296 | tf_op jit(solution)/shard_map/ppermute | solution.py:116
  15.2 3.0 %collective-permute-done.1 = f32[8,128]{1,0:T(8,128)S(1)} collective-permute-done((f32[8,128]{1,0:T(8,128)S(1)}, f32[8,128]{1,0:T(8,128)S(1)}, u32[]{:S(2)}, u32[]{:S(2)}) %collective-permute-start.1) | collective-permute-done | bytes 4128 | tf_op jit(solution)/shard_map/ppermute | solution.py:116
  18.2 0.6 broadcast_in_dim.15
  18.8 8.7 %all-to-all-start.1 = ((f32[8,8,128]{2,1,0:T(8,128)}), f32[8,8,128]{2,1,0:T(8,128)S(1)}, u32[]{:S(2)}, u32[]{:S(2)}) async-start(f32[8,8,128]{2,1,0:T(8,128)} %broadcast_in_dim.15), calls=%async_computation.1 | async-start | bytes 65536 | tf_op jit(solution)/shard_map/all_to_all | solution.py:16
  27.5 0.0 collective-permute-done
  27.5 1.4 add.31
  28.9 5.5 %all-to-all-done.1 = f32[8,8,128]{2,1,0:T(8,128)S(1)} async-done(((f32[8,8,128]{2,1,0:T(8,128)}), f32[8,8,128]{2,1,0:T(8,128)S(1)}, u32[]{:S(2)}, u32[]{:S(2)}) %all-to-all-start.1) | async-done | bytes 32800 | tf_op jit(solution)/shard_map/all_to_all | solution.py:16
  34.4 16.3 %all_to_all.40 = f32[4,64,1024]{2,1,0:T(8,128)S(1)} all-to-all(f32[4,64,1024]{2,1,0:T(8,128)S(1)} %add.31), channel_id=1, replica_groups={{0,128,256,384},{64,192,320,448},{1,129,257,385},{65,193,321,449},{2,13..., dimensions={0} | all-to-all | bytes 2097152 | tf_op jit(solution)/shard_map/all_to_all | solution.py:16
  50.7 0.7 broadcast_in_dim.17
  51.4 10.1 %all-to-all-start.2 = ((f32[8,64,128]{2,1,0:T(8,128)}), f32[8,64,128]{2,1,0:T(8,128)S(1)}, u32[]{:S(2)}, u32[]{:S(2)}) async-start(f32[8,64,128]{2,1,0:T(8,128)} %broadcast_in_dim.17), calls=%async_computation.2 | async-start | bytes 524288 | tf_op jit(solution)/shard_map/all_to_all | solution.py:16
  61.5 0.1 reduce_sum.36
  61.6 9.4 %all-to-all-done.2 = f32[8,64,128]{2,1,0:T(8,128)S(1)} async-done(((f32[8,64,128]{2,1,0:T(8,128)}), f32[8,64,128]{2,1,0:T(8,128)S(1)}, u32[]{:S(2)}, u32[]{:S(2)}) %all-to-all-start.2) | async-done | bytes 262176 | tf_op jit(solution)/shard_map/all_to_all | solution.py:16
  71.0 0.4 fusion
  71.3 0.1 pad_maximum_fusion.4
  71.4 11.2 %all_to_all.41 = f32[8,32,128]{2,1,0:T(8,128)S(1)} all-to-all(f32[8,32,128]{2,1,0:T(8,128)S(1)} %broadcast_in_dim.18), channel_id=1, replica_groups=mesh['replica'=8,'mp'=64] {'replica'}, dimensions={0} | all-to-all | bytes 262144 | tf_op jit(solution)/shard_map/all_to_all | solution.py:16
  82.6 0.1 fusion.29
  82.7 0.4 convolution_bitcast_fusion
  83.2 16.6 %all_to_all.42 = f32[64,8,128]{2,1,0:T(8,128)S(1)} all-to-all(f32[64,8,128]{2,1,0:T(8,128)S(1)} %bitcast.44), channel_id=1, replica_groups=mesh['replica'=8,'mp'=64] {'mp'}, dimensions={0} | all-to-all | bytes 524288 | tf_op jit(solution)/shard_map/all_to_all | solution.py:16
  99.8 0.1 reduce_sum.38
  99.9 18.0 %all_to_all.43 = f32[64,8,128]{2,1,0:T(8,128)S(1)} all-to-all(f32[64,8,128]{2,1,0:T(8,128)S(1)} %broadcast_in_dim.19), channel_id=1, replica_groups=mesh['replica'=8,'mp'=64] {'mp'}, dimensions={0} | all-to-all | bytes 524288 | tf_op jit(solution)/shard_map/all_to_all | solution.py:16
  117.8 0.4 convolution_bitcast_fusion.1
  118.2 0.1 pad_maximum_fusion.5
  118.3 11.1 %all_to_all.44 = f32[8,32,128]{2,1,0:T(8,128)S(1)} all-to-all(f32[8,32,128]{2,1,0:T(8,128)S(1)} %broadcast_in_dim.20), channel_id=1, replica_groups=mesh['replica'=8,'mp'=64] {'replica'}, dimensions={0} | all-to-all | bytes 262144 | tf_op jit(solution)/shard_map/all_to_all | solution.py:16
  129.4 1.1 broadcast_in_dim.21
  130.5 3.5 %all-to-all-start.7 = ((f32[4,8,64,128]{3,2,1,0:T(8,128)}), f32[4,8,64,128]{3,2,1,0:T(8,128)S(1)}, u32[]{:S(2)}, u32[]{:S(2)}) async-start(f32[4,8,64,128]{3,2,1,0:T(8,128)} %broadcast_in_dim.21), calls=%async_computation.7 | async-start | bytes 2097152 | tf_op jit(solution)/shard_map/all_to_all | solution.py:16
  134.0 0.1 fusion.28
  134.1 0.1 copy.15
  134.2 0.1 copy.16
  134.3 0.1 pad_maximum_fusion.1
  134.4 0.1 copy.14
  134.4 13.8 %all-to-all-done.7.mine = f32[4,8,64,128]{3,2,1,0:T(8,128)S(1)} async-done(((f32[4,8,64,128]{3,2,1,0:T(8,128)}), f32[4,8,64,128]{3,2,1,0:T(8,128)S(1)}, u32[]{:S(2)}, u32[]{:S(2)}) %all-to-all-start.7) | async-done | bytes 1048608 | tf_op jit(solution)/shard_map/all_to_all | solution.py:16
  148.2 3.7 %collective-permute-start.2 = (f32[4,8,64,128]{3,2,1,0:T(8,128)S(1)}, f32[4,8,64,128]{3,2,1,0:T(8,128)S(1)}, u32[]{:S(2)}, u32[]{:S(2)}) collective-permute-start(f32[4,8,64,128]{3,2,1,0:T(8,128)S(1)} %all-to-all-done.7.mine), channel_id=1, source_target_pairs={{0,64},{64,0},{128,192},{192,128},{256,320},{320,256},{384,448},{4... | collective-permute-start | bytes 3145736 | tf_op jit(solution)/shard_map/ppermute | solution.py:25
  151.9 0.1 fusion.16
  152.0 5.8 %cholesky.16 = f32[64,64]{1,0:T(8,128)S(1)} custom-call(f32[64,64]{1,0:T(8,128)S(1)} %fusion.16), custom_call_target="Cholesky" | custom-call | tf_op jit(solution)/shard_map/jit(cholesky)/cholesky | solution.py:138
  157.9 0.6 compare_reduce_fusion
  158.5 0.7 fusion.8
  159.2 4.9 %custom-call.10 = f32[1,64,64]{1,2,0:T(8,128)S(1)} custom-call(f32[1,64,64]{2,1,0:T(8,128)S(1)} %fusion.8), custom_call_target="InvertDiagBlocksLowerTriangular" | custom-call | tf_op jit(solution)/shard_map/triangular_solve | solution.py:139
  164.1 0.2 fusion.14
  164.3 0.0 copy-start.3
  164.3 0.8 fusion.12.weights
  165.1 0.0 collective-permute-done.2.theirs
  165.1 1.0 copy-done.2
  166.1 5.1 %update_error.1 = bf16[1,64,8192]{2,1,0:T(8,128)(2,1)} custom-call(s32[1]{0:T(128)} %bitcast.core_ref, f32[64,64]{1,0:T(8,128)} %fusion.12.weights, f32[4,8,64,128]{3,2,1,0:T(8,128)} %copy-done.1, f32[4,8,64,128]{3,2,1,0:T(8,128)} %copy-done.2, bf16[1,64,8192]{2,1,0:T(8,128)(2,1)} %gradient.1, bf16[1,64,8192]{2,1,0:T(8,128)(2,1)} %error.1), custom_call_target="tpu_custom_call" | custom-call | flops 67108864 | bytes 5242880 | tf_op jit(solution)/shard_map/update_error/pallas_call | solution.py:83
  171.2 1.6 fusion.9
  (14 shorter events, 0.1 us)
Async XLA Ops:
  0.6 12.6 %copy-start = (f32[128,64]{0,1:T(8,128)S(1)}, f32[128,64]{0,1:T(8,128)}, u32[]{:S(2)}) copy-start(f32[128,64]{0,1:T(8,128)} %param.5) | copy-start | bytes 98308
  4.5 23.0 %collective-permute-start = (f32[4,64,1024]{2,1,0:T(8,128)}, f32[4,64,1024]{2,1,0:T(8,128)S(1)}, u32[]{:S(2)}, u32[]{:S(2)}) collective-permute-start(f32[4,64,1024]{2,1,0:T(8,128)} %get-tuple-element.6), channel_id=1, source_target_pairs={{0,64},{64,0},{128,192},{192,128},{256,320},{320,256},{384,448},{4... | collective-permute-start | bytes 3145736 | tf_op jit(solution)/shard_map/ppermute | solution.py:25
  13.3 4.9 %collective-permute-start.1 = (f32[8,128]{1,0:T(8,128)S(1)}, f32[8,128]{1,0:T(8,128)S(1)}, u32[]{:S(2)}, u32[]{:S(2)}) collective-permute-start(f32[8,128]{1,0:T(8,128)S(1)} %dynamic-slice_bitcast_fusion), channel_id=1, source_target_pairs={{0,0},{64,1},{128,2},{192,3},{256,4},{320,5},{384,6},{448,7},{1,8}... | collective-permute-start | bytes 12296 | tf_op jit(solution)/shard_map/ppermute | solution.py:116
  18.8 15.5 %all-to-all-start.1 = ((f32[8,8,128]{2,1,0:T(8,128)}), f32[8,8,128]{2,1,0:T(8,128)S(1)}, u32[]{:S(2)}, u32[]{:S(2)}) async-start(f32[8,8,128]{2,1,0:T(8,128)} %broadcast_in_dim.15), calls=%async_computation.1 | async-start | bytes 65536 | tf_op jit(solution)/shard_map/all_to_all | solution.py:16
  51.4 19.5 %all-to-all-start.2 = ((f32[8,64,128]{2,1,0:T(8,128)}), f32[8,64,128]{2,1,0:T(8,128)S(1)}, u32[]{:S(2)}, u32[]{:S(2)}) async-start(f32[8,64,128]{2,1,0:T(8,128)} %broadcast_in_dim.17), calls=%async_computation.2 | async-start | bytes 524288 | tf_op jit(solution)/shard_map/all_to_all | solution.py:16
  130.5 17.8 %all-to-all-start.7 = ((f32[4,8,64,128]{3,2,1,0:T(8,128)}), f32[4,8,64,128]{3,2,1,0:T(8,128)S(1)}, u32[]{:S(2)}, u32[]{:S(2)}) async-start(f32[4,8,64,128]{3,2,1,0:T(8,128)} %broadcast_in_dim.21), calls=%async_computation.7 | async-start | bytes 2097152 | tf_op jit(solution)/shard_map/all_to_all | solution.py:16
  148.2 16.8 %copy-start.1 = (f32[4,8,64,128]{3,2,1,0:T(8,128)}, f32[4,8,64,128]{3,2,1,0:T(8,128)S(1)}, u32[]{:S(2)}) copy-start(f32[4,8,64,128]{3,2,1,0:T(8,128)S(1)} %all-to-all-done.7.mine) | copy-start | bytes 3145732
  148.2 16.8 %collective-permute-start.2 = (f32[4,8,64,128]{3,2,1,0:T(8,128)S(1)}, f32[4,8,64,128]{3,2,1,0:T(8,128)S(1)}, u32[]{:S(2)}, u32[]{:S(2)}) collective-permute-start(f32[4,8,64,128]{3,2,1,0:T(8,128)S(1)} %all-to-all-done.7.mine), channel_id=1, source_target_pairs={{0,64},{64,0},{128,192},{192,128},{256,320},{320,256},{384,448},{4... | collective-permute-start | bytes 3145736 | tf_op jit(solution)/shard_map/ppermute | solution.py:25
  164.3 0.8 copy-start.3
  165.1 1.0 copy-start.2

commit v2 on v0

v2 whole, which is shorter than its diff:
```python
import jax
import jax.numpy as jnp
from jax import lax
from jax.experimental import pallas as pl
from jax.experimental.pallas import tpu as pltpu
from jax.sharding import PartitionSpec as P

HIGHEST = lax.Precision.HIGHEST
BLOCK = 128
CORES = 2
SLAB = 16


def exchange(value, axis, groups=None):
    return lax.all_to_all(value, axis, 0, 0, axis_index_groups=groups)


def spread(value, axis, groups=None):
    count = len(groups[0]) if groups else lax.axis_size(axis)
    return exchange(jnp.broadcast_to(value[None], (count,) + value.shape), axis, groups)


def swap_cores(value, replicas):
    return lax.ppermute(value, "replica", [(r, r ^ 1) for r in range(replicas)])


def fold(square):
    half = square.shape[0] // 2
    return jnp.concatenate([square[:half], square[half:]], axis=1)


def unfold(folded):
    half = folded.shape[1] // 2
    return jnp.concatenate([folded[:, :half], folded[:, half:]], axis=0)


def own_columns(ref, chunk, k, stride):
    return ref[0, :, pl.ds(pl.multiple_of((k * stride + chunk) * BLOCK, BLOCK), BLOCK)]


def give_kernel(core_ref, gradient, error, give):
    chips, _, own = give.shape
    for x in range(chips):
        chunk = CORES * x + 1 - core_ref[0]
        for k in range(own // BLOCK):
            g, e = (own_columns(ref, chunk, k, CORES * chips) for ref in (gradient, error))
            give[x, :, k * BLOCK:(k + 1) * BLOCK] = g.astype(jnp.float32) + e.astype(jnp.float32)


def keep_kernel(core_ref, gradient, error, came, total):
    chips, _, own = total.shape
    for x in range(chips):
        chunk = CORES * x + core_ref[0]
        for k in range(own // BLOCK):
            g, e = (own_columns(ref, chunk, k, CORES * chips) for ref in (gradient, error))
            columns = slice(k * BLOCK, (k + 1) * BLOCK)
            moment = g.astype(jnp.float32) + e.astype(jnp.float32)
            total[x, :, columns] = moment + came[x, :, columns]


def moment_chunks(kernel, core, gradient, error, own, came=()):
    _, rows, cols = gradient.shape
    chips = cols // own // CORES
    band = pl.BlockSpec((1, SLAB, cols), lambda i, core: (0, i, 0))
    part = pl.BlockSpec((chips, SLAB, own), lambda i, core: (0, i, 0))
    return pl.pallas_call(
        kernel,
        grid_spec=pltpu.PrefetchScalarGridSpec(
            num_scalar_prefetch=1, grid=(rows // SLAB,),
            in_specs=[band, band] + [part] * len(came), out_specs=part),
        out_shape=jax.ShapeDtypeStruct((chips, rows, own), jnp.float32),
        cost_estimate=pl.CostEstimate(flops=rows * cols, bytes_accessed=6 * rows * cols, transcendentals=0),
        name="moment_chunks",
    )(core, gradient, error, *came)


def update_kernel(place, weights, inverse, mine, theirs, gradient, error, out, right):
    chips, _, rank, _ = mine.shape
    core, block, chip, parity = (place[i] for i in range(4))
    factor = weights[...]
    high = factor.astype(jnp.bfloat16).astype(jnp.float32)
    lane = lax.broadcasted_iota(jnp.int32, factor.shape, 1)
    factor = jnp.where(lane < 2 * rank, high, factor - high).astype(jnp.bfloat16)
    for x in range(chips):
        own, other = mine[x, 0], theirs[x, 0]
        s = jnp.concatenate([jnp.where(core == 0, own, other), jnp.where(core == 0, other, own)], axis=1)
        s_high = s.astype(jnp.bfloat16)
        s_low = (s - s_high.astype(jnp.float32)).astype(jnp.bfloat16)
        stack = jnp.concatenate([s_high, s_low, s_high, s_low], axis=0)
        change = jnp.dot(factor, stack, preferred_element_type=jnp.float32)
        columns = slice(CORES * x * BLOCK, CORES * (x + 1) * BLOCK)
        moment = gradient[0, :, columns].astype(jnp.float32) + error[0, :, columns].astype(jnp.float32)
        out[0, :, columns] = (moment - change).astype(out.dtype)

    @pl.when(pl.program_id(0) == block)
    def _():
        s = jnp.where(core == parity, mine[chip, 0], theirs[chip, 0])
        right[...] = jnp.dot(inverse[...], s, precision=HIGHEST, preferred_element_type=jnp.float32)


def update_error(place, weights, inverse, mine, theirs, gradient, error):
    _, rows, cols = gradient.shape
    chips, groups, rank, _ = mine.shape
    factor = pl.BlockSpec(weights.shape, lambda a, place: (0, 0))
    lower = pl.BlockSpec(inverse.shape, lambda a, place: (0, 0))
    tiles = pl.BlockSpec((chips, 1, rank, BLOCK), lambda a, place: (0, a, 0, 0))
    band = pl.BlockSpec((1, rows, cols // groups), lambda a, place: (0, 0, a))
    right = pl.BlockSpec((rank, BLOCK), lambda a, place: (0, 0))
    return pl.pallas_call(
        update_kernel,
        grid_spec=pltpu.PrefetchScalarGridSpec(
            num_scalar_prefetch=1, grid=(groups,),
            in_specs=[factor, lower, tiles, tiles, band, band], out_specs=[band, right]),
        out_shape=[jax.ShapeDtypeStruct(gradient.shape, gradient.dtype),
                   jax.ShapeDtypeStruct((rank, BLOCK), jnp.float32)],
        cost_estimate=pl.CostEstimate(
            flops=8 * rows * cols * rank, bytes_accessed=6 * rows * cols + 4 * rank * cols, transcendentals=0),
        name="update_error",
    )(place, weights, inverse, mine, theirs, gradient, error)


def unpack_kernel(tiles, copies, gram):
    count, groups, rank, _ = copies.shape
    slab = tiles.shape[1] // 2
    for a in range(groups):
        for b in range(rank // slab):
            tile = tiles[a * (rank // slab) + b, :slab]
            for x in range(count):
                copies[x, a, b * slab:(b + 1) * slab] = tile
    gram[...] = tiles[:, slab][:, :rank]


def unpack(tiles, count, groups, rank):
    return pl.pallas_call(
        unpack_kernel,
        out_shape=[jax.ShapeDtypeStruct((count, groups, rank, BLOCK), jnp.float32),
                   jax.ShapeDtypeStruct((rank, rank), jnp.float32)],
        cost_estimate=pl.CostEstimate(flops=0, bytes_accessed=tiles.size * 12, transcendentals=0),
        name="unpack",
    )(tiles)


def body(gradient, error, q_prev):
    replicas = lax.axis_size("replica")
    shards = lax.axis_size("mp")
    rows, cols = gradient.shape[1:]
    rank = q_prev.shape[1]
    own = cols // replicas
    groups = own // BLOCK
    slab = rank // replicas
    replica = lax.axis_index("replica").astype(jnp.int32)
    shard = lax.axis_index("mp").astype(jnp.int32)
    core = replica % CORES
    outer, inner = shard // replicas, shard % replicas
    chip_groups = [[c + CORES * x for x in range(replicas // CORES)] for c in range(CORES)]
    outer_groups = [[o * replicas + i for o in range(groups)] for i in range(replicas)]

    q_near = spread(q_prev.T, "mp", outer_groups)

    core_arg = core.reshape(1)
    give = moment_chunks(give_kernel, core_arg, gradient, error, own)
    came = swap_cores(give, replicas)
    total = moment_chunks(keep_kernel, core_arg, gradient, error, own, (came,))
    q_near, total = lax.optimization_barrier((q_near, total))
    q_blocks = lax.ppermute(q_near, ("replica", "mp"), [
        (r * shards + o * replicas + i, i * shards + o * replicas + r)
        for r in range(replicas) for o in range(groups) for i in range(replicas)
    ])
    q_own = q_blocks.transpose(1, 0, 2).reshape(rank, own)
    mean = exchange(total, "replica", chip_groups).sum(0) / replicas

    p_part = lax.dot_general(mean, q_own, (((1,), (1,)), ((), ())), precision=HIGHEST)
    p_mean = unfold(spread(fold(p_part), "replica").sum(0))

    s_part = lax.dot_general(p_mean, mean, (((0,), (0,)), ((), ())), precision=HIGHEST)
    s_part = s_part.reshape(replicas, slab, groups, BLOCK).transpose(2, 0, 1, 3)
    gram_part = lax.dot_general(p_mean, p_mean, (((0,), (0,)), ((), ())), precision=HIGHEST)
    gram_part = jnp.pad(gram_part[:, None], ((0, 0), (0, slab - 1), (0, BLOCK - rank)))
    tiles = jnp.concatenate([s_part.reshape(shards, slab, BLOCK), gram_part], axis=1)
    tiles = spread(exchange(tiles, "mp").sum(0), "mp")
    copies, gram = unpack(tiles, replicas // CORES, groups, rank)
    mine = exchange(copies, "replica", chip_groups)

    lower = jnp.linalg.cholesky(gram)
    inverse = lax.linalg.triangular_solve(
        lower, jnp.eye(rank, dtype=jnp.float32), left_side=True, lower=True
    )
    p_factor = lax.dot_general(p_mean, inverse, (((1,), (1,)), ((), ())), precision=HIGHEST)
    weights = jnp.dot(p_factor, inverse, precision=HIGHEST)
    weights = jnp.tile(weights, (1, 4))
    mine, weights, inverse = lax.optimization_barrier((mine, weights, inverse))
    theirs = swap_cores(mine, replicas)

    place = jnp.stack([core, outer, inner // CORES, inner % CORES])
    new_error, right = update_error(place, weights, inverse, mine, theirs, gradient, error)
    return (new_error, right.T, p_factor)


def solution(mesh):
    return jax.shard_map(
        body,
        mesh=mesh,
        in_specs=(P("replica", "mp", None), P("replica", "mp", None), P("mp", None)),
        out_specs=(P("replica", "mp", None), P("mp", None), P("mp", None)),
        check_vma=False,
    )
```

time: 475 us -> 158 us (0.33)
  waiting for transfers between devices: 389 us -> 25.9 us
  blocking collectives: 24.4 us -> 61.5 us
  Pallas kernels: 0 us -> 17.1 us
  between operations: 14.2 us -> 0.9 us
  starting transfers between devices: 20.6 us -> 31.7 us
  matrix products: 11.1 us -> 1.58 us
    psum x1 -> x0, waiting for transfers between devices: 283 us -> none  [body(): q_full = lax.psum(q_term, ('replica', 'mp')) / replicas]
    all_gather x1 -> x0, waiting for transfers between devices: 88.4 us -> none  [body(): q_whole = lax.all_gather(q_prev, 'mp', axis=0, tiled=True)]
    all_to_all x0 -> x3, blocking collectives: none -> 61.5 us  [exchange(): return lax.all_to_all(value, axis, 0, 0, axis_index_groups=groups)]
    psum x1 -> x0, blocking collectives: 24.4 us -> none  [body(): p_mean = lax.psum(p_local, 'replica') / replicas]
    all_to_all x0 -> x3, waiting for transfers between devices: none -> 24.3 us  [exchange(): return lax.all_to_all(value, axis, 0, 0, axis_index_groups=groups)]
    pallas_call x0 -> x4, Pallas kernels: none -> 17.1 us  [the longest x2 7.52 us: moment_chunks(): pl.pallas_call(kernel, grid_spec=pltpu.PrefetchScalarGridSpec(num_scalar_...]
    ppermute x6 -> x3, waiting for transfers between devices: 17.3 us -> 1.57 us  [the longest x2 1.57 us: swap_cores(): return lax.ppermute(value, 'replica', [(r, r ^ 1) for r in range(replicas)])]
    all_to_all x0 -> x3, starting transfers between devices: none -> 12.3 us  [exchange(): return lax.all_to_all(value, axis, 0, 0, axis_index_groups=groups)]
  transfers between devices with their start and end apart: 8 -> 6, of which waited for: 8 -> 3; matrix products, arithmetic and copies ran while one was open for 0% -> 10% of each run, Pallas kernels for 0% -> 2%
where the time goes in v2:
time: 158 us; the launch traced here: 157 us
  blocking collectives  61.5 us (39%)
  starting transfers between devices  31.7 us (20%)
  waiting for transfers between devices  25.9 us (16%)
  Pallas kernels  17.1 us (11%)
  other arithmetic  13 us (8%)
  local copies, waits for them, and re-layouts  5 us (3%)
  matrix products  1.58 us (1%)
    all_to_all x3, blocking collectives, exchange(): return lax.all_to_all(value, axis, 0, 0, axis_index_groups=groups)  61.5 us
    all_to_all x3, waiting for transfers between devices, exchange(): return lax.all_to_all(value, axis, 0, 0, axis_index_groups=groups)  24.3 us
    ppermute x2, starting transfers between devices, swap_cores(): return lax.ppermute(value, 'replica', [(r, r ^ 1) for r in range(replicas)])  15.5 us
    all_to_all x3, starting transfers between devices, exchange(): return lax.all_to_all(value, axis, 0, 0, axis_index_groups=groups)  12.3 us
    pallas_call x2, Pallas kernels, moment_chunks(): pl.pallas_call(kernel, grid_spec=pltpu.PrefetchScalarGridSpec(num_scalar_...  7.52 us
    pallas_call x1, Pallas kernels, update_error(): pl.pallas_call(update_kernel, grid_spec=pltpu.PrefetchScalarGridSpec(num_...  7.51 us
    another operation x3, other arithmetic, body(): lower = jnp.linalg.cholesky(gram)  6.52 us
    another operation x2, other arithmetic, body(): lax.linalg.triangular_solve(lower, jnp.eye(rank, dtype=jnp.float32), left...  5.55 us
  transfers between devices with their start and end apart: 6, of which 3 were waited for; matrix products, arithmetic and copies ran while one was open for 10% of the time, Pallas kernels for 2%

profile of v2, /device:TPU:1, one launch (start us, length us, event | category | flops | bytes accessed | tf_op | source)
XLA Modules:
  0.0 156.6 jit_solution(13412252748205962348)
XLA Ops:
  0.6 0.0 copy-start.6
  0.7 3.7 %moment_chunks.2 = f32[4,64,1024]{2,1,0:T(8,128)} custom-call(s32[1]{0:T(128)} %bitcast.core_ref, bf16[1,64,8192]{2,1,0:T(8,128)(2,1)} %gradient.5, bf16[1,64,8192]{2,1,0:T(8,128)(2,1)} %error.5), custom_call_target="tpu_custom_call" | custom-call | flops 524288 | bytes 3145728 | tf_op jit(solution)/shard_map/moment_chunks/pallas_call | solution.py:66
  4.3 8.8 %collective-permute-start = (f32[4,64,1024]{2,1,0:T(8,128)}, f32[4,64,1024]{2,1,0:T(8,128)S(1)}, u32[]{:S(2)}, u32[]{:S(2)}) collective-permute-start(f32[4,64,1024]{2,1,0:T(8,128)} %moment_chunks.2), channel_id=1, source_target_pairs={{0,64},{64,0},{128,192},{192,128},{256,320},{320,256},{384,448},{4... | collective-permute-start | bytes 3145736 | tf_op jit(solution)/shard_map/ppermute | solution.py:24
  13.1 0.0 copy-done.6
  13.1 0.7 broadcast_in_dim.9
  13.8 4.7 %all-to-all-start = ((f32[8,64,128]{2,1,0:T(8,128)}), f32[8,64,128]{2,1,0:T(8,128)S(1)}, u32[]{:S(2)}, u32[]{:S(2)}) async-start(f32[8,64,128]{2,1,0:T(8,128)} %broadcast_in_dim.9), calls=%async_computation | async-start | bytes 524288 | tf_op jit(solution)/shard_map/all_to_all | solution.py:15
  18.5 0.0 collective-permute-done.came
  18.5 0.0 copy-start.2
  18.5 1.0 copy-done.2
  19.4 3.9 %moment_chunks.3 = f32[4,64,1024]{2,1,0:T(8,128)} custom-call(s32[1]{0:T(128)} %bitcast.core_ref, bf16[1,64,8192]{2,1,0:T(8,128)(2,1)} %gradient.5, bf16[1,64,8192]{2,1,0:T(8,128)(2,1)} %error.5, f32[4,64,1024]{2,1,0:T(8,128)} %copy-done.2), custom_call_target="tpu_custom_call" | custom-call | flops 524288 | bytes 3145728 | tf_op jit(solution)/shard_map/moment_chunks/pallas_call | solution.py:66
  23.3 7.5 %all-to-all-done = f32[8,64,128]{2,1,0:T(8,128)S(1)} async-done(((f32[8,64,128]{2,1,0:T(8,128)}), f32[8,64,128]{2,1,0:T(8,128)S(1)}, u32[]{:S(2)}, u32[]{:S(2)}) %all-to-all-start) | async-done | bytes 262176 | tf_op jit(solution)/shard_map/all_to_all | solution.py:15
  30.8 4.0 %all-to-all-start.1 = ((f32[4,64,1024]{2,1,0:T(8,128)}), f32[4,64,1024]{2,1,0:T(8,128)S(1)}, u32[]{:S(2)}, u32[]{:S(2)}) async-start(f32[4,64,1024]{2,1,0:T(8,128)} %moment_chunks.3), calls=%async_computation.1 | async-start | bytes 2097152 | tf_op jit(solution)/shard_map/all_to_all | solution.py:15
  34.9 3.8 %collective-permute-start.1 = (f32[8,64,128]{2,1,0:T(8,128)S(1)}, f32[8,64,128]{2,1,0:T(8,128)S(1)}, u32[]{:S(2)}, u32[]{:S(2)}) collective-permute-start(f32[8,64,128]{2,1,0:T(8,128)S(1)} %all-to-all-done), channel_id=1, source_target_pairs={{0,0},{1,64},{2,128},{3,192},{4,256},{5,320},{6,384},{7,448},{8,8}... | collective-permute-start | bytes 786440 | tf_op jit(solution)/shard_map/ppermute | solution.py:165
  38.7 16.8 %all-to-all-done.1 = f32[4,64,1024]{2,1,0:T(8,128)S(1)} async-done(((f32[4,64,1024]{2,1,0:T(8,128)}), f32[4,64,1024]{2,1,0:T(8,128)S(1)}, u32[]{:S(2)}, u32[]{:S(2)}) %all-to-all-start.1) | async-done | bytes 1048608 | tf_op jit(solution)/shard_map/all_to_all | solution.py:15
  55.4 0.1 reduce_sum.27
  55.5 0.0 collective-permute-done.1
  55.5 0.4 fusion
  55.9 0.1 pad_maximum_fusion.4
  56.0 13.4 %all_to_all.30 = f32[8,32,128]{2,1,0:T(8,128)S(1)} all-to-all(f32[8,32,128]{2,1,0:T(8,128)S(1)} %broadcast_in_dim.10), channel_id=1, replica_groups=mesh['replica'=8,'mp'=64] {'replica'}, dimensions={0} | all-to-all | bytes 262144 | tf_op jit(solution)/shard_map/all_to_all | solution.py:15
  69.4 0.1 fusion.18
  69.5 0.4 convolution_bitcast_fusion
  69.9 0.2 convolution_bitcast_fusion.1
  70.2 0.2 copy.24
  70.4 0.3 copy.16
  70.7 25.6 %all_to_all.31 = f32[64,16,128]{2,1,0:T(8,128)S(1)} all-to-all(f32[64,16,128]{2,1,0:T(8,128)S(1)} %copy.16), channel_id=1, replica_groups=mesh['replica'=8,'mp'=64] {'mp'}, dimensions={0} | all-to-all | bytes 1048576 | tf_op jit(solution)/shard_map/all_to_all | solution.py:15
  96.2 0.1 reduce_sum.29
  96.4 22.5 %all_to_all.32.tiles = f32[64,16,128]{2,1,0:T(8,128)} all-to-all(f32[64,16,128]{2,1,0:T(8,128)S(1)} %broadcast_in_dim.12), channel_id=1, replica_groups=mesh['replica'=8,'mp'=64] {'mp'}, dimensions={0} | all-to-all | bytes 1048576 | tf_op jit(solution)/shard_map/all_to_all | solution.py:15
  118.9 2.1 %unpack.1 = (f32[4,8,64,128]{3,2,1,0:T(8,128)}, f32[64,64]{1,0:T(8,128)}) custom-call(f32[64,16,128]{2,1,0:T(8,128)} %all_to_all.32.tiles), custom_call_target="tpu_custom_call" | custom-call | bytes 1572864 | tf_op jit(solution)/shard_map/unpack/pallas_call | solution.py:134
  121.0 3.6 %all-to-all-start.5 = ((f32[4,8,64,128]{3,2,1,0:T(8,128)}), f32[4,8,64,128]{3,2,1,0:T(8,128)S(1)}, u32[]{:S(2)}, u32[]{:S(2)}) async-start(f32[4,8,64,128]{3,2,1,0:T(8,128)} %get-tuple-element.14), calls=%async_computation.5 | async-start | bytes 2097152 | tf_op jit(solution)/shard_map/all_to_all | solution.py:15
  124.6 0.0 copy-done.5
  124.7 0.1 copy.17
  124.7 5.8 %cholesky.17 = f32[64,64]{1,0:T(8,128)S(1)} custom-call(f32[64,64]{1,0:T(8,128)S(1)} %fusion.10), custom_call_target="Cholesky" | custom-call | tf_op jit(solution)/shard_map/jit(cholesky)/cholesky | solution.py:184
  130.6 0.6 compare_reduce_fusion
  131.3 0.7 fusion.7
  131.9 4.9 %custom-call.6 = f32[1,64,64]{1,2,0:T(8,128)S(1)} custom-call(f32[1,64,64]{2,1,0:T(8,128)S(1)} %fusion.7), custom_call_target="InvertDiagBlocksLowerTriangular" | custom-call | tf_op jit(solution)/shard_map/triangular_solve | solution.py:185
  136.8 0.2 fusion.8.inverse
  137.1 0.0 copy-start.3
  137.1 0.2 fusion.11
  137.3 0.4 copy-done.3
  137.7 0.2 fusion.19
  137.8 0.4 copy-done.4
  138.3 0.8 tile.10.weights
  139.1 0.0 all-to-all-done.5.mine
  139.1 6.7 %collective-permute-start.2 = (f32[4,8,64,128]{3,2,1,0:T(8,128)S(1)}, f32[4,8,64,128]{3,2,1,0:T(8,128)S(1)}, u32[]{:S(2)}, u32[]{:S(2)}) collective-permute-start(f32[4,8,64,128]{3,2,1,0:T(8,128)S(1)} %all-to-all-done.5.mine), channel_id=1, source_target_pairs={{0,64},{64,0},{128,192},{192,128},{256,320},{320,256},{384,448},{4... | collective-permute-start | bytes 3145736 | tf_op jit(solution)/shard_map/ppermute | solution.py:24
  145.9 0.7 pad_add_fusion.place
  146.5 1.6 collective-permute-done.2.theirs
  148.1 1.0 copy-done.1
  149.1 7.5 %update_error.1 = (bf16[1,64,8192]{2,1,0:T(8,128)(2,1)}, f32[64,128]{1,0:T(8,128)}) custom-call(s32[4]{0:T(128)} %pad_add_fusion.place, f32[64,256]{1,0:T(8,128)} %tile.10.weights, f32[64,64]{1,0:T(8,128)} %copy-done.3, f32[4,8,64,128]{3,2,1,0:T(8,128)} %copy-done, f32[4,8,64,128]{3,2,1,0:T(8,128)} %copy-done.1, bf16[1,64,8192]{2,1,0:T(8,128)(2,1)} %gradient.5, ...), custom_call_target="tpu_custom_call" | custom-call | flops 268435456 | bytes 5242880 | tf_op jit(solution)/shard_map/update_error/pallas_call | solution.py:109
  (13 shorter events, 0.2 us)
Async XLA Ops:
  0.6 12.4 %copy-start.6 = (f32[128,64]{0,1:T(8,128)S(1)}, f32[128,64]{0,1:T(8,128)}, u32[]{:S(2)}) copy-start(f32[128,64]{0,1:T(8,128)} %param.5) | copy-start | bytes 98308
  4.3 14.2 %collective-permute-start = (f32[4,64,1024]{2,1,0:T(8,128)}, f32[4,64,1024]{2,1,0:T(8,128)S(1)}, u32[]{:S(2)}, u32[]{:S(2)}) collective-permute-start(f32[4,64,1024]{2,1,0:T(8,128)} %moment_chunks.2), channel_id=1, source_target_pairs={{0,64},{64,0},{128,192},{192,128},{256,320},{320,256},{384,448},{4... | collective-permute-start | bytes 3145736 | tf_op jit(solution)/shard_map/ppermute | solution.py:24
  13.8 17.0 %all-to-all-start = ((f32[8,64,128]{2,1,0:T(8,128)}), f32[8,64,128]{2,1,0:T(8,128)S(1)}, u32[]{:S(2)}, u32[]{:S(2)}) async-start(f32[8,64,128]{2,1,0:T(8,128)} %broadcast_in_dim.9), calls=%async_computation | async-start | bytes 524288 | tf_op jit(solution)/shard_map/all_to_all | solution.py:15
  18.5 1.0 copy-start.2
  30.8 24.6 %all-to-all-start.1 = ((f32[4,64,1024]{2,1,0:T(8,128)}), f32[4,64,1024]{2,1,0:T(8,128)S(1)}, u32[]{:S(2)}, u32[]{:S(2)}) async-start(f32[4,64,1024]{2,1,0:T(8,128)} %moment_chunks.3), calls=%async_computation.1 | async-start | bytes 2097152 | tf_op jit(solution)/shard_map/all_to_all | solution.py:15
  34.9 20.7 %collective-permute-start.1 = (f32[8,64,128]{2,1,0:T(8,128)S(1)}, f32[8,64,128]{2,1,0:T(8,128)S(1)}, u32[]{:S(2)}, u32[]{:S(2)}) collective-permute-start(f32[8,64,128]{2,1,0:T(8,128)S(1)} %all-to-all-done), channel_id=1, source_target_pairs={{0,0},{1,64},{2,128},{3,192},{4,256},{5,320},{6,384},{7,448},{8,8}... | collective-permute-start | bytes 786440 | tf_op jit(solution)/shard_map/ppermute | solution.py:165
  121.0 3.7 %copy-start.5 = (f32[64,64]{1,0:T(8,128)S(1)}, f32[64,64]{1,0:T(8,128)}, u32[]{:S(2)}) copy-start(f32[64,64]{1,0:T(8,128)} %get-tuple-element.15) | copy-start | bytes 49156
  121.0 18.1 %all-to-all-start.5 = ((f32[4,8,64,128]{3,2,1,0:T(8,128)}), f32[4,8,64,128]{3,2,1,0:T(8,128)S(1)}, u32[]{:S(2)}, u32[]{:S(2)}) async-start(f32[4,8,64,128]{3,2,1,0:T(8,128)} %get-tuple-element.14), calls=%async_computation.5 | async-start | bytes 2097152 | tf_op jit(solution)/shard_map/all_to_all | solution.py:15
  137.1 0.6 copy-start.3
  137.7 0.6 copy-start.4
  139.1 9.0 %copy-start = (f32[4,8,64,128]{3,2,1,0:T(8,128)}, f32[4,8,64,128]{3,2,1,0:T(8,128)S(1)}, u32[]{:S(2)}) copy-start(f32[4,8,64,128]{3,2,1,0:T(8,128)S(1)} %all-to-all-done.5.mine) | copy-start | bytes 3145732
  139.1 9.0 %collective-permute-start.2 = (f32[4,8,64,128]{3,2,1,0:T(8,128)S(1)}, f32[4,8,64,128]{3,2,1,0:T(8,128)S(1)}, u32[]{:S(2)}, u32[]{:S(2)}) collective-permute-start(f32[4,8,64,128]{3,2,1,0:T(8,128)S(1)} %all-to-all-done.5.mine), channel_id=1, source_target_pairs={{0,64},{64,0},{128,192},{192,128},{256,320},{320,256},{384,448},{4... | collective-permute-start | bytes 3145736 | tf_op jit(solution)/shard_map/ppermute | solution.py:24
  148.1 1.0 copy-start.1

commit v3 on v0

v3 whole, which is shorter than its diff:
```python
import jax
import jax.numpy as jnp
from jax import lax
from jax.experimental import pallas as pl
from jax.experimental.pallas import tpu as pltpu
from jax.sharding import PartitionSpec as P

HIGHEST = lax.Precision.HIGHEST
BLOCK = 128
CORES = 2
SLAB = 16
TILE = 8
PACK = 9
PARAMS = pltpu.CompilerParams(vmem_limit_bytes=16 * 2**20)


def exchange(value, axis, groups=None):
    return lax.all_to_all(value, axis, 0, 0, axis_index_groups=groups)


def swap_cores(value, replicas):
    return lax.ppermute(value, "replica", [(r, r ^ 1) for r in range(replicas)])


def split_kernel(core_ref, gradient, error, keep, give):
    chips, _, own = keep.shape
    for x in range(chips):
        for out, core in ((keep, core_ref[0]), (give, 1 - core_ref[0])):
            for k in range(own // BLOCK):
                start = pl.multiple_of((k * CORES * chips + CORES * x + core) * BLOCK, BLOCK)
                g, e = (ref[0, :, pl.ds(start, BLOCK)].astype(jnp.float32) for ref in (gradient, error))
                out[x, :, k * BLOCK:(k + 1) * BLOCK] = g + e


def split_moment(core, gradient, error, own):
    _, rows, cols = gradient.shape
    chips = cols // own // CORES
    band = pl.BlockSpec((1, SLAB, cols), lambda i, core: (0, i, 0))
    part = pl.BlockSpec((chips, SLAB, own), lambda i, core: (0, i, 0))
    shape = jax.ShapeDtypeStruct((chips, rows, own), jnp.float32)
    return pl.pallas_call(
        split_kernel,
        grid_spec=pltpu.PrefetchScalarGridSpec(
            num_scalar_prefetch=1, grid=(rows // SLAB,), in_specs=[band, band], out_specs=[part, part]),
        out_shape=[shape, shape],
        cost_estimate=pl.CostEstimate(flops=rows * cols, bytes_accessed=8 * rows * cols, transcendentals=0),
        compiler_params=PARAMS,
        name="split_moment",
    )(core, gradient, error)


def product_kernel(outer_ref, parts, *refs):
    *lists, mean, copies, q_list = refs
    mean[...] = (parts[0] + parts[1] + parts[2] + parts[3]) * (1.0 / copies.shape[0])
    near = lists[0].shape[0]
    for i, piece in enumerate(lists):
        q_list[i * near:(i + 1) * near] = piece[...]
    blocks = []
    for a in range(q_list.shape[0]):
        apart = outer_ref[0] ^ a
        blocks.append(q_list[((apart & 3) << 1) | (apart >> 2)])
    q_own = jnp.concatenate(blocks, axis=1)
    p = lax.dot_general(mean[...], q_own, (((1,), (1,)), ((), ())), precision=HIGHEST,
                        preferred_element_type=jnp.float32)
    half = p.shape[0] // 2
    folded = jnp.concatenate([p[:half], p[half:]], axis=1)
    for r in range(copies.shape[0]):
        copies[r] = folded


def product(outer, parts, lists, replicas):
    _, rows, own = parts.shape
    near, rank, _ = lists[0].shape
    full = lambda *shape: pl.BlockSpec(shape, lambda i, outer: (0,) * len(shape))
    return pl.pallas_call(
        product_kernel,
        grid_spec=pltpu.PrefetchScalarGridSpec(
            num_scalar_prefetch=1, grid=(1,),
            in_specs=[full(*parts.shape)] + [full(*piece.shape) for piece in lists],
            out_specs=[full(rows, own), full(replicas, rows // 2, 2 * rank)],
            scratch_shapes=[pltpu.VMEM((near * len(lists), rank, BLOCK), jnp.float32)]),
        out_shape=[jax.ShapeDtypeStruct((rows, own), jnp.float32),
                   jax.ShapeDtypeStruct((replicas, rows // 2, 2 * rank), jnp.float32)],
        cost_estimate=pl.CostEstimate(flops=2 * rows * own * rank, bytes_accessed=4 * parts.size, transcendentals=0),
        compiler_params=PARAMS,
        name="product",
    )(outer, parts, *lists)


def pack_kernel(p_parts, mean, p_mean, tiles):
    folded = p_parts[0]
    for r in range(1, p_parts.shape[0]):
        folded = folded + p_parts[r]
    rank = folded.shape[1] // 2
    p = jnp.concatenate([folded[:, :rank], folded[:, rank:]], axis=0)
    p_mean[...] = p
    over_rows = (((0,), (0,)), ((), ()))
    s = lax.dot_general(p, mean[...], over_rows, precision=HIGHEST, preferred_element_type=jnp.float32)
    gram = lax.dot_general(p, p, over_rows, precision=HIGHEST, preferred_element_type=jnp.float32)
    gram = jnp.concatenate([gram] * (BLOCK // rank), axis=1)
    slabs = rank // TILE
    for a in range(mean.shape[1] // BLOCK):
        for b in range(slabs):
            t = a * slabs + b
            tiles[t * PACK:t * PACK + TILE] = s[b * TILE:(b + 1) * TILE, a * BLOCK:(a + 1) * BLOCK]
            tiles[t * PACK + TILE:(t + 1) * PACK] = gram[t:t + 1]


def pack(p_parts, mean, shards):
    rows, own = mean.shape
    rank = p_parts.shape[2] // 2
    return pl.pallas_call(
        pack_kernel,
        out_shape=[jax.ShapeDtypeStruct((rows, rank), jnp.float32),
                   jax.ShapeDtypeStruct((shards * PACK, BLOCK), jnp.float32)],
        cost_estimate=pl.CostEstimate(flops=2 * rows * own * rank, bytes_accessed=8 * mean.size, transcendentals=0),
        compiler_params=PARAMS,
        name="pack",
    )(p_parts, mean)


def total_kernel(tiles, copies):
    shards = tiles.shape[0] // PACK
    parts = [tiles[t * PACK:(t + 1) * PACK] for t in range(shards)]
    while len(parts) > 1:
        parts = [parts[i] + parts[i + 1] for i in range(0, len(parts), 2)]
    for t in range(shards):
        copies[t * PACK:(t + 1) * PACK] = parts[0]


def total(tiles):
    return pl.pallas_call(
        total_kernel,
        out_shape=jax.ShapeDtypeStruct(tiles.shape, tiles.dtype),
        cost_estimate=pl.CostEstimate(flops=tiles.size, bytes_accessed=8 * tiles.size, transcendentals=0),
        compiler_params=PARAMS,
        name="total",
    )(tiles)


def unpack_kernel(tiles, copies, gram):
    count, groups, rank, _ = copies.shape
    slabs = rank // TILE
    for a in range(groups):
        for b in range(slabs):
            t = a * slabs + b
            tile = tiles[t * PACK:t * PACK + TILE]
            for x in range(count):
                copies[x, a, b * TILE:(b + 1) * TILE] = tile
            gram[t:t + 1] = tiles[t * PACK + TILE:(t + 1) * PACK, :rank]


def unpack(tiles, count, groups, rank):
    return pl.pallas_call(
        unpack_kernel,
        out_shape=[jax.ShapeDtypeStruct((count, groups, rank, BLOCK), jnp.float32),
                   jax.ShapeDtypeStruct((rank, rank), jnp.float32)],
        cost_estimate=pl.CostEstimate(flops=0, bytes_accessed=tiles.size * 20, transcendentals=0),
        compiler_params=PARAMS,
        name="unpack",
    )(tiles)


def factors_kernel(p_mean, inverse, p_factor, weights):
    p = lax.dot_general(p_mean[...], inverse[...], (((1,), (1,)), ((), ())), precision=HIGHEST,
                        preferred_element_type=jnp.float32)
    w = jnp.dot(p, inverse[...], precision=HIGHEST, preferred_element_type=jnp.float32)
    p_factor[...] = p
    weights[...] = jnp.concatenate([w, w], axis=1)


def factors(p_mean, inverse):
    rows, rank = p_mean.shape
    return pl.pallas_call(
        factors_kernel,
        out_shape=[jax.ShapeDtypeStruct((rows, rank), jnp.float32),
                   jax.ShapeDtypeStruct((rows, 2 * rank), jnp.float32)],
        cost_estimate=pl.CostEstimate(flops=4 * rows * rank * rank, bytes_accessed=20 * rows * rank, transcendentals=0),
        compiler_params=PARAMS,
        name="factors",
    )(p_mean, inverse)


def update_kernel(place, weights, inverse, mine, theirs, gradient, error, out, right):
    chips, blocks, rank, _ = mine.shape
    core, block, chip, parity = (place[i] for i in range(4))
    high = weights[...].astype(jnp.bfloat16)
    low = (weights[...] - high.astype(jnp.float32)).astype(jnp.bfloat16)
    factor = jnp.concatenate([high, low], axis=0)
    rows = high.shape[0]
    for a in range(blocks):
        for x in range(chips):
            own, other = mine[x, a], theirs[x, a]
            s = jnp.concatenate([jnp.where(core == 0, own, other), jnp.where(core == 0, other, own)], axis=1)
            s_high = s.astype(jnp.bfloat16)
            s_low = (s - s_high.astype(jnp.float32)).astype(jnp.bfloat16)
            stack = jnp.concatenate([s_high, s_low], axis=0)
            change = jnp.dot(factor, stack, preferred_element_type=jnp.float32)
            start = CORES * (a * chips + x) * BLOCK
            columns = slice(start, start + CORES * BLOCK)
            moment = gradient[0, :, columns].astype(jnp.float32) + error[0, :, columns].astype(jnp.float32)
            out[0, :, columns] = (moment - (change[:rows] + change[rows:])).astype(out.dtype)

    @pl.when(pl.program_id(0) == block // blocks)
    def _():
        within = block % blocks
        s = jnp.where(core == parity, mine[chip, within], theirs[chip, within])
        right[...] = jnp.dot(inverse[...], s, precision=HIGHEST, preferred_element_type=jnp.float32)


def update_error(place, weights, inverse, mine, theirs, gradient, error):
    _, rows, cols = gradient.shape
    chips, groups, rank, _ = mine.shape
    steps = 4
    factor = pl.BlockSpec(weights.shape, lambda a, place: (0, 0))
    lower = pl.BlockSpec(inverse.shape, lambda a, place: (0, 0))
    tiles = pl.BlockSpec((chips, groups // steps, rank, BLOCK), lambda a, place: (0, a, 0, 0))
    band = pl.BlockSpec((1, rows, cols // steps), lambda a, place: (0, 0, a))
    right = pl.BlockSpec((rank, BLOCK), lambda a, place: (0, 0))
    return pl.pallas_call(
        update_kernel,
        grid_spec=pltpu.PrefetchScalarGridSpec(
            num_scalar_prefetch=1, grid=(steps,),
            in_specs=[factor, lower, tiles, tiles, band, band], out_specs=[band, right]),
        out_shape=[jax.ShapeDtypeStruct(gradient.shape, gradient.dtype),
                   jax.ShapeDtypeStruct((rank, BLOCK), jnp.float32)],
        cost_estimate=pl.CostEstimate(
            flops=8 * rows * cols * rank, bytes_accessed=6 * rows * cols + 8 * rank * cols, transcendentals=0),
        compiler_params=PARAMS,
        name="update_error",
    )(place, weights, inverse, mine, theirs, gradient, error)


def body(gradient, error, q_prev):
    replicas = lax.axis_size("replica")
    shards = lax.axis_size("mp")
    rows, cols = gradient.shape[1:]
    rank = q_prev.shape[1]
    own = cols // replicas
    groups = own // BLOCK
    replica = lax.axis_index("replica").astype(jnp.int32)
    shard = lax.axis_index("mp").astype(jnp.int32)
    core = replica % CORES
    outer, inner = shard // replicas, shard % replicas
    chip_groups = [[c + CORES * x for x in range(replicas // CORES)] for c in range(CORES)]

    def along(apart):
        return [(r * shards + o * replicas + i, i * shards + (o ^ apart) * replicas + r)
                for r in range(replicas) for o in range(groups) for i in range(replicas)]
    near = [lax.ppermute(q_prev.T[None], ("replica", "mp"), along(apart)) for apart in (0, 4)]

    keep, give = split_moment(core.reshape(1), gradient, error, own)
    paired, near = lax.optimization_barrier((keep + swap_cores(give, replicas), jnp.concatenate(near, axis=0)))
    parts = exchange(paired, "replica", chip_groups)
    lists = [near] + [
        lax.ppermute(near, "mp", [(j, j ^ (apart * replicas)) for j in range(shards)]) for apart in (1, 2, 3)]
    mean, copies = product(outer.reshape(1), parts, lists, replicas)

    p_mean, tiles = pack(exchange(copies, "replica"), mean, shards)
    packed = (shards, PACK, 1, BLOCK)
    tiles = exchange(tiles.reshape(packed), "mp").reshape(tiles.shape)
    tiles = exchange(total(tiles).reshape(packed), "mp").reshape(tiles.shape)
    copies, gram = unpack(tiles, replicas // CORES, groups, rank)
    mine = exchange(copies, "replica", chip_groups)

    lower = jnp.linalg.cholesky(gram)
    inverse = lax.linalg.triangular_solve(
        lower, jnp.eye(rank, dtype=jnp.float32), left_side=True, lower=True
    )
    p_factor, weights = factors(p_mean, inverse)
    mine, weights, inverse = lax.optimization_barrier((mine, weights, inverse))
    theirs = swap_cores(mine, replicas)

    place = jnp.stack([core, outer, inner // CORES, inner % CORES])
    new_error, right = update_error(place, weights, inverse, mine, theirs, gradient, error)
    return (new_error, right.T, p_factor)


def solution(mesh):
    return jax.shard_map(
        body,
        mesh=mesh,
        in_specs=(P("replica", "mp", None), P("replica", "mp", None), P("mp", None)),
        out_specs=(P("replica", "mp", None), P("mp", None), P("mp", None)),
        check_vma=False,
    )
```

time: 475 us -> 134 us (0.28)
  waiting for transfers between devices: 389 us -> 8.19 us
  starting transfers between devices: 20.6 us -> 48.8 us
  blocking collectives: 24.4 us -> 51.2 us
  between operations: 14.2 us -> 0.87 us
  matrix products: 11.1 us -> 0.23 us
  Pallas kernels: 0 us -> 7.45 us
    psum x1 -> x0, waiting for transfers between devices: 283 us -> none  [body(): q_full = lax.psum(q_term, ('replica', 'mp')) / replicas]
    all_gather x1 -> x0, waiting for transfers between devices: 88.4 us -> none  [body(): q_whole = lax.all_gather(q_prev, 'mp', axis=0, tiled=True)]
    all_to_all x0 -> x3, blocking collectives: none -> 51.2 us  [exchange(): return lax.all_to_all(value, axis, 0, 0, axis_index_groups=groups)]
    psum x1 -> x0, blocking collectives: 24.4 us -> none  [body(): p_mean = lax.psum(p_local, 'replica') / replicas]
    all_to_all x0 -> x2, starting transfers between devices: none -> 16.4 us  [exchange(): return lax.all_to_all(value, axis, 0, 0, axis_index_groups=groups)]
    ppermute x6 -> x7, starting transfers between devices: 20.5 us -> 32.4 us  [the longest x2 14.5 us: swap_cores(): return lax.ppermute(value, 'replica', [(r, r ^ 1) for r in range(replicas)])]
    dot_general x4 -> x0, matrix products: 10.9 us -> none  [the longest x1 4.23 us: body(): p_local = jnp.dot(moment, q_whole, precision=highest)]
    ppermute x6 -> x7, waiting for transfers between devices: 17.3 us -> 8.18 us  [the longest x3 3.1 us: body(): lax.ppermute(near, 'mp', [(j, j ^ apart * replicas) for j in range(shards)])]
  transfers between devices with their start and end apart: 8 -> 9, of which waited for: 8 -> 4; matrix products, arithmetic and copies ran while one was open for 0% -> 9% of each run, Pallas kernels for 0% -> 1%
where the time goes in v3:
time: 134 us
  blocking collectives  51.2 us (38%)
  starting transfers between devices  48.8 us (36%)
  other arithmetic  13.3 us (10%)
  waiting for transfers between devices  8.19 us (6%)
  Pallas kernels  7.45 us (6%)
  local copies, waits for them, and re-layouts  3.49 us (3%)
    all_to_all x3, blocking collectives, exchange(): return lax.all_to_all(value, axis, 0, 0, axis_index_groups=groups)  51.2 us
    all_to_all x2, starting transfers between devices, exchange(): return lax.all_to_all(value, axis, 0, 0, axis_index_groups=groups)  16.4 us
    ppermute x2, starting transfers between devices, swap_cores(): return lax.ppermute(value, 'replica', [(r, r ^ 1) for r in range(replicas)])  14.5 us
    ppermute x3, starting transfers between devices, body(): lax.ppermute(near, 'mp', [(j, j ^ apart * replicas) for j in range(shards)])  9.26 us
    ppermute x2, starting transfers between devices, body(): lax.ppermute(q_prev.T[None], ('replica', 'mp'), along(apart))  8.63 us
    another operation x3, other arithmetic, body(): lower = jnp.linalg.cholesky(gram)  6.52 us
    another operation x2, other arithmetic, body(): lax.linalg.triangular_solve(lower, jnp.eye(rank, dtype=jnp.float32), left...  5.55 us
    pallas_call x1, Pallas kernels, update_error(): pl.pallas_call(update_kernel, grid_spec=pltpu.PrefetchScalarGridSpec(num_...  4.67 us
  transfers between devices with their start and end apart: 9, of which 4 were waited for; matrix products, arithmetic and copies ran while one was open for 9% of the time, Pallas kernels for 1%

profile of v3, /device:TPU:1, one launch (start us, length us, event | category | flops | bytes accessed | tf_op | source)
XLA Modules:
  0.0 133.5 jit_solution(16537587699436368518)
XLA Ops:
  0.6 0.0 copy-start
  0.7 1.2 copy-done
  1.9 0.0 copy-start.2
  1.9 1.2 copy-done.2
  3.1 0.0 copy-start.5
  3.1 0.7 split_moment.1
  3.8 8.8 %collective-permute-start = (f32[4,64,1024]{2,1,0:T(8,128)S(1)}, f32[4,64,1024]{2,1,0:T(8,128)S(1)}, u32[]{:S(2)}, u32[]{:S(2)}) collective-permute-start(f32[4,64,1024]{2,1,0:T(8,128)S(1)} %get-tuple-element.21), channel_id=1, source_target_pairs={{0,64},{64,0},{128,192},{192,128},{256,320},{320,256},{384,448},{4... | collective-permute-start | bytes 3145736 | tf_op jit(solution)/shard_map/ppermute | solution.py:22
  12.6 0.0 copy-done.5
  12.6 6.2 %collective-permute-start.2 = (f32[1,64,128]{2,1,0:T(8,128)S(1)}, f32[1,64,128]{2,1,0:T(8,128)S(1)}, u32[]{:S(2)}, u32[]{:S(2)}) collective-permute-start(f32[1,64,128]{2,1,0:T(8,128)S(1)} %bitcast.25), channel_id=1, source_target_pairs={{0,32},{1,96},{2,160},{3,224},{4,288},{5,352},{6,416},{7,480},{8,4... | collective-permute-start | bytes 98312 | tf_op jit(solution)/shard_map/ppermute | solution.py:250
  18.8 2.5 %collective-permute-start.1 = (f32[1,64,128]{2,1,0:T(8,128)S(1)}, f32[1,64,128]{2,1,0:T(8,128)S(1)}, u32[]{:S(2)}, u32[]{:S(2)}) collective-permute-start(f32[1,64,128]{2,1,0:T(8,128)S(1)} %bitcast.26), channel_id=1, source_target_pairs={{0,0},{1,64},{2,128},{3,192},{4,256},{5,320},{6,384},{7,448},{8,8}... | collective-permute-start | bytes 98312 | tf_op jit(solution)/shard_map/ppermute | solution.py:250
  21.3 2.8 %collective-permute-done.2 = f32[1,64,128]{2,1,0:T(8,128)S(1)} collective-permute-done((f32[1,64,128]{2,1,0:T(8,128)S(1)}, f32[1,64,128]{2,1,0:T(8,128)S(1)}, u32[]{:S(2)}, u32[]{:S(2)}) %collective-permute-start.2) | collective-permute-done | bytes 32800 | tf_op jit(solution)/shard_map/ppermute | solution.py:250
  24.1 0.0 collective-permute-done.1
  24.1 0.0 collective-permute-done
  24.1 1.2 add.29
  25.3 12.8 %all-to-all-start = ((f32[4,64,1024]{2,1,0:T(8,128)}), f32[4,64,1024]{2,1,0:T(8,128)S(1)}, u32[]{:S(2)}, u32[]{:S(2)}) async-start(f32[4,64,1024]{2,1,0:T(8,128)} %add.29), calls=%async_computation | async-start | bytes 2097152 | tf_op jit(solution)/shard_map/all_to_all | solution.py:18
  38.1 4.9 %collective-permute-start.5 = (f32[2,64,128]{2,1,0:T(8,128)S(1)}, f32[2,64,128]{2,1,0:T(8,128)S(1)}, u32[]{:S(2)}, u32[]{:S(2)}) collective-permute-start(f32[2,64,128]{2,1,0:T(8,128)S(1)} %pad_maximum_fusion.refs_0_), channel_id=1, source_target_pairs={{0,24},{1,25},{2,26},{3,27},{4,28},{5,29},{6,30},{7,31},{8,16},{9,... | collective-permute-start | bytes 196616 | tf_op jit(solution)/shard_map/ppermute | solution.py:256
  43.0 1.9 %collective-permute-start.4 = (f32[2,64,128]{2,1,0:T(8,128)S(1)}, f32[2,64,128]{2,1,0:T(8,128)S(1)}, u32[]{:S(2)}, u32[]{:S(2)}) collective-permute-start(f32[2,64,128]{2,1,0:T(8,128)S(1)} %pad_maximum_fusion.refs_0_), channel_id=1, source_target_pairs={{0,16},{1,17},{2,18},{3,19},{4,20},{5,21},{6,22},{7,23},{8,24},{9,... | collective-permute-start | bytes 196616 | tf_op jit(solution)/shard_map/ppermute | solution.py:256
  44.9 2.4 %collective-permute-start.3 = (f32[2,64,128]{2,1,0:T(8,128)S(1)}, f32[2,64,128]{2,1,0:T(8,128)S(1)}, u32[]{:S(2)}, u32[]{:S(2)}) collective-permute-start(f32[2,64,128]{2,1,0:T(8,128)S(1)} %pad_maximum_fusion.refs_0_), channel_id=1, source_target_pairs={{0,8},{1,9},{2,10},{3,11},{4,12},{5,13},{6,14},{7,15},{8,0},{9,1},... | collective-permute-start | bytes 196616 | tf_op jit(solution)/shard_map/ppermute | solution.py:256
  47.4 0.0 collective-permute-done.5.refs_3_
  47.4 2.4 %collective-permute-done.4.refs_2_ = f32[2,64,128]{2,1,0:T(8,128)S(1)} collective-permute-done((f32[2,64,128]{2,1,0:T(8,128)S(1)}, f32[2,64,128]{2,1,0:T(8,128)S(1)}, u32[]{:S(2)}, u32[]{:S(2)}) %collective-permute-start.4) | collective-permute-done | bytes 65568 | tf_op jit(solution)/shard_map/ppermute | solution.py:256
  49.8 0.7 collective-permute-done.3.refs_1_
  50.5 0.0 all-to-all-done.parts
  50.5 0.5 product.1
  51.0 13.7 %all_to_all.25.p_parts = f32[8,32,128]{2,1,0:T(8,128)S(1)} all-to-all(f32[8,32,128]{2,1,0:T(8,128)S(1)} %get-tuple-element.24), channel_id=1, replica_groups=mesh['replica'=8,'mp'=64] {'replica'}, dimensions={0} | all-to-all | bytes 262144 | tf_op jit(solution)/shard_map/all_to_all | solution.py:18
  64.6 0.6 pack.1
  65.2 19.1 %all_to_all.26 = f32[64,9,1,128]{3,2,1,0:T(1,128)S(1)} all-to-all(f32[64,9,1,128]{3,2,1,0:T(1,128)S(1)} %bitcast.24), channel_id=1, replica_groups=mesh['replica'=8,'mp'=64] {'mp'}, dimensions={0} | all-to-all | bytes 589824 | tf_op jit(solution)/shard_map/all_to_all | solution.py:18
  84.3 0.1 total.1
  84.4 18.4 %all_to_all.27 = f32[64,9,1,128]{3,2,1,0:T(1,128)S(1)} all-to-all(f32[64,9,1,128]{3,2,1,0:T(1,128)S(1)} %bitcast.23), channel_id=1, replica_groups=mesh['replica'=8,'mp'=64] {'mp'}, dimensions={0} | all-to-all | bytes 589824 | tf_op jit(solution)/shard_map/all_to_all | solution.py:18
  102.8 0.1 unpack.1
  102.9 0.0 copy-start.4
  102.9 1.0 copy-done.4
  103.8 0.0 copy-start.1
  103.8 0.0 copy-start.3
  103.9 3.6 %all-to-all-start.4 = ((f32[4,8,64,128]{3,2,1,0:T(8,128)}), f32[4,8,64,128]{3,2,1,0:T(8,128)S(1)}, u32[]{:S(2)}, u32[]{:S(2)}) async-start(f32[4,8,64,128]{3,2,1,0:T(8,128)} %copy-done.4), calls=%async_computation.4 | async-start | bytes 2097152 | tf_op jit(solution)/shard_map/all_to_all | solution.py:18
  107.5 0.1 copy.10
  107.6 5.8 %cholesky.17 = f32[64,64]{1,0:T(8,128)S(1)} custom-call(f32[64,64]{1,0:T(8,128)S(1)} %fusion.3), custom_call_target="Cholesky" | custom-call | tf_op jit(solution)/shard_map/jit(cholesky)/cholesky | solution.py:266
  113.5 0.6 compare_reduce_fusion
  114.1 0.7 fusion
  114.8 4.9 %custom-call.6 = f32[1,64,64]{1,2,0:T(8,128)S(1)} custom-call(f32[1,64,64]{2,1,0:T(8,128)S(1)} %fusion), custom_call_target="InvertDiagBlocksLowerTriangular" | custom-call | tf_op jit(solution)/shard_map/triangular_solve | solution.py:267
  119.7 0.2 fusion.1.inverse
  119.9 0.8 factors.1
  120.8 0.0 all-to-all-done.4.mine
  120.8 5.7 %collective-permute-start.6 = (f32[4,8,64,128]{3,2,1,0:T(8,128)S(1)}, f32[4,8,64,128]{3,2,1,0:T(8,128)}, u32[]{:S(2)}, u32[]{:S(2)}) collective-permute-start(f32[4,8,64,128]{3,2,1,0:T(8,128)S(1)} %all-to-all-done.4.mine), channel_id=1, source_target_pairs={{0,64},{64,0},{128,192},{192,128},{256,320},{320,256},{384,448},{4... | collective-permute-start | bytes 3145736 | tf_op jit(solution)/shard_map/ppermute | solution.py:22
  126.5 0.1 pad_add_fusion.place
  126.6 2.3 %collective-permute-done.6.theirs = f32[4,8,64,128]{3,2,1,0:T(8,128)} collective-permute-done((f32[4,8,64,128]{3,2,1,0:T(8,128)S(1)}, f32[4,8,64,128]{3,2,1,0:T(8,128)}, u32[]{:S(2)}, u32[]{:S(2)}) %collective-permute-start.6) | collective-permute-done | bytes 1048608 | tf_op jit(solution)/shard_map/ppermute | solution.py:22
  128.9 0.0 copy-done.1
  128.9 0.0 copy-done.3
  128.9 4.7 %update_error.1 = (bf16[1,64,8192]{2,1,0:T(8,128)(2,1)}, f32[64,128]{1,0:T(8,128)}) custom-call(s32[4]{0:T(128)S(1)} %pad_add_fusion.place, f32[64,128]{1,0:T(8,128)S(1)} %get-tuple-element.31.weights, f32[64,64]{1,0:T(8,128)S(1)} %fusion.1.inverse, f32[4,8,64,128]{3,2,1,0:T(8,128)S(1)} %all-to-all-done.4.mine, ...), custom_call_target="tpu_custom_call" | custom-call | flops 268435456 | bytes 7340032 | tf_op jit(solution)/shard_map/update_error/pallas_call | solution.py:220
  (3 shorter events, 0.0 us)
Async XLA Ops:
  0.6 1.2 copy-start
  1.9 1.2 copy-start.2
  3.1 9.5 %copy-start.5 = (f32[128,64]{0,1:T(8,128)S(1)}, f32[128,64]{0,1:T(8,128)}, u32[]{:S(2)}) copy-start(f32[128,64]{0,1:T(8,128)} %param.5) | copy-start | bytes 98308
  3.8 20.3 %collective-permute-start = (f32[4,64,1024]{2,1,0:T(8,128)S(1)}, f32[4,64,1024]{2,1,0:T(8,128)S(1)}, u32[]{:S(2)}, u32[]{:S(2)}) collective-permute-start(f32[4,64,1024]{2,1,0:T(8,128)S(1)} %get-tuple-element.21), channel_id=1, source_target_pairs={{0,64},{64,0},{128,192},{192,128},{256,320},{320,256},{384,448},{4... | collective-permute-start | bytes 3145736 | tf_op jit(solution)/shard_map/ppermute | solution.py:22
  12.6 11.5 %collective-permute-start.2 = (f32[1,64,128]{2,1,0:T(8,128)S(1)}, f32[1,64,128]{2,1,0:T(8,128)S(1)}, u32[]{:S(2)}, u32[]{:S(2)}) collective-permute-start(f32[1,64,128]{2,1,0:T(8,128)S(1)} %bitcast.25), channel_id=1, source_target_pairs={{0,32},{1,96},{2,160},{3,224},{4,288},{5,352},{6,416},{7,480},{8,4... | collective-permute-start | bytes 98312 | tf_op jit(solution)/shard_map/ppermute | solution.py:250
  18.8 5.3 %collective-permute-start.1 = (f32[1,64,128]{2,1,0:T(8,128)S(1)}, f32[1,64,128]{2,1,0:T(8,128)S(1)}, u32[]{:S(2)}, u32[]{:S(2)}) collective-permute-start(f32[1,64,128]{2,1,0:T(8,128)S(1)} %bitcast.26), channel_id=1, source_target_pairs={{0,0},{1,64},{2,128},{3,192},{4,256},{5,320},{6,384},{7,448},{8,8}... | collective-permute-start | bytes 98312 | tf_op jit(solution)/shard_map/ppermute | solution.py:250
  25.3 25.2 %all-to-all-start = ((f32[4,64,1024]{2,1,0:T(8,128)}), f32[4,64,1024]{2,1,0:T(8,128)S(1)}, u32[]{:S(2)}, u32[]{:S(2)}) async-start(f32[4,64,1024]{2,1,0:T(8,128)} %add.29), calls=%async_computation | async-start | bytes 2097152 | tf_op jit(solution)/shard_map/all_to_all | solution.py:18
  38.1 9.3 %collective-permute-start.5 = (f32[2,64,128]{2,1,0:T(8,128)S(1)}, f32[2,64,128]{2,1,0:T(8,128)S(1)}, u32[]{:S(2)}, u32[]{:S(2)}) collective-permute-start(f32[2,64,128]{2,1,0:T(8,128)S(1)} %pad_maximum_fusion.refs_0_), channel_id=1, source_target_pairs={{0,24},{1,25},{2,26},{3,27},{4,28},{5,29},{6,30},{7,31},{8,16},{9,... | collective-permute-start | bytes 196616 | tf_op jit(solution)/shard_map/ppermute | solution.py:256
  43.0 6.8 %collective-permute-start.4 = (f32[2,64,128]{2,1,0:T(8,128)S(1)}, f32[2,64,128]{2,1,0:T(8,128)S(1)}, u32[]{:S(2)}, u32[]{:S(2)}) collective-permute-start(f32[2,64,128]{2,1,0:T(8,128)S(1)} %pad_maximum_fusion.refs_0_), channel_id=1, source_target_pairs={{0,16},{1,17},{2,18},{3,19},{4,20},{5,21},{6,22},{7,23},{8,24},{9,... | collective-permute-start | bytes 196616 | tf_op jit(solution)/shard_map/ppermute | solution.py:256
  44.9 5.6 %collective-permute-start.3 = (f32[2,64,128]{2,1,0:T(8,128)S(1)}, f32[2,64,128]{2,1,0:T(8,128)S(1)}, u32[]{:S(2)}, u32[]{:S(2)}) collective-permute-start(f32[2,64,128]{2,1,0:T(8,128)S(1)} %pad_maximum_fusion.refs_0_), channel_id=1, source_target_pairs={{0,8},{1,9},{2,10},{3,11},{4,12},{5,13},{6,14},{7,15},{8,0},{9,1},... | collective-permute-start | bytes 196616 | tf_op jit(solution)/shard_map/ppermute | solution.py:256
  102.9 1.0 copy-start.4
  103.8 25.0 %copy-start.1 = (bf16[1,64,8192]{2,1,0:T(8,128)(2,1)S(1)}, bf16[1,64,8192]{2,1,0:T(8,128)(2,1)}, u32[]{:S(2)}) copy-start(bf16[1,64,8192]{2,1,0:T(8,128)(2,1)} %gradient.3) | copy-start | bytes 3145732
  103.8 25.0 %copy-start.3 = (bf16[1,64,8192]{2,1,0:T(8,128)(2,1)S(1)}, bf16[1,64,8192]{2,1,0:T(8,128)(2,1)}, u32[]{:S(2)}) copy-start(bf16[1,64,8192]{2,1,0:T(8,128)(2,1)} %error.3) | copy-start | bytes 3145732
  103.9 16.9 %all-to-all-start.4 = ((f32[4,8,64,128]{3,2,1,0:T(8,128)}), f32[4,8,64,128]{3,2,1,0:T(8,128)S(1)}, u32[]{:S(2)}, u32[]{:S(2)}) async-start(f32[4,8,64,128]{3,2,1,0:T(8,128)} %copy-done.4), calls=%async_computation.4 | async-start | bytes 2097152 | tf_op jit(solution)/shard_map/all_to_all | solution.py:18
  120.8 8.1 %collective-permute-start.6 = (f32[4,8,64,128]{3,2,1,0:T(8,128)S(1)}, f32[4,8,64,128]{3,2,1,0:T(8,128)}, u32[]{:S(2)}, u32[]{:S(2)}) collective-permute-start(f32[4,8,64,128]{3,2,1,0:T(8,128)S(1)} %all-to-all-done.4.mine), channel_id=1, source_target_pairs={{0,64},{64,0},{128,192},{192,128},{256,320},{320,256},{384,448},{4... | collective-permute-start | bytes 3145736 | tf_op jit(solution)/shard_map/ppermute | solution.py:22

commit v4 on v3

--- a/solution.py
+++ b/solution.py
@@ -8,7 +8,6 @@
 HIGHEST = lax.Precision.HIGHEST
 BLOCK = 128
 CORES = 2
-SLAB = 16
 TILE = 8
 PACK = 9
 PARAMS = pltpu.CompilerParams(vmem_limit_bytes=16 * 2**20)
@@ -20,6 +19,15 @@
 
 def swap_cores(value, replicas):
     return lax.ppermute(value, "replica", [(r, r ^ 1) for r in range(replicas)])
+
+
+SCALARS = pl.BlockSpec(memory_space=pltpu.SMEM)
+VECTORS = pl.BlockSpec(memory_space=pltpu.VMEM)
+
+
+def moment_block(gradient, error, block):
+    columns = pl.ds(pl.multiple_of(block * BLOCK, BLOCK), BLOCK)
+    return gradient[0, :, columns].astype(jnp.float32) + error[0, :, columns].astype(jnp.float32)
 
 
 def split_kernel(core_ref, gradient, error, keep, give):
@@ -27,21 +35,16 @@
     for x in range(chips):
         for out, core in ((keep, core_ref[0]), (give, 1 - core_ref[0])):
             for k in range(own // BLOCK):
-                start = pl.multiple_of((k * CORES * chips + CORES * x + core) * BLOCK, BLOCK)
-                g, e = (ref[0, :, pl.ds(start, BLOCK)].astype(jnp.float32) for ref in (gradient, error))
-                out[x, :, k * BLOCK:(k + 1) * BLOCK] = g + e
+                out[x, :, k * BLOCK:(k + 1) * BLOCK] = moment_block(
+                    gradient, error, CORES * (k * chips + x) + core)
 
 
 def split_moment(core, gradient, error, own):
     _, rows, cols = gradient.shape
-    chips = cols // own // CORES
-    band = pl.BlockSpec((1, SLAB, cols), lambda i, core: (0, i, 0))
-    part = pl.BlockSpec((chips, SLAB, own), lambda i, core: (0, i, 0))
-    shape = jax.ShapeDtypeStruct((chips, rows, own), jnp.float32)
+    shape = jax.ShapeDtypeStruct((cols // own // CORES, rows, own), jnp.float32)
     return pl.pallas_call(
         split_kernel,
-        grid_spec=pltpu.PrefetchScalarGridSpec(
-            num_scalar_prefetch=1, grid=(rows // SLAB,), in_specs=[band, band], out_specs=[part, part]),
+        in_specs=[SCALARS, VECTORS, VECTORS],
         out_shape=[shape, shape],
         cost_estimate=pl.CostEstimate(flops=rows * cols, bytes_accessed=8 * rows * cols, transcendentals=0),
         compiler_params=PARAMS,
@@ -50,16 +53,11 @@
 
 
 def product_kernel(outer_ref, parts, *refs):
-    *lists, mean, copies, q_list = refs
+    *blocks, mean, copies, q_list = refs
     mean[...] = (parts[0] + parts[1] + parts[2] + parts[3]) * (1.0 / copies.shape[0])
-    near = lists[0].shape[0]
-    for i, piece in enumerate(lists):
-        q_list[i * near:(i + 1) * near] = piece[...]
-    blocks = []
-    for a in range(q_list.shape[0]):
-        apart = outer_ref[0] ^ a
-        blocks.append(q_list[((apart & 3) << 1) | (apart >> 2)])
-    q_own = jnp.concatenate(blocks, axis=1)
+    for apart, block in enumerate(blocks):
+        q_list[apart] = block[...]
+    q_own = jnp.concatenate([q_list[outer_ref[0] ^ a] for a in range(len(blocks))], axis=1)
     p = lax.dot_general(mean[...], q_own, (((1,), (1,)), ((), ())), precision=HIGHEST,
                         preferred_element_type=jnp.float32)
     half = p.shape[0] // 2
@@ -68,23 +66,19 @@
         copies[r] = folded
 
 
-def product(outer, parts, lists, replicas):
+def product(outer, parts, blocks, replicas):
     _, rows, own = parts.shape
-    near, rank, _ = lists[0].shape
-    full = lambda *shape: pl.BlockSpec(shape, lambda i, outer: (0,) * len(shape))
+    rank = blocks[0].shape[0]
     return pl.pallas_call(
         product_kernel,
-        grid_spec=pltpu.PrefetchScalarGridSpec(
-            num_scalar_prefetch=1, grid=(1,),
-            in_specs=[full(*parts.shape)] + [full(*piece.shape) for piece in lists],
-            out_specs=[full(rows, own), full(replicas, rows // 2, 2 * rank)],
-            scratch_shapes=[pltpu.VMEM((near * len(lists), rank, BLOCK), jnp.float32)]),
+        in_specs=[SCALARS, VECTORS] + [VECTORS] * len(blocks),
         out_shape=[jax.ShapeDtypeStruct((rows, own), jnp.float32),
                    jax.ShapeDtypeStruct((replicas, rows // 2, 2 * rank), jnp.float32)],
+        scratch_shapes=[pltpu.VMEM((len(blocks), rank, BLOCK), jnp.float32)],
         cost_estimate=pl.CostEstimate(flops=2 * rows * own * rank, bytes_accessed=4 * parts.size, transcendentals=0),
         compiler_params=PARAMS,
         name="product",
-    )(outer, parts, *lists)
+    )(outer, parts, *blocks)
 
 
 def pack_kernel(p_parts, mean, p_mean, tiles):
@@ -181,54 +175,83 @@
     )(p_mean, inverse)
 
 
-def update_kernel(place, weights, inverse, mine, theirs, gradient, error, out, right):
-    chips, blocks, rank, _ = mine.shape
-    core, block, chip, parity = (place[i] for i in range(4))
-    high = weights[...].astype(jnp.bfloat16)
-    low = (weights[...] - high.astype(jnp.float32)).astype(jnp.bfloat16)
-    factor = jnp.concatenate([high, low], axis=0)
-    rows = high.shape[0]
-    for a in range(blocks):
-        for x in range(chips):
-            own, other = mine[x, a], theirs[x, a]
-            s = jnp.concatenate([jnp.where(core == 0, own, other), jnp.where(core == 0, other, own)], axis=1)
-            s_high = s.astype(jnp.bfloat16)
-            s_low = (s - s_high.astype(jnp.float32)).astype(jnp.bfloat16)
-            stack = jnp.concatenate([s_high, s_low], axis=0)
-            change = jnp.dot(factor, stack, preferred_element_type=jnp.float32)
-            start = CORES * (a * chips + x) * BLOCK
-            columns = slice(start, start + CORES * BLOCK)
-            moment = gradient[0, :, columns].astype(jnp.float32) + error[0, :, columns].astype(jnp.float32)
-            out[0, :, columns] = (moment - (change[:rows] + change[rows:])).astype(out.dtype)
-
-    @pl.when(pl.program_id(0) == block // blocks)
-    def _():
-        within = block % blocks
-        s = jnp.where(core == parity, mine[chip, within], theirs[chip, within])
-        right[...] = jnp.dot(inverse[...], s, precision=HIGHEST, preferred_element_type=jnp.float32)
-
-
-def update_error(place, weights, inverse, mine, theirs, gradient, error):
+def halves(value, axis):
+    high = value.astype(jnp.bfloat16)
+    low = (value - high.astype(jnp.float32)).astype(jnp.bfloat16)
+    return jnp.concatenate([high, low], axis=axis)
+
+
+def remainder(factor, s, x, a, core, gradient, error):
+    chips, _, rank, _ = s.shape
+    stack = halves(jnp.concatenate([s[x, a], s[x + 1, a]], axis=1), 0)
+    change = jnp.dot(factor, stack, preferred_element_type=jnp.float32)
+    rows = change.shape[0] // 2
+    change = change[:rows] + change[rows:]
+    return [
+        (moment_block(gradient, error, CORES * (a * chips + x + i) + core)
+         - change[:, i * BLOCK:(i + 1) * BLOCK]).astype(gradient.dtype)
+        for i in range(2)]
+
+
+def near_kernel(place, weights, mine, gradient, error, out):
+    chips, groups, _, _ = mine.shape
+    factor = halves(weights[...], 0)
+    for a in range(groups):
+        for x in range(0, chips, 2):
+            out[x, a], out[x + 1, a] = remainder(factor, mine, x, a, place[0], gradient, error)
+
+
+def update_near(place, weights, mine, gradient, error):
     _, rows, cols = gradient.shape
     chips, groups, rank, _ = mine.shape
-    steps = 4
-    factor = pl.BlockSpec(weights.shape, lambda a, place: (0, 0))
-    lower = pl.BlockSpec(inverse.shape, lambda a, place: (0, 0))
-    tiles = pl.BlockSpec((chips, groups // steps, rank, BLOCK), lambda a, place: (0, a, 0, 0))
-    band = pl.BlockSpec((1, rows, cols // steps), lambda a, place: (0, 0, a))
-    right = pl.BlockSpec((rank, BLOCK), lambda a, place: (0, 0))
-    return pl.pallas_call(
-        update_kernel,
-        grid_spec=pltpu.PrefetchScalarGridSpec(
-            num_scalar_prefetch=1, grid=(steps,),
-            in_specs=[factor, lower, tiles, tiles, band, band], out_specs=[band, right]),
+    return pl.pallas_call(
+        near_kernel,
+        in_specs=[SCALARS] + [VECTORS] * 4,
+        out_shape=jax.ShapeDtypeStruct((chips, groups, rows, BLOCK), gradient.dtype),
+        cost_estimate=pl.CostEstimate(
+            flops=4 * rows * cols * rank, bytes_accessed=4 * rows * cols, transcendentals=0),
+        compiler_params=PARAMS,
+        name="update_near",
+    )(place, weights, mine, gradient, error)
+
+
+def far_kernel(place, weights, inverse, mine, theirs, near, gradient, error, out, right, bands, done):
+    chips, groups, _, _ = mine.shape
+    core, block, chip, parity = (place[i] for i in range(4))
+    factor = halves(weights[...], 0)
+    copies = []
+    for a in range(groups):
+        for x in range(0, chips, 2):
+            far = remainder(factor, theirs, x, a, 1 - core, gradient, error)
+            for i in range(2):
+                for value, owner in ((near[x + i, a], core), (far[i], 1 - core)):
+                    start = pl.multiple_of((CORES * (x + i) + owner) * BLOCK, BLOCK)
+                    bands[a, :, pl.ds(start, BLOCK)] = value
+        width = bands.shape[2]
+        copies.append(pltpu.make_async_copy(bands.at[a], out.at[0, :, a * width:(a + 1) * width], done.at[a]))
+        copies[a].start()
+    s = jnp.where(core == parity, mine[chip, block], theirs[chip, block])
+    right[...] = jnp.dot(inverse[...], s, precision=HIGHEST, preferred_element_type=jnp.float32)
+    for copy in copies:
+        copy.wait()
+
+
+def update_far(place, weights, inverse, mine, theirs, near, gradient, error):
+    _, rows, cols = gradient.shape
+    chips, groups, rank, _ = mine.shape
+    return pl.pallas_call(
+        far_kernel,
+        in_specs=[SCALARS] + [VECTORS] * 7,
+        out_specs=[pl.BlockSpec(memory_space=pl.ANY), VECTORS],
         out_shape=[jax.ShapeDtypeStruct(gradient.shape, gradient.dtype),
                    jax.ShapeDtypeStruct((rank, BLOCK), jnp.float32)],
+        scratch_shapes=[pltpu.VMEM((groups, rows, cols // groups), gradient.dtype),
+                        pltpu.SemaphoreType.DMA((groups,))],
         cost_estimate=pl.CostEstimate(
-            flops=8 * rows * cols * rank, bytes_accessed=6 * rows * cols + 8 * rank * cols, transcendentals=0),
-        compiler_params=PARAMS,
-        name="update_error",
-    )(place, weights, inverse, mine, theirs, gradient, error)
+            flops=4 * rows * cols * rank, bytes_accessed=6 * rows * cols, transcendentals=0),
+        compiler_params=PARAMS,
+        name="update_far",
+    )(place, weights, inverse, mine, theirs, near, gradient, error)
 
 
 def body(gradient, error, q_prev):
@@ -244,17 +267,15 @@
     outer, inner = shard // replicas, shard % replicas
     chip_groups = [[c + CORES * x for x in range(replicas // CORES)] for c in range(CORES)]
 
+    keep, give = split_moment(core.reshape(1), gradient, error, own)
+    paired, q_block = lax.optimization_barrier((keep + swap_cores(give, replicas), q_prev.T))
+    parts = exchange(paired, "replica", chip_groups)
+
     def along(apart):
         return [(r * shards + o * replicas + i, i * shards + (o ^ apart) * replicas + r)
                 for r in range(replicas) for o in range(groups) for i in range(replicas)]
-    near = [lax.ppermute(q_prev.T[None], ("replica", "mp"), along(apart)) for apart in (0, 4)]
-
-    keep, give = split_moment(core.reshape(1), gradient, error, own)
-    paired, near = lax.optimization_barrier((keep + swap_cores(give, replicas), jnp.concatenate(near, axis=0)))
-    parts = exchange(paired, "replica", chip_groups)
-    lists = [near] + [
-        lax.ppermute(near, "mp", [(j, j ^ (apart * replicas)) for j in range(shards)]) for apart in (1, 2, 3)]
-    mean, copies = product(outer.reshape(1), parts, lists, replicas)
+    blocks = [lax.ppermute(q_block, ("replica", "mp"), along(apart)) for apart in range(groups)]
+    mean, copies = product(outer.reshape(1), parts, blocks, replicas)
 
     p_mean, tiles = pack(exchange(copies, "replica"), mean, shards)
     packed = (shards, PACK, 1, BLOCK)
@@ -272,7 +293,8 @@
     theirs = swap_cores(mine, replicas)
 
     place = jnp.stack([core, outer, inner // CORES, inner % CORES])
-    new_error, right = update_error(place, weights, inverse, mine, theirs, gradient, error)
+    near = update_near(place, weights, mine, gradient, error)
+    new_error, right = update_far(place, weights, inverse, mine, theirs, near, gradient, error)
     return (new_error, right.T, p_factor)
 
 

time: 134 us -> 166 us (1.24)
  blocking collectives: 51.2 us -> 79.7 us
  starting transfers between devices: 48.8 us -> 55.2 us
  waiting for transfers between devices: 8.19 us -> 5.02 us
    all_to_all x3, blocking collectives: 51.2 us -> 79.7 us  [exchange(): return lax.all_to_all(value, axis, 0, 0, axis_index_groups=groups)]
    ppermute x5 -> x8, starting transfers between devices: 17.9 us -> 33.4 us  [body(): lax.ppermute(q_block, ('replica', 'mp'), along(apart))]
    all_to_all x2, starting transfers between devices: 16.4 us -> 7.3 us  [exchange(): return lax.all_to_all(value, axis, 0, 0, axis_index_groups=groups)]
    ppermute x5 -> x8, waiting for transfers between devices: 5.9 us -> 1.54 us  [body(): lax.ppermute(q_block, ('replica', 'mp'), along(apart))]
    pallas_call x3 -> x4, Pallas kernels: 5.89 us -> 5.31 us  [the longest x1 3.21 us: update_far(): pl.pallas_call(far_kernel, in_specs=[SCALARS] + [VECTORS] * 7, out_specs=...]
  transfers between devices with their start and end apart: 9 -> 12, of which waited for: 4 -> 3; matrix products, arithmetic and copies ran while one was open for 9% -> 8% of each run, Pallas kernels for 1% -> 1%
where the time goes in v4:
time: 166 us; the launch traced here: 165 us
  blocking collectives  79.7 us (48%)
  starting transfers between devices  55.2 us (33%)
  other arithmetic  13.3 us (8%)
  Pallas kernels  6.87 us (4%)
  waiting for transfers between devices  5.02 us (3%)
  local copies, waits for them, and re-layouts  3.49 us (2%)
    all_to_all x3, blocking collectives, exchange(): return lax.all_to_all(value, axis, 0, 0, axis_index_groups=groups)  79.7 us
    ppermute x8, starting transfers between devices, body(): lax.ppermute(q_block, ('replica', 'mp'), along(apart))  33.4 us
    ppermute x2, starting transfers between devices, swap_cores(): return lax.ppermute(value, 'replica', [(r, r ^ 1) for r in range(replicas)])  14.5 us
    all_to_all x2, starting transfers between devices, exchange(): return lax.all_to_all(value, axis, 0, 0, axis_index_groups=groups)  7.3 us
    another operation x3, other arithmetic, body(): lower = jnp.linalg.cholesky(gram)  6.52 us
    another operation x2, other arithmetic, body(): lax.linalg.triangular_solve(lower, jnp.eye(rank, dtype=jnp.float32), left...  5.55 us
    ppermute x2, waiting for transfers between devices, swap_cores(): return lax.ppermute(value, 'replica', [(r, r ^ 1) for r in range(replicas)])  3.47 us
    unnamed x12, local copies, waits for them, and re-layouts  3.42 us
  transfers between devices with their start and end apart: 12, of which 3 were waited for; matrix products, arithmetic and copies ran while one was open for 8% of the time, Pallas kernels for 1%

profile of v4, /device:TPU:1, one launch (start us, length us, event | category | flops | bytes accessed | tf_op | source)
XLA Modules:
  0.0 164.7 jit_solution(1636961268215373259)
XLA Ops:
  0.6 0.0 copy-start
  0.7 1.2 copy-done
  1.9 1.2 copy-done.2
  3.1 0.5 split_moment.1
  3.6 8.8 %collective-permute-start = (f32[4,64,1024]{2,1,0:T(8,128)S(1)}, f32[4,64,1024]{2,1,0:T(8,128)S(1)}, u32[]{:S(2)}, u32[]{:S(2)}) collective-permute-start(f32[4,64,1024]{2,1,0:T(8,128)S(1)} %get-tuple-element.21), channel_id=1, source_target_pairs={{0,64},{64,0},{128,192},{192,128},{256,320},{320,256},{384,448},{4... | collective-permute-start | bytes 3145736 | tf_op jit(solution)/shard_map/ppermute | solution.py:21
  12.4 2.3 %collective-permute-done = f32[4,64,1024]{2,1,0:T(8,128)S(1)} collective-permute-done((f32[4,64,1024]{2,1,0:T(8,128)S(1)}, f32[4,64,1024]{2,1,0:T(8,128)S(1)}, u32[]{:S(2)}, u32[]{:S(2)}) %collective-permute-start) | collective-permute-done | bytes 1048608 | tf_op jit(solution)/shard_map/ppermute | solution.py:21
  14.7 1.2 add.29
  15.9 3.6 %all-to-all-start = ((f32[4,64,1024]{2,1,0:T(8,128)}), f32[4,64,1024]{2,1,0:T(8,128)S(1)}, u32[]{:S(2)}, u32[]{:S(2)}) async-start(f32[4,64,1024]{2,1,0:T(8,128)} %add.29), calls=%async_computation | async-start | bytes 2097152 | tf_op jit(solution)/shard_map/all_to_all | solution.py:17
  19.5 7.3 %collective-permute-start.8 = (f32[64,128]{1,0:T(8,128)S(1)}, f32[64,128]{1,0:T(8,128)S(1)}, u32[]{:S(2)}, u32[]{:S(2)}) collective-permute-start(f32[64,128]{1,0:T(8,128)S(1)} %bitcast.23), channel_id=1, source_target_pairs={{0,56},{1,120},{2,184},{3,248},{4,312},{5,376},{6,440},{7,504},{8,... | collective-permute-start | bytes 98312 | tf_op jit(solution)/shard_map/ppermute | solution.py:277
  26.8 1.9 %collective-permute-start.7 = (f32[64,128]{1,0:T(8,128)S(1)}, f32[64,128]{1,0:T(8,128)S(1)}, u32[]{:S(2)}, u32[]{:S(2)}) collective-permute-start(f32[64,128]{1,0:T(8,128)S(1)} %bitcast.24), channel_id=1, source_target_pairs={{0,48},{1,112},{2,176},{3,240},{4,304},{5,368},{6,432},{7,496},{8,... | collective-permute-start | bytes 98312 | tf_op jit(solution)/shard_map/ppermute | solution.py:277
  28.8 5.7 %collective-permute-start.6 = (f32[64,128]{1,0:T(8,128)S(1)}, f32[64,128]{1,0:T(8,128)S(1)}, u32[]{:S(2)}, u32[]{:S(2)}) collective-permute-start(f32[64,128]{1,0:T(8,128)S(1)} %bitcast.25), channel_id=1, source_target_pairs={{0,40},{1,104},{2,168},{3,232},{4,296},{5,360},{6,424},{7,488},{8,... | collective-permute-start | bytes 98312 | tf_op jit(solution)/shard_map/ppermute | solution.py:277
  34.5 4.6 %collective-permute-start.5 = (f32[64,128]{1,0:T(8,128)S(1)}, f32[64,128]{1,0:T(8,128)S(1)}, u32[]{:S(2)}, u32[]{:S(2)}) collective-permute-start(f32[64,128]{1,0:T(8,128)S(1)} %bitcast.26), channel_id=1, source_target_pairs={{0,32},{1,96},{2,160},{3,224},{4,288},{5,352},{6,416},{7,480},{8,4... | collective-permute-start | bytes 98312 | tf_op jit(solution)/shard_map/ppermute | solution.py:277
  39.2 2.7 %collective-permute-start.4 = (f32[64,128]{1,0:T(8,128)S(1)}, f32[64,128]{1,0:T(8,128)S(1)}, u32[]{:S(2)}, u32[]{:S(2)}) collective-permute-start(f32[64,128]{1,0:T(8,128)S(1)} %bitcast.27), channel_id=1, source_target_pairs={{0,24},{1,88},{2,152},{3,216},{4,280},{5,344},{6,408},{7,472},{8,1... | collective-permute-start | bytes 98312 | tf_op jit(solution)/shard_map/ppermute | solution.py:277
  41.9 0.0 collective-permute-done.8.refs_7_
  41.9 3.8 %collective-permute-start.3 = (f32[64,128]{1,0:T(8,128)S(1)}, f32[64,128]{1,0:T(8,128)S(1)}, u32[]{:S(2)}, u32[]{:S(2)}) collective-permute-start(f32[64,128]{1,0:T(8,128)S(1)} %bitcast.28), channel_id=1, source_target_pairs={{0,16},{1,80},{2,144},{3,208},{4,272},{5,336},{6,400},{7,464},{8,2... | collective-permute-start | bytes 98312 | tf_op jit(solution)/shard_map/ppermute | solution.py:277
  45.6 0.0 collective-permute-done.7.refs_6_
  45.7 3.6 %collective-permute-start.2 = (f32[64,128]{1,0:T(8,128)S(1)}, f32[64,128]{1,0:T(8,128)S(1)}, u32[]{:S(2)}, u32[]{:S(2)}) collective-permute-start(f32[64,128]{1,0:T(8,128)S(1)} %bitcast.29), channel_id=1, source_target_pairs={{0,8},{1,72},{2,136},{3,200},{4,264},{5,328},{6,392},{7,456},{8,0}... | collective-permute-start | bytes 98312 | tf_op jit(solution)/shard_map/ppermute | solution.py:277
  49.3 0.0 collective-permute-done.6.refs_5_
  49.3 3.7 %collective-permute-start.1 = (f32[64,128]{1,0:T(8,128)S(1)}, f32[64,128]{1,0:T(8,128)S(1)}, u32[]{:S(2)}, u32[]{:S(2)}) collective-permute-start(f32[64,128]{1,0:T(8,128)S(1)} %bitcast.30), channel_id=1, source_target_pairs={{0,0},{1,64},{2,128},{3,192},{4,256},{5,320},{6,384},{7,448},{8,8}... | collective-permute-start | bytes 98312 | tf_op jit(solution)/shard_map/ppermute | solution.py:277
  53.1 0.0 collective-permute-done.5.refs_4_
  53.1 0.0 collective-permute-done.4.refs_3_
  53.1 0.0 collective-permute-done.3.refs_2_
  53.1 0.0 collective-permute-done.2.refs_1_
  53.1 1.5 collective-permute-done.1.refs_0_
  54.6 0.0 all-to-all-done.parts
  54.6 0.5 product.1
  55.1 37.1 %all_to_all.25.p_parts = f32[8,32,128]{2,1,0:T(8,128)S(1)} all-to-all(f32[8,32,128]{2,1,0:T(8,128)S(1)} %get-tuple-element.24), channel_id=1, replica_groups=mesh['replica'=8,'mp'=64] {'replica'}, dimensions={0} | all-to-all | bytes 262144 | tf_op jit(solution)/shard_map/all_to_all | solution.py:17
  92.2 0.6 pack.1
  92.8 24.2 %all_to_all.26 = f32[64,9,1,128]{3,2,1,0:T(1,128)S(1)} all-to-all(f32[64,9,1,128]{3,2,1,0:T(1,128)S(1)} %bitcast.22), channel_id=1, replica_groups=mesh['replica'=8,'mp'=64] {'mp'}, dimensions={0} | all-to-all | bytes 589824 | tf_op jit(solution)/shard_map/all_to_all | solution.py:17
  117.0 0.1 total.1
  117.1 18.4 %all_to_all.27 = f32[64,9,1,128]{3,2,1,0:T(1,128)S(1)} all-to-all(f32[64,9,1,128]{3,2,1,0:T(1,128)S(1)} %bitcast.21), channel_id=1, replica_groups=mesh['replica'=8,'mp'=64] {'mp'}, dimensions={0} | all-to-all | bytes 589824 | tf_op jit(solution)/shard_map/all_to_all | solution.py:17
  135.5 0.1 unpack.1
  135.6 0.0 copy-start.4
  135.6 1.0 copy-done.4
  136.5 3.6 %all-to-all-start.4 = ((f32[4,8,64,128]{3,2,1,0:T(8,128)}), f32[4,8,64,128]{3,2,1,0:T(8,128)S(1)}, u32[]{:S(2)}, u32[]{:S(2)}) async-start(f32[4,8,64,128]{3,2,1,0:T(8,128)} %copy-done.4), calls=%async_computation.4 | async-start | bytes 2097152 | tf_op jit(solution)/shard_map/all_to_all | solution.py:17
  140.2 0.1 copy.10
  140.3 5.8 %cholesky.17 = f32[64,64]{1,0:T(8,128)S(1)} custom-call(f32[64,64]{1,0:T(8,128)S(1)} %fusion.3), custom_call_target="Cholesky" | custom-call | tf_op jit(solution)/shard_map/jit(cholesky)/cholesky | solution.py:287
  146.2 0.6 compare_reduce_fusion
  146.8 0.7 fusion
  147.5 4.9 %custom-call.6 = f32[1,64,64]{1,2,0:T(8,128)S(1)} custom-call(f32[1,64,64]{2,1,0:T(8,128)S(1)} %fusion), custom_call_target="InvertDiagBlocksLowerTriangular" | custom-call | tf_op jit(solution)/shard_map/triangular_solve | solution.py:288
  152.4 0.2 fusion.1.inverse
  152.6 0.8 factors.1
  153.4 0.0 all-to-all-done.4.mine
  153.4 5.7 %collective-permute-start.9 = (f32[4,8,64,128]{3,2,1,0:T(8,128)S(1)}, f32[4,8,64,128]{3,2,1,0:T(8,128)}, u32[]{:S(2)}, u32[]{:S(2)}) collective-permute-start(f32[4,8,64,128]{3,2,1,0:T(8,128)S(1)} %all-to-all-done.4.mine), channel_id=1, source_target_pairs={{0,64},{64,0},{128,192},{192,128},{256,320},{320,256},{384,448},{4... | collective-permute-start | bytes 3145736 | tf_op jit(solution)/shard_map/ppermute | solution.py:21
  159.2 0.1 pad_add_fusion.place
  159.2 1.1 update_near.1.near
  160.3 1.2 collective-permute-done.9.theirs
  161.5 3.2 %update_far.1 = (bf16[1,64,8192]{2,1,0:T(8,128)(2,1)}, f32[64,128]{1,0:T(8,128)}) custom-call(s32[4]{0:T(128)S(1)} %pad_add_fusion.place, f32[64,128]{1,0:T(8,128)S(1)} %get-tuple-element.31.weights, f32[64,64]{1,0:T(8,128)S(1)} %fusion.1.inverse, f32[4,8,64,128]{3,2,1,0:T(8,128)S(1)} %all-to-all-done.4.mine, ...), custom_call_target="tpu_custom_call" | custom-call | flops 134217728 | bytes 3145728 | tf_op jit(solution)/shard_map/update_far/pallas_call | solution.py:242
  (9 shorter events, 0.1 us)
Async XLA Ops:
  0.6 1.2 copy-start
  1.9 1.2 copy-start.2
  3.6 11.1 %collective-permute-start = (f32[4,64,1024]{2,1,0:T(8,128)S(1)}, f32[4,64,1024]{2,1,0:T(8,128)S(1)}, u32[]{:S(2)}, u32[]{:S(2)}) collective-permute-start(f32[4,64,1024]{2,1,0:T(8,128)S(1)} %get-tuple-element.21), channel_id=1, source_target_pairs={{0,64},{64,0},{128,192},{192,128},{256,320},{320,256},{384,448},{4... | collective-permute-start | bytes 3145736 | tf_op jit(solution)/shard_map/ppermute | solution.py:21
  15.9 3.7 %copy-start.5 = (f32[128,64]{0,1:T(8,128)S(1)}, f32[128,64]{0,1:T(8,128)}, u32[]{:S(2)}) copy-start(f32[128,64]{0,1:T(8,128)} %param.5) | copy-start | bytes 98308
  15.9 38.8 %all-to-all-start = ((f32[4,64,1024]{2,1,0:T(8,128)}), f32[4,64,1024]{2,1,0:T(8,128)S(1)}, u32[]{:S(2)}, u32[]{:S(2)}) async-start(f32[4,64,1024]{2,1,0:T(8,128)} %add.29), calls=%async_computation | async-start | bytes 2097152 | tf_op jit(solution)/shard_map/all_to_all | solution.py:17
  19.5 22.4 %collective-permute-start.8 = (f32[64,128]{1,0:T(8,128)S(1)}, f32[64,128]{1,0:T(8,128)S(1)}, u32[]{:S(2)}, u32[]{:S(2)}) collective-permute-start(f32[64,128]{1,0:T(8,128)S(1)} %bitcast.23), channel_id=1, source_target_pairs={{0,56},{1,120},{2,184},{3,248},{4,312},{5,376},{6,440},{7,504},{8,... | collective-permute-start | bytes 98312 | tf_op jit(solution)/shard_map/ppermute | solution.py:277
  26.8 18.8 %collective-permute-start.7 = (f32[64,128]{1,0:T(8,128)S(1)}, f32[64,128]{1,0:T(8,128)S(1)}, u32[]{:S(2)}, u32[]{:S(2)}) collective-permute-start(f32[64,128]{1,0:T(8,128)S(1)} %bitcast.24), channel_id=1, source_target_pairs={{0,48},{1,112},{2,176},{3,240},{4,304},{5,368},{6,432},{7,496},{8,... | collective-permute-start | bytes 98312 | tf_op jit(solution)/shard_map/ppermute | solution.py:277
  28.8 20.5 %collective-permute-start.6 = (f32[64,128]{1,0:T(8,128)S(1)}, f32[64,128]{1,0:T(8,128)S(1)}, u32[]{:S(2)}, u32[]{:S(2)}) collective-permute-start(f32[64,128]{1,0:T(8,128)S(1)} %bitcast.25), channel_id=1, source_target_pairs={{0,40},{1,104},{2,168},{3,232},{4,296},{5,360},{6,424},{7,488},{8,... | collective-permute-start | bytes 98312 | tf_op jit(solution)/shard_map/ppermute | solution.py:277
  34.5 18.6 %collective-permute-start.5 = (f32[64,128]{1,0:T(8,128)S(1)}, f32[64,128]{1,0:T(8,128)S(1)}, u32[]{:S(2)}, u32[]{:S(2)}) collective-permute-start(f32[64,128]{1,0:T(8,128)S(1)} %bitcast.26), channel_id=1, source_target_pairs={{0,32},{1,96},{2,160},{3,224},{4,288},{5,352},{6,416},{7,480},{8,4... | collective-permute-start | bytes 98312 | tf_op jit(solution)/shard_map/ppermute | solution.py:277
  39.2 13.9 %collective-permute-start.4 = (f32[64,128]{1,0:T(8,128)S(1)}, f32[64,128]{1,0:T(8,128)S(1)}, u32[]{:S(2)}, u32[]{:S(2)}) collective-permute-start(f32[64,128]{1,0:T(8,128)S(1)} %bitcast.27), channel_id=1, source_target_pairs={{0,24},{1,88},{2,152},{3,216},{4,280},{5,344},{6,408},{7,472},{8,1... | collective-permute-start | bytes 98312 | tf_op jit(solution)/shard_map/ppermute | solution.py:277
  41.9 11.2 %collective-permute-start.3 = (f32[64,128]{1,0:T(8,128)S(1)}, f32[64,128]{1,0:T(8,128)S(1)}, u32[]{:S(2)}, u32[]{:S(2)}) collective-permute-start(f32[64,128]{1,0:T(8,128)S(1)} %bitcast.28), channel_id=1, source_target_pairs={{0,16},{1,80},{2,144},{3,208},{4,272},{5,336},{6,400},{7,464},{8,2... | collective-permute-start | bytes 98312 | tf_op jit(solution)/shard_map/ppermute | solution.py:277
  45.7 7.4 %collective-permute-start.2 = (f32[64,128]{1,0:T(8,128)S(1)}, f32[64,128]{1,0:T(8,128)S(1)}, u32[]{:S(2)}, u32[]{:S(2)}) collective-permute-start(f32[64,128]{1,0:T(8,128)S(1)} %bitcast.29), channel_id=1, source_target_pairs={{0,8},{1,72},{2,136},{3,200},{4,264},{5,328},{6,392},{7,456},{8,0}... | collective-permute-start | bytes 98312 | tf_op jit(solution)/shard_map/ppermute | solution.py:277
  49.3 5.3 %collective-permute-start.1 = (f32[64,128]{1,0:T(8,128)S(1)}, f32[64,128]{1,0:T(8,128)S(1)}, u32[]{:S(2)}, u32[]{:S(2)}) collective-permute-start(f32[64,128]{1,0:T(8,128)S(1)} %bitcast.30), channel_id=1, source_target_pairs={{0,0},{1,64},{2,128},{3,192},{4,256},{5,320},{6,384},{7,448},{8,8}... | collective-permute-start | bytes 98312 | tf_op jit(solution)/shard_map/ppermute | solution.py:277
  135.6 1.0 copy-start.4
  136.5 22.7 %copy-start.1 = (bf16[1,64,8192]{2,1,0:T(8,128)(2,1)S(1)}, bf16[1,64,8192]{2,1,0:T(8,128)(2,1)}, u32[]{:S(2)}) copy-start(bf16[1,64,8192]{2,1,0:T(8,128)(2,1)} %gradient.5) | copy-start | bytes 3145732
  136.5 22.7 %copy-start.3 = (bf16[1,64,8192]{2,1,0:T(8,128)(2,1)S(1)}, bf16[1,64,8192]{2,1,0:T(8,128)(2,1)}, u32[]{:S(2)}) copy-start(bf16[1,64,8192]{2,1,0:T(8,128)(2,1)} %error.5) | copy-start | bytes 3145732
  136.5 16.9 %all-to-all-start.4 = ((f32[4,8,64,128]{3,2,1,0:T(8,128)}), f32[4,8,64,128]{3,2,1,0:T(8,128)S(1)}, u32[]{:S(2)}, u32[]{:S(2)}) async-start(f32[4,8,64,128]{3,2,1,0:T(8,128)} %copy-done.4), calls=%async_computation.4 | async-start | bytes 2097152 | tf_op jit(solution)/shard_map/all_to_all | solution.py:17
  153.4 8.1 %collective-permute-start.9 = (f32[4,8,64,128]{3,2,1,0:T(8,128)S(1)}, f32[4,8,64,128]{3,2,1,0:T(8,128)}, u32[]{:S(2)}, u32[]{:S(2)}) collective-permute-start(f32[4,8,64,128]{3,2,1,0:T(8,128)S(1)} %all-to-all-done.4.mine), channel_id=1, source_target_pairs={{0,64},{64,0},{128,192},{192,128},{256,320},{320,256},{384,448},{4... | collective-permute-start | bytes 3145736 | tf_op jit(solution)/shard_map/ppermute | solution.py:21

commit v5 on v4

--- a/solution.py
+++ b/solution.py
@@ -30,16 +30,17 @@
     return gradient[0, :, columns].astype(jnp.float32) + error[0, :, columns].astype(jnp.float32)
 
 
-def split_kernel(core_ref, gradient, error, keep, give):
+def split_kernel(place, gradient, error, keep, give):
     chips, _, own = keep.shape
-    for x in range(chips):
-        for out, core in ((keep, core_ref[0]), (give, 1 - core_ref[0])):
+    for apart in range(chips):
+        chip = place[1] ^ apart
+        for out, core in ((keep, place[0]), (give, 1 - place[0])):
             for k in range(own // BLOCK):
-                out[x, :, k * BLOCK:(k + 1) * BLOCK] = moment_block(
-                    gradient, error, CORES * (k * chips + x) + core)
-
-
-def split_moment(core, gradient, error, own):
+                out[apart, :, k * BLOCK:(k + 1) * BLOCK] = moment_block(
+                    gradient, error, CORES * (k * chips + chip) + core)
+
+
+def split_moment(place, gradient, error, own):
     _, rows, cols = gradient.shape
     shape = jax.ShapeDtypeStruct((cols // own // CORES, rows, own), jnp.float32)
     return pl.pallas_call(
@@ -49,15 +50,12 @@
         cost_estimate=pl.CostEstimate(flops=rows * cols, bytes_accessed=8 * rows * cols, transcendentals=0),
         compiler_params=PARAMS,
         name="split_moment",
-    )(core, gradient, error)
-
-
-def product_kernel(outer_ref, parts, *refs):
-    *blocks, mean, copies, q_list = refs
-    mean[...] = (parts[0] + parts[1] + parts[2] + parts[3]) * (1.0 / copies.shape[0])
-    for apart, block in enumerate(blocks):
-        q_list[apart] = block[...]
-    q_own = jnp.concatenate([q_list[outer_ref[0] ^ a] for a in range(len(blocks))], axis=1)
+    )(place, gradient, error)
+
+
+def product_kernel(own, one, two, three, q_blocks, mean, copies):
+    mean[...] = (own[...] + one[...] + two[...] + three[...]) * (1.0 / copies.shape[0])
+    q_own = jnp.concatenate([q_blocks[a] for a in range(q_blocks.shape[0])], axis=1)
     p = lax.dot_general(mean[...], q_own, (((1,), (1,)), ((), ())), precision=HIGHEST,
                         preferred_element_type=jnp.float32)
     half = p.shape[0] // 2
@@ -66,19 +64,18 @@
         copies[r] = folded
 
 
-def product(outer, parts, blocks, replicas):
-    _, rows, own = parts.shape
-    rank = blocks[0].shape[0]
+def product(parts, q_blocks, replicas):
+    rows, own = parts[0].shape
+    rank = q_blocks.shape[1]
     return pl.pallas_call(
         product_kernel,
-        in_specs=[SCALARS, VECTORS] + [VECTORS] * len(blocks),
         out_shape=[jax.ShapeDtypeStruct((rows, own), jnp.float32),
                    jax.ShapeDtypeStruct((replicas, rows // 2, 2 * rank), jnp.float32)],
-        scratch_shapes=[pltpu.VMEM((len(blocks), rank, BLOCK), jnp.float32)],
-        cost_estimate=pl.CostEstimate(flops=2 * rows * own * rank, bytes_accessed=4 * parts.size, transcendentals=0),
+        cost_estimate=pl.CostEstimate(
+            flops=2 * rows * own * rank, bytes_accessed=4 * len(parts) * rows * own, transcendentals=0),
         compiler_params=PARAMS,
         name="product",
-    )(outer, parts, *blocks)
+    )(*parts, q_blocks)
 
 
 def pack_kernel(p_parts, mean, p_mean, tiles):
@@ -265,17 +262,24 @@
     shard = lax.axis_index("mp").astype(jnp.int32)
     core = replica % CORES
     outer, inner = shard // replicas, shard % replicas
+    outer_groups = [[o * replicas + i for o in range(groups)] for i in range(replicas)]
     chip_groups = [[c + CORES * x for x in range(replicas // CORES)] for c in range(CORES)]
 
-    keep, give = split_moment(core.reshape(1), gradient, error, own)
-    paired, q_block = lax.optimization_barrier((keep + swap_cores(give, replicas), q_prev.T))
-    parts = exchange(paired, "replica", chip_groups)
-
-    def along(apart):
-        return [(r * shards + o * replicas + i, i * shards + (o ^ apart) * replicas + r)
-                for r in range(replicas) for o in range(groups) for i in range(replicas)]
-    blocks = [lax.ppermute(q_block, ("replica", "mp"), along(apart)) for apart in range(groups)]
-    mean, copies = product(outer.reshape(1), parts, blocks, replicas)
+    q_block = lax.ppermute(q_prev.T, ("replica", "mp"), [
+        (r * shards + o * replicas + i, i * shards + o * replicas + r)
+        for r in range(replicas) for o in range(groups) for i in range(replicas)
+    ])
+
+    keep, give = split_moment(jnp.stack([core, replica // CORES]), gradient, error, own)
+    came = swap_cores(give, replicas)
+    paired = [keep[apart] + came[apart] for apart in range(replicas // CORES)]
+    *paired, q_block = lax.optimization_barrier((*paired, q_block))
+    parts = paired[:1] + [
+        lax.ppermute(paired[apart], "replica", [(r, r ^ (CORES * apart)) for r in range(replicas)])
+        for apart in range(1, len(paired))]
+    q_copies = jnp.broadcast_to(q_block[None], (groups,) + q_block.shape)
+    q_blocks = exchange(q_copies, "mp", outer_groups)
+    mean, copies = product(parts, q_blocks, replicas)
 
     p_mean, tiles = pack(exchange(copies, "replica"), mean, shards)
     packed = (shards, PACK, 1, BLOCK)

time: 166 us -> 135 us (0.81)
  blocking collectives: 79.7 us -> 53.2 us
  starting transfers between devices: 55.2 us -> 38.9 us
  waiting for transfers between devices: 5.02 us -> 17 us
    all_to_all x3, blocking collectives: 79.7 us -> 53.2 us  [exchange(): return lax.all_to_all(value, axis, 0, 0, axis_index_groups=groups)]
    ppermute x8 -> x4, starting transfers between devices: 33.4 us -> 16.1 us  [the longest x3 14.2 us: body(): lax.ppermute(paired[apart], 'replica', [(r, r ^ CORES * apart) for r in r...]
    ppermute x8 -> x4, waiting for transfers between devices: 1.54 us -> 15.5 us  [the longest x3 12.7 us: body(): lax.ppermute(paired[apart], 'replica', [(r, r ^ CORES * apart) for r in r...]
    ppermute x2, waiting for transfers between devices: 3.47 us -> 1.52 us  [swap_cores(): return lax.ppermute(value, 'replica', [(r, r ^ 1) for r in range(replicas)])]
  transfers between devices with their start and end apart: 12 -> 8, of which waited for: 3 -> 5; matrix products, arithmetic and copies ran while one was open for 8% -> 9% of each run, Pallas kernels for 1% -> 1%
where the time goes in v5:
time: 135 us; the launch traced here: 134 us
  blocking collectives  53.2 us (39%)
  starting transfers between devices  38.9 us (29%)
  waiting for transfers between devices  17 us (13%)
  other arithmetic  12.4 us (9%)
  Pallas kernels  7.4 us (5%)
  local copies, waits for them, and re-layouts  4.22 us (3%)
    all_to_all x3, blocking collectives, exchange(): return lax.all_to_all(value, axis, 0, 0, axis_index_groups=groups)  53.2 us
    ppermute x2, starting transfers between devices, swap_cores(): return lax.ppermute(value, 'replica', [(r, r ^ 1) for r in range(replicas)])  14.5 us
    ppermute x3, starting transfers between devices, body(): lax.ppermute(paired[apart], 'replica', [(r, r ^ CORES * apart) for r in r...  14.2 us
    ppermute x3, waiting for transfers between devices, body(): lax.ppermute(paired[apart], 'replica', [(r, r ^ CORES * apart) for r in r...  12.7 us
    all_to_all x2, starting transfers between devices, exchange(): return lax.all_to_all(value, axis, 0, 0, axis_index_groups=groups)  8.31 us
    another operation x3, other arithmetic, body(): lower = jnp.linalg.cholesky(gram)  6.52 us
    another operation x2, other arithmetic, body(): lax.linalg.triangular_solve(lower, jnp.eye(rank, dtype=jnp.float32), left...  5.55 us
    unnamed x12, local copies, waits for them, and re-layouts  3.42 us
  transfers between devices with their start and end apart: 8, of which 5 were waited for; matrix products, arithmetic and copies ran while one was open for 9% of the time, Pallas kernels for 1%

profile of v5, /device:TPU:1, one launch (start us, length us, event | category | flops | bytes accessed | tf_op | source)
XLA Modules:
  0.0 134.2 jit_solution(14123939500812166201)
XLA Ops:
  0.6 0.1 pad_add_fusion.1.place
  0.7 0.0 copy-start
  0.7 1.2 copy-done
  2.0 0.0 copy-start.2
  2.0 1.2 copy-done.2
  3.2 0.0 copy-start.5
  3.2 1.1 split_moment.1
  4.3 8.8 %collective-permute-start = (f32[4,64,1024]{2,1,0:T(8,128)S(1)}, f32[4,64,1024]{2,1,0:T(8,128)S(1)}, u32[]{:S(2)}, u32[]{:S(2)}) collective-permute-start(f32[4,64,1024]{2,1,0:T(8,128)S(1)} %get-tuple-element.24), channel_id=1, source_target_pairs={{0,64},{64,0},{128,192},{192,128},{256,320},{320,256},{384,448},{4... | collective-permute-start | bytes 3145736 | tf_op jit(solution)/shard_map/ppermute | solution.py:21
  13.1 0.0 copy-done.5
  13.1 1.9 %collective-permute-start.1 = (f32[64,128]{1,0:T(8,128)S(1)}, f32[64,128]{1,0:T(8,128)S(1)}, u32[]{:S(2)}, u32[]{:S(2)}) collective-permute-start(f32[64,128]{1,0:T(8,128)S(1)} %bitcast.32), channel_id=1, source_target_pairs={{0,0},{1,64},{2,128},{3,192},{4,256},{5,320},{6,384},{7,448},{8,8}... | collective-permute-start | bytes 98312 | tf_op jit(solution)/shard_map/ppermute | solution.py:268
  15.0 0.3 collective-permute-done
  15.3 0.1 fusion
  15.5 2.8 %collective-permute-done.1 = f32[64,128]{1,0:T(8,128)S(1)} collective-permute-done((f32[64,128]{1,0:T(8,128)S(1)}, f32[64,128]{1,0:T(8,128)S(1)}, u32[]{:S(2)}, u32[]{:S(2)}) %collective-permute-start.1) | collective-permute-done | bytes 32800 | tf_op jit(solution)/shard_map/ppermute | solution.py:268
  18.3 0.7 broadcast_in_dim.3
  19.0 4.7 %all-to-all-start = ((f32[8,64,128]{2,1,0:T(8,128)}), f32[8,64,128]{2,1,0:T(8,128)S(1)}, u32[]{:S(2)}, u32[]{:S(2)}) async-start(f32[8,64,128]{2,1,0:T(8,128)} %broadcast_in_dim.3), calls=%async_computation | async-start | bytes 524288 | tf_op jit(solution)/shard_map/all_to_all | solution.py:17
  23.7 5.8 %collective-permute-start.2 = (f32[64,1024]{1,0:T(8,128)S(1)}, f32[64,1024]{1,0:T(8,128)S(1)}, u32[]{:S(2)}, u32[]{:S(2)}) collective-permute-start(f32[64,1024]{1,0:T(8,128)S(1)} %get-tuple-element.26), channel_id=1, source_target_pairs={{0,128},{64,192},{128,0},{192,64},{256,384},{320,448},{384,256},{4... | collective-permute-start | bytes 786440 | tf_op jit(solution)/shard_map/ppermute | solution.py:278
  29.5 6.2 %collective-permute-start.3 = (f32[64,1024]{1,0:T(8,128)S(1)}, f32[64,1024]{1,0:T(8,128)S(1)}, u32[]{:S(2)}, u32[]{:S(2)}) collective-permute-start(f32[64,1024]{1,0:T(8,128)S(1)} %get-tuple-element.27), channel_id=1, source_target_pairs={{0,256},{64,320},{128,384},{192,448},{256,0},{320,64},{384,128},{4... | collective-permute-start | bytes 786440 | tf_op jit(solution)/shard_map/ppermute | solution.py:278
  35.7 2.2 %collective-permute-start.4 = (f32[64,1024]{1,0:T(8,128)S(1)}, f32[64,1024]{1,0:T(8,128)S(1)}, u32[]{:S(2)}, u32[]{:S(2)}) collective-permute-start(f32[64,1024]{1,0:T(8,128)S(1)} %get-tuple-element.28), channel_id=1, source_target_pairs={{0,384},{64,448},{128,256},{192,320},{256,128},{320,192},{384,0},{... | collective-permute-start | bytes 786440 | tf_op jit(solution)/shard_map/ppermute | solution.py:278
  37.9 0.0 collective-permute-done.2.one
  37.9 6.4 %collective-permute-done.3.two = f32[64,1024]{1,0:T(8,128)S(1)} collective-permute-done((f32[64,1024]{1,0:T(8,128)S(1)}, f32[64,1024]{1,0:T(8,128)S(1)}, u32[]{:S(2)}, u32[]{:S(2)}) %collective-permute-start.3) | collective-permute-done | bytes 262176 | tf_op jit(solution)/shard_map/ppermute | solution.py:278
  44.3 6.3 %collective-permute-done.4.three = f32[64,1024]{1,0:T(8,128)S(1)} collective-permute-done((f32[64,1024]{1,0:T(8,128)S(1)}, f32[64,1024]{1,0:T(8,128)S(1)}, u32[]{:S(2)}, u32[]{:S(2)}) %collective-permute-start.4) | collective-permute-done | bytes 262176 | tf_op jit(solution)/shard_map/ppermute | solution.py:278
  50.6 0.0 all-to-all-done.q_blocks
  50.6 0.5 product.1
  51.0 8.8 %all_to_all.25.p_parts = f32[8,32,128]{2,1,0:T(8,128)S(1)} all-to-all(f32[8,32,128]{2,1,0:T(8,128)S(1)} %get-tuple-element.30), channel_id=1, replica_groups=mesh['replica'=8,'mp'=64] {'replica'}, dimensions={0} | all-to-all | bytes 262144 | tf_op jit(solution)/shard_map/all_to_all | solution.py:17
  59.8 0.6 pack.1
  60.4 26.0 %all_to_all.26 = f32[64,9,1,128]{3,2,1,0:T(1,128)S(1)} all-to-all(f32[64,9,1,128]{3,2,1,0:T(1,128)S(1)} %bitcast.31), channel_id=1, replica_groups=mesh['replica'=8,'mp'=64] {'mp'}, dimensions={0} | all-to-all | bytes 589824 | tf_op jit(solution)/shard_map/all_to_all | solution.py:17
  86.4 0.1 total.1
  86.5 18.4 %all_to_all.27 = f32[64,9,1,128]{3,2,1,0:T(1,128)S(1)} all-to-all(f32[64,9,1,128]{3,2,1,0:T(1,128)S(1)} %bitcast.30), channel_id=1, replica_groups=mesh['replica'=8,'mp'=64] {'mp'}, dimensions={0} | all-to-all | bytes 589824 | tf_op jit(solution)/shard_map/all_to_all | solution.py:17
  104.9 0.1 unpack.1
  105.0 0.0 copy-start.4
  105.0 1.0 copy-done.4
  105.9 0.0 copy-start.1
  105.9 3.6 %all-to-all-start.4 = ((f32[4,8,64,128]{3,2,1,0:T(8,128)}), f32[4,8,64,128]{3,2,1,0:T(8,128)S(1)}, u32[]{:S(2)}, u32[]{:S(2)}) async-start(f32[4,8,64,128]{3,2,1,0:T(8,128)} %copy-done.4), calls=%async_computation.4 | async-start | bytes 2097152 | tf_op jit(solution)/shard_map/all_to_all | solution.py:17
  109.6 0.1 copy.10
  109.7 5.8 %cholesky.17 = f32[64,64]{1,0:T(8,128)S(1)} custom-call(f32[64,64]{1,0:T(8,128)S(1)} %fusion.7), custom_call_target="Cholesky" | custom-call | tf_op jit(solution)/shard_map/jit(cholesky)/cholesky | solution.py:291
  115.6 0.6 compare_reduce_fusion
  116.2 0.7 fusion.4
  116.9 4.9 %custom-call.6 = f32[1,64,64]{1,2,0:T(8,128)S(1)} custom-call(f32[1,64,64]{2,1,0:T(8,128)S(1)} %fusion.4), custom_call_target="InvertDiagBlocksLowerTriangular" | custom-call | tf_op jit(solution)/shard_map/triangular_solve | solution.py:292
  121.8 0.2 fusion.5.inverse
  122.0 0.8 factors.1
  122.8 0.0 all-to-all-done.4.mine
  122.8 5.7 %collective-permute-start.5 = (f32[4,8,64,128]{3,2,1,0:T(8,128)S(1)}, f32[4,8,64,128]{3,2,1,0:T(8,128)}, u32[]{:S(2)}, u32[]{:S(2)}) collective-permute-start(f32[4,8,64,128]{3,2,1,0:T(8,128)S(1)} %all-to-all-done.4.mine), channel_id=1, source_target_pairs={{0,64},{64,0},{128,192},{192,128},{256,320},{320,256},{384,448},{4... | collective-permute-start | bytes 3145736 | tf_op jit(solution)/shard_map/ppermute | solution.py:21
  128.6 0.1 pad_add_fusion.place
  128.7 0.0 copy-done.1
  128.7 0.0 copy-done.3
  128.7 1.1 update_near.1.near
  129.7 1.2 collective-permute-done.5.theirs
  130.9 3.2 %update_far.1 = (bf16[1,64,8192]{2,1,0:T(8,128)(2,1)}, f32[64,128]{1,0:T(8,128)}) custom-call(s32[4]{0:T(128)S(1)} %pad_add_fusion.place, f32[64,128]{1,0:T(8,128)S(1)} %get-tuple-element.37.weights, f32[64,64]{1,0:T(8,128)S(1)} %fusion.5.inverse, f32[4,8,64,128]{3,2,1,0:T(8,128)S(1)} %all-to-all-done.4.mine, ...), custom_call_target="tpu_custom_call" | custom-call | flops 134217728 | bytes 3145728 | tf_op jit(solution)/shard_map/update_far/pallas_call | solution.py:239
  (3 shorter events, 0.0 us)
Async XLA Ops:
  0.7 1.2 copy-start
  2.0 1.2 copy-start.2
  3.2 9.9 %copy-start.5 = (f32[128,64]{0,1:T(8,128)S(1)}, f32[128,64]{0,1:T(8,128)}, u32[]{:S(2)}) copy-start(f32[128,64]{0,1:T(8,128)} %param.5) | copy-start | bytes 98308
  4.3 11.1 %collective-permute-start = (f32[4,64,1024]{2,1,0:T(8,128)S(1)}, f32[4,64,1024]{2,1,0:T(8,128)S(1)}, u32[]{:S(2)}, u32[]{:S(2)}) collective-permute-start(f32[4,64,1024]{2,1,0:T(8,128)S(1)} %get-tuple-element.24), channel_id=1, source_target_pairs={{0,64},{64,0},{128,192},{192,128},{256,320},{320,256},{384,448},{4... | collective-permute-start | bytes 3145736 | tf_op jit(solution)/shard_map/ppermute | solution.py:21
  13.1 5.2 %collective-permute-start.1 = (f32[64,128]{1,0:T(8,128)S(1)}, f32[64,128]{1,0:T(8,128)S(1)}, u32[]{:S(2)}, u32[]{:S(2)}) collective-permute-start(f32[64,128]{1,0:T(8,128)S(1)} %bitcast.32), channel_id=1, source_target_pairs={{0,0},{1,64},{2,128},{3,192},{4,256},{5,320},{6,384},{7,448},{8,8}... | collective-permute-start | bytes 98312 | tf_op jit(solution)/shard_map/ppermute | solution.py:268
  19.0 31.5 %all-to-all-start = ((f32[8,64,128]{2,1,0:T(8,128)}), f32[8,64,128]{2,1,0:T(8,128)S(1)}, u32[]{:S(2)}, u32[]{:S(2)}) async-start(f32[8,64,128]{2,1,0:T(8,128)} %broadcast_in_dim.3), calls=%async_computation | async-start | bytes 524288 | tf_op jit(solution)/shard_map/all_to_all | solution.py:17
  23.7 14.2 %collective-permute-start.2 = (f32[64,1024]{1,0:T(8,128)S(1)}, f32[64,1024]{1,0:T(8,128)S(1)}, u32[]{:S(2)}, u32[]{:S(2)}) collective-permute-start(f32[64,1024]{1,0:T(8,128)S(1)} %get-tuple-element.26), channel_id=1, source_target_pairs={{0,128},{64,192},{128,0},{192,64},{256,384},{320,448},{384,256},{4... | collective-permute-start | bytes 786440 | tf_op jit(solution)/shard_map/ppermute | solution.py:278
  29.5 14.7 %collective-permute-start.3 = (f32[64,1024]{1,0:T(8,128)S(1)}, f32[64,1024]{1,0:T(8,128)S(1)}, u32[]{:S(2)}, u32[]{:S(2)}) collective-permute-start(f32[64,1024]{1,0:T(8,128)S(1)} %get-tuple-element.27), channel_id=1, source_target_pairs={{0,256},{64,320},{128,384},{192,448},{256,0},{320,64},{384,128},{4... | collective-permute-start | bytes 786440 | tf_op jit(solution)/shard_map/ppermute | solution.py:278
  35.7 14.9 %collective-permute-start.4 = (f32[64,1024]{1,0:T(8,128)S(1)}, f32[64,1024]{1,0:T(8,128)S(1)}, u32[]{:S(2)}, u32[]{:S(2)}) collective-permute-start(f32[64,1024]{1,0:T(8,128)S(1)} %get-tuple-element.28), channel_id=1, source_target_pairs={{0,384},{64,448},{128,256},{192,320},{256,128},{320,192},{384,0},{... | collective-permute-start | bytes 786440 | tf_op jit(solution)/shard_map/ppermute | solution.py:278
  105.0 1.0 copy-start.4
  105.9 22.7 %copy-start.1 = (bf16[1,64,8192]{2,1,0:T(8,128)(2,1)S(1)}, bf16[1,64,8192]{2,1,0:T(8,128)(2,1)}, u32[]{:S(2)}) copy-start(bf16[1,64,8192]{2,1,0:T(8,128)(2,1)} %gradient.5) | copy-start | bytes 3145732
  105.9 22.7 %copy-start.3 = (bf16[1,64,8192]{2,1,0:T(8,128)(2,1)S(1)}, bf16[1,64,8192]{2,1,0:T(8,128)(2,1)}, u32[]{:S(2)}) copy-start(bf16[1,64,8192]{2,1,0:T(8,128)(2,1)} %error.5) | copy-start | bytes 3145732
  105.9 16.9 %all-to-all-start.4 = ((f32[4,8,64,128]{3,2,1,0:T(8,128)}), f32[4,8,64,128]{3,2,1,0:T(8,128)S(1)}, u32[]{:S(2)}, u32[]{:S(2)}) async-start(f32[4,8,64,128]{3,2,1,0:T(8,128)} %copy-done.4), calls=%async_computation.4 | async-start | bytes 2097152 | tf_op jit(solution)/shard_map/all_to_all | solution.py:17
  122.8 8.1 %collective-permute-start.5 = (f32[4,8,64,128]{3,2,1,0:T(8,128)S(1)}, f32[4,8,64,128]{3,2,1,0:T(8,128)}, u32[]{:S(2)}, u32[]{:S(2)}) collective-permute-start(f32[4,8,64,128]{3,2,1,0:T(8,128)S(1)} %all-to-all-done.4.mine), channel_id=1, source_target_pairs={{0,64},{64,0},{128,192},{192,128},{256,320},{320,256},{384,448},{4... | collective-permute-start | bytes 3145736 | tf_op jit(solution)/shard_map/ppermute | solution.py:21

commit v6 on v4

--- a/solution.py
+++ b/solution.py
@@ -53,11 +53,15 @@
 
 
 def product_kernel(outer_ref, parts, *refs):
-    *blocks, mean, copies, q_list = refs
+    *pairs, mean, copies, q_list = refs
     mean[...] = (parts[0] + parts[1] + parts[2] + parts[3]) * (1.0 / copies.shape[0])
-    for apart, block in enumerate(blocks):
-        q_list[apart] = block[...]
-    q_own = jnp.concatenate([q_list[outer_ref[0] ^ a] for a in range(len(blocks))], axis=1)
+    for i, pair in enumerate(pairs):
+        q_list[2 * i:2 * (i + 1)] = pair[...]
+    blocks = []
+    for a in range(q_list.shape[0]):
+        apart = outer_ref[0] ^ a
+        blocks.append(q_list[((apart & 3) << 1) | (apart >> 2)])
+    q_own = jnp.concatenate(blocks, axis=1)
     p = lax.dot_general(mean[...], q_own, (((1,), (1,)), ((), ())), precision=HIGHEST,
                         preferred_element_type=jnp.float32)
     half = p.shape[0] // 2
@@ -66,19 +70,19 @@
         copies[r] = folded
 
 
-def product(outer, parts, blocks, replicas):
+def product(outer, parts, pairs, replicas):
     _, rows, own = parts.shape
-    rank = blocks[0].shape[0]
+    rank = pairs[0].shape[1]
     return pl.pallas_call(
         product_kernel,
-        in_specs=[SCALARS, VECTORS] + [VECTORS] * len(blocks),
+        in_specs=[SCALARS, VECTORS] + [VECTORS] * len(pairs),
         out_shape=[jax.ShapeDtypeStruct((rows, own), jnp.float32),
                    jax.ShapeDtypeStruct((replicas, rows // 2, 2 * rank), jnp.float32)],
-        scratch_shapes=[pltpu.VMEM((len(blocks), rank, BLOCK), jnp.float32)],
+        scratch_shapes=[pltpu.VMEM((2 * len(pairs), rank, BLOCK), jnp.float32)],
         cost_estimate=pl.CostEstimate(flops=2 * rows * own * rank, bytes_accessed=4 * parts.size, transcendentals=0),
         compiler_params=PARAMS,
         name="product",
-    )(outer, parts, *blocks)
+    )(outer, parts, *pairs)
 
 
 def pack_kernel(p_parts, mean, p_mean, tiles):
@@ -267,15 +271,20 @@
     outer, inner = shard // replicas, shard % replicas
     chip_groups = [[c + CORES * x for x in range(replicas // CORES)] for c in range(CORES)]
 
+    q_block = lax.ppermute(q_prev.T[None], ("replica", "mp"), [
+        (r * shards + o * replicas + i, i * shards + o * replicas + r)
+        for r in range(replicas) for o in range(groups) for i in range(replicas)
+    ])
+
     keep, give = split_moment(core.reshape(1), gradient, error, own)
-    paired, q_block = lax.optimization_barrier((keep + swap_cores(give, replicas), q_prev.T))
+    paired, q_block = lax.optimization_barrier((keep + swap_cores(give, replicas), q_block))
     parts = exchange(paired, "replica", chip_groups)
 
-    def along(apart):
-        return [(r * shards + o * replicas + i, i * shards + (o ^ apart) * replicas + r)
-                for r in range(replicas) for o in range(groups) for i in range(replicas)]
-    blocks = [lax.ppermute(q_block, ("replica", "mp"), along(apart)) for apart in range(groups)]
-    mean, copies = product(outer.reshape(1), parts, blocks, replicas)
+    def along(value, apart):
+        return lax.ppermute(value, "mp", [(j, j ^ (apart * replicas)) for j in range(shards)])
+    pair = jnp.concatenate([q_block, along(q_block, 4)], axis=0)
+    pairs = [pair] + [along(pair, apart) for apart in (1, 2, 3)]
+    mean, copies = product(outer.reshape(1), parts, pairs, replicas)
 
     p_mean, tiles = pack(exchange(copies, "replica"), mean, shards)
     packed = (shards, PACK, 1, BLOCK)

time: 166 us -> 135 us (0.81)
  blocking collectives: 79.7 us -> 57.9 us
  starting transfers between devices: 55.2 us -> 44 us
  waiting for transfers between devices: 5.02 us -> 7.46 us
    all_to_all x3, blocking collectives: 79.7 us -> 57.9 us  [exchange(): return lax.all_to_all(value, axis, 0, 0, axis_index_groups=groups)]
    ppermute x8 -> x5, starting transfers between devices: 33.4 us -> 21.8 us  [the longest x4 19.9 us: along(): lax.ppermute(value, 'mp', [(j, j ^ apart * replicas) for j in range(shard...]
    ppermute x8 -> x5, waiting for transfers between devices: 1.54 us -> 5.93 us  [the longest x4 4.11 us: along(): lax.ppermute(value, 'mp', [(j, j ^ apart * replicas) for j in range(shard...]
    ppermute x2, waiting for transfers between devices: 3.47 us -> 1.53 us  [swap_cores(): return lax.ppermute(value, 'replica', [(r, r ^ 1) for r in range(replicas)])]
    unnamed x12 -> x13, local copies, waits for them, and re-layouts: 3.42 us -> 3.42 us
  transfers between devices with their start and end apart: 12 -> 9, of which waited for: 3 -> 6; matrix products, arithmetic and copies ran while one was open for 8% -> 10% of each run, Pallas kernels for 1% -> 1%
where the time goes in v6:
time: 135 us; the launch traced here: 134 us
  blocking collectives  57.9 us (43%)
  starting transfers between devices  44 us (33%)
  other arithmetic  13.3 us (10%)
  waiting for transfers between devices  7.46 us (6%)
  Pallas kernels  6.86 us (5%)
  local copies, waits for them, and re-layouts  3.5 us (3%)
    all_to_all x3, blocking collectives, exchange(): return lax.all_to_all(value, axis, 0, 0, axis_index_groups=groups)  57.9 us
    ppermute x4, starting transfers between devices, along(): lax.ppermute(value, 'mp', [(j, j ^ apart * replicas) for j in range(shard...  19.9 us
    ppermute x2, starting transfers between devices, swap_cores(): return lax.ppermute(value, 'replica', [(r, r ^ 1) for r in range(replicas)])  14.5 us
    all_to_all x2, starting transfers between devices, exchange(): return lax.all_to_all(value, axis, 0, 0, axis_index_groups=groups)  7.7 us
    another operation x3, other arithmetic, body(): lower = jnp.linalg.cholesky(gram)  6.52 us
    another operation x2, other arithmetic, body(): lax.linalg.triangular_solve(lower, jnp.eye(rank, dtype=jnp.float32), left...  5.55 us
    ppermute x4, waiting for transfers between devices, along(): lax.ppermute(value, 'mp', [(j, j ^ apart * replicas) for j in range(shard...  4.11 us
    unnamed x13, local copies, waits for them, and re-layouts  3.42 us
  transfers between devices with their start and end apart: 9, of which 6 were waited for; matrix products, arithmetic and copies ran while one was open for 10% of the time, Pallas kernels for 1%

profile of v6, /device:TPU:1, one launch (start us, length us, event | category | flops | bytes accessed | tf_op | source)
XLA Modules:
  0.0 134.1 jit_solution(7596638099477791731)
XLA Ops:
  0.6 0.0 copy-start
  0.7 1.2 copy-done
  1.9 0.0 copy-start.2
  1.9 1.2 copy-done.2
  3.1 0.0 copy-start.5
  3.1 0.5 split_moment.1
  3.6 8.8 %collective-permute-start = (f32[4,64,1024]{2,1,0:T(8,128)S(1)}, f32[4,64,1024]{2,1,0:T(8,128)S(1)}, u32[]{:S(2)}, u32[]{:S(2)}) collective-permute-start(f32[4,64,1024]{2,1,0:T(8,128)S(1)} %get-tuple-element.21), channel_id=1, source_target_pairs={{0,64},{64,0},{128,192},{192,128},{256,320},{320,256},{384,448},{4... | collective-permute-start | bytes 3145736 | tf_op jit(solution)/shard_map/ppermute | solution.py:21
  12.4 0.0 copy-done.5
  12.4 1.9 %collective-permute-start.1 = (f32[1,64,128]{2,1,0:T(8,128)S(1)}, f32[1,64,128]{2,1,0:T(8,128)S(1)}, u32[]{:S(2)}, u32[]{:S(2)}) collective-permute-start(f32[1,64,128]{2,1,0:T(8,128)S(1)} %bitcast.25), channel_id=1, source_target_pairs={{0,0},{1,64},{2,128},{3,192},{4,256},{5,320},{6,384},{7,448},{8,8}... | collective-permute-start | bytes 98312 | tf_op jit(solution)/shard_map/ppermute | solution.py:274
  14.4 0.3 collective-permute-done
  14.7 1.2 add.29
  15.9 1.8 %collective-permute-done.1 = f32[1,64,128]{2,1,0:T(8,128)S(1)} collective-permute-done((f32[1,64,128]{2,1,0:T(8,128)S(1)}, f32[1,64,128]{2,1,0:T(8,128)S(1)}, u32[]{:S(2)}, u32[]{:S(2)}) %collective-permute-start.1) | collective-permute-done | bytes 32800 | tf_op jit(solution)/shard_map/ppermute | solution.py:274
  17.7 4.1 %all-to-all-start = ((f32[4,64,1024]{2,1,0:T(8,128)}), f32[4,64,1024]{2,1,0:T(8,128)S(1)}, u32[]{:S(2)}, u32[]{:S(2)}) async-start(f32[4,64,1024]{2,1,0:T(8,128)} %add.29), calls=%async_computation | async-start | bytes 2097152 | tf_op jit(solution)/shard_map/all_to_all | solution.py:17
  21.7 10.6 %collective-permute-start.2 = (f32[1,64,128]{2,1,0:T(8,128)S(1)}, f32[1,64,128]{2,1,0:T(8,128)S(1)}, u32[]{:S(2)}, u32[]{:S(2)}) collective-permute-start(f32[1,64,128]{2,1,0:T(8,128)S(1)} %collective-permute-done.1), channel_id=1, source_target_pairs={{0,32},{1,33},{2,34},{3,35},{4,36},{5,37},{6,38},{7,39},{8,40},{9,... | collective-permute-start | bytes 98312 | tf_op jit(solution)/shard_map/ppermute | solution.py:284
  32.4 1.3 collective-permute-done.2
  33.7 4.9 %collective-permute-start.5 = (f32[2,64,128]{2,1,0:T(8,128)S(1)}, f32[2,64,128]{2,1,0:T(8,128)S(1)}, u32[]{:S(2)}, u32[]{:S(2)}) collective-permute-start(f32[2,64,128]{2,1,0:T(8,128)S(1)} %constant_dynamic-update-slice_fusion.refs_0_), channel_id=1, source_target_pairs={{0,24},{1,25},{2,26},{3,27},{4,28},{5,29},{6,30},{7,31},{8,16},{9,... | collective-permute-start | bytes 196616 | tf_op jit(solution)/shard_map/ppermute | solution.py:284
  38.6 1.9 %collective-permute-start.4 = (f32[2,64,128]{2,1,0:T(8,128)S(1)}, f32[2,64,128]{2,1,0:T(8,128)S(1)}, u32[]{:S(2)}, u32[]{:S(2)}) collective-permute-start(f32[2,64,128]{2,1,0:T(8,128)S(1)} %constant_dynamic-update-slice_fusion.refs_0_), channel_id=1, source_target_pairs={{0,16},{1,17},{2,18},{3,19},{4,20},{5,21},{6,22},{7,23},{8,24},{9,... | collective-permute-start | bytes 196616 | tf_op jit(solution)/shard_map/ppermute | solution.py:284
  40.5 2.4 %collective-permute-start.3 = (f32[2,64,128]{2,1,0:T(8,128)S(1)}, f32[2,64,128]{2,1,0:T(8,128)S(1)}, u32[]{:S(2)}, u32[]{:S(2)}) collective-permute-start(f32[2,64,128]{2,1,0:T(8,128)S(1)} %constant_dynamic-update-slice_fusion.refs_0_), channel_id=1, source_target_pairs={{0,8},{1,9},{2,10},{3,11},{4,12},{5,13},{6,14},{7,15},{8,0},{9,1},... | collective-permute-start | bytes 196616 | tf_op jit(solution)/shard_map/ppermute | solution.py:284
  43.0 0.0 collective-permute-done.5.refs_3_
  43.0 2.1 %collective-permute-done.4.refs_2_ = f32[2,64,128]{2,1,0:T(8,128)S(1)} collective-permute-done((f32[2,64,128]{2,1,0:T(8,128)S(1)}, f32[2,64,128]{2,1,0:T(8,128)S(1)}, u32[]{:S(2)}, u32[]{:S(2)}) %collective-permute-start.4) | collective-permute-done | bytes 65568 | tf_op jit(solution)/shard_map/ppermute | solution.py:284
  45.1 0.7 collective-permute-done.3.refs_1_
  45.8 0.0 all-to-all-done.parts
  45.8 0.5 product.1
  46.3 13.7 %all_to_all.25.p_parts = f32[8,32,128]{2,1,0:T(8,128)S(1)} all-to-all(f32[8,32,128]{2,1,0:T(8,128)S(1)} %get-tuple-element.24), channel_id=1, replica_groups=mesh['replica'=8,'mp'=64] {'replica'}, dimensions={0} | all-to-all | bytes 262144 | tf_op jit(solution)/shard_map/all_to_all | solution.py:17
  60.0 0.6 pack.1
  60.6 25.8 %all_to_all.26 = f32[64,9,1,128]{3,2,1,0:T(1,128)S(1)} all-to-all(f32[64,9,1,128]{3,2,1,0:T(1,128)S(1)} %bitcast.24), channel_id=1, replica_groups=mesh['replica'=8,'mp'=64] {'mp'}, dimensions={0} | all-to-all | bytes 589824 | tf_op jit(solution)/shard_map/all_to_all | solution.py:17
  86.4 0.1 total.1
  86.5 18.4 %all_to_all.27 = f32[64,9,1,128]{3,2,1,0:T(1,128)S(1)} all-to-all(f32[64,9,1,128]{3,2,1,0:T(1,128)S(1)} %bitcast.23), channel_id=1, replica_groups=mesh['replica'=8,'mp'=64] {'mp'}, dimensions={0} | all-to-all | bytes 589824 | tf_op jit(solution)/shard_map/all_to_all | solution.py:17
  104.8 0.1 unpack.1
  104.9 0.0 copy-start.4
  104.9 1.0 copy-done.4
  105.9 0.0 copy-start.1
  105.9 3.6 %all-to-all-start.4 = ((f32[4,8,64,128]{3,2,1,0:T(8,128)}), f32[4,8,64,128]{3,2,1,0:T(8,128)S(1)}, u32[]{:S(2)}, u32[]{:S(2)}) async-start(f32[4,8,64,128]{3,2,1,0:T(8,128)} %copy-done.4), calls=%async_computation.4 | async-start | bytes 2097152 | tf_op jit(solution)/shard_map/all_to_all | solution.py:17
  109.6 0.1 copy.10
  109.7 5.8 %cholesky.17 = f32[64,64]{1,0:T(8,128)S(1)} custom-call(f32[64,64]{1,0:T(8,128)S(1)} %fusion.3), custom_call_target="Cholesky" | custom-call | tf_op jit(solution)/shard_map/jit(cholesky)/cholesky | solution.py:296
  115.5 0.6 compare_reduce_fusion
  116.2 0.7 fusion
  116.8 4.9 %custom-call.6 = f32[1,64,64]{1,2,0:T(8,128)S(1)} custom-call(f32[1,64,64]{2,1,0:T(8,128)S(1)} %fusion), custom_call_target="InvertDiagBlocksLowerTriangular" | custom-call | tf_op jit(solution)/shard_map/triangular_solve | solution.py:297
  121.7 0.2 fusion.1.inverse
  122.0 0.8 factors.1
  122.8 0.0 all-to-all-done.4.mine
  122.8 5.7 %collective-permute-start.6 = (f32[4,8,64,128]{3,2,1,0:T(8,128)S(1)}, f32[4,8,64,128]{3,2,1,0:T(8,128)}, u32[]{:S(2)}, u32[]{:S(2)}) collective-permute-start(f32[4,8,64,128]{3,2,1,0:T(8,128)S(1)} %all-to-all-done.4.mine), channel_id=1, source_target_pairs={{0,64},{64,0},{128,192},{192,128},{256,320},{320,256},{384,448},{4... | collective-permute-start | bytes 3145736 | tf_op jit(solution)/shard_map/ppermute | solution.py:21
  128.6 0.1 pad_add_fusion.place
  128.6 0.0 copy-done.1
  128.6 0.0 copy-done.3
  128.6 1.1 update_near.1.near
  129.7 1.2 collective-permute-done.6.theirs
  130.9 3.2 %update_far.1 = (bf16[1,64,8192]{2,1,0:T(8,128)(2,1)}, f32[64,128]{1,0:T(8,128)}) custom-call(s32[4]{0:T(128)S(1)} %pad_add_fusion.place, f32[64,128]{1,0:T(8,128)S(1)} %get-tuple-element.31.weights, f32[64,64]{1,0:T(8,128)S(1)} %fusion.1.inverse, f32[4,8,64,128]{3,2,1,0:T(8,128)S(1)} %all-to-all-done.4.mine, ...), custom_call_target="tpu_custom_call" | custom-call | flops 134217728 | bytes 3145728 | tf_op jit(solution)/shard_map/update_far/pallas_call | solution.py:246
  (5 shorter events, 0.0 us)
Async XLA Ops:
  0.6 1.2 copy-start
  1.9 1.2 copy-start.2
  3.1 9.3 %copy-start.5 = (f32[128,64]{0,1:T(8,128)S(1)}, f32[128,64]{0,1:T(8,128)}, u32[]{:S(2)}) copy-start(f32[128,64]{0,1:T(8,128)} %param.5) | copy-start | bytes 98308
  3.6 11.1 %collective-permute-start = (f32[4,64,1024]{2,1,0:T(8,128)S(1)}, f32[4,64,1024]{2,1,0:T(8,128)S(1)}, u32[]{:S(2)}, u32[]{:S(2)}) collective-permute-start(f32[4,64,1024]{2,1,0:T(8,128)S(1)} %get-tuple-element.21), channel_id=1, source_target_pairs={{0,64},{64,0},{128,192},{192,128},{256,320},{320,256},{384,448},{4... | collective-permute-start | bytes 3145736 | tf_op jit(solution)/shard_map/ppermute | solution.py:21
  12.4 5.2 %collective-permute-start.1 = (f32[1,64,128]{2,1,0:T(8,128)S(1)}, f32[1,64,128]{2,1,0:T(8,128)S(1)}, u32[]{:S(2)}, u32[]{:S(2)}) collective-permute-start(f32[1,64,128]{2,1,0:T(8,128)S(1)} %bitcast.25), channel_id=1, source_target_pairs={{0,0},{1,64},{2,128},{3,192},{4,256},{5,320},{6,384},{7,448},{8,8}... | collective-permute-start | bytes 98312 | tf_op jit(solution)/shard_map/ppermute | solution.py:274
  17.7 28.1 %all-to-all-start = ((f32[4,64,1024]{2,1,0:T(8,128)}), f32[4,64,1024]{2,1,0:T(8,128)S(1)}, u32[]{:S(2)}, u32[]{:S(2)}) async-start(f32[4,64,1024]{2,1,0:T(8,128)} %add.29), calls=%async_computation | async-start | bytes 2097152 | tf_op jit(solution)/shard_map/all_to_all | solution.py:17
  21.7 12.0 %collective-permute-start.2 = (f32[1,64,128]{2,1,0:T(8,128)S(1)}, f32[1,64,128]{2,1,0:T(8,128)S(1)}, u32[]{:S(2)}, u32[]{:S(2)}) collective-permute-start(f32[1,64,128]{2,1,0:T(8,128)S(1)} %collective-permute-done.1), channel_id=1, source_target_pairs={{0,32},{1,33},{2,34},{3,35},{4,36},{5,37},{6,38},{7,39},{8,40},{9,... | collective-permute-start | bytes 98312 | tf_op jit(solution)/shard_map/ppermute | solution.py:284
  33.7 9.3 %collective-permute-start.5 = (f32[2,64,128]{2,1,0:T(8,128)S(1)}, f32[2,64,128]{2,1,0:T(8,128)S(1)}, u32[]{:S(2)}, u32[]{:S(2)}) collective-permute-start(f32[2,64,128]{2,1,0:T(8,128)S(1)} %constant_dynamic-update-slice_fusion.refs_0_), channel_id=1, source_target_pairs={{0,24},{1,25},{2,26},{3,27},{4,28},{5,29},{6,30},{7,31},{8,16},{9,... | collective-permute-start | bytes 196616 | tf_op jit(solution)/shard_map/ppermute | solution.py:284
  38.6 6.5 %collective-permute-start.4 = (f32[2,64,128]{2,1,0:T(8,128)S(1)}, f32[2,64,128]{2,1,0:T(8,128)S(1)}, u32[]{:S(2)}, u32[]{:S(2)}) collective-permute-start(f32[2,64,128]{2,1,0:T(8,128)S(1)} %constant_dynamic-update-slice_fusion.refs_0_), channel_id=1, source_target_pairs={{0,16},{1,17},{2,18},{3,19},{4,20},{5,21},{6,22},{7,23},{8,24},{9,... | collective-permute-start | bytes 196616 | tf_op jit(solution)/shard_map/ppermute | solution.py:284
  40.5 5.3 %collective-permute-start.3 = (f32[2,64,128]{2,1,0:T(8,128)S(1)}, f32[2,64,128]{2,1,0:T(8,128)S(1)}, u32[]{:S(2)}, u32[]{:S(2)}) collective-permute-start(f32[2,64,128]{2,1,0:T(8,128)S(1)} %constant_dynamic-update-slice_fusion.refs_0_), channel_id=1, source_target_pairs={{0,8},{1,9},{2,10},{3,11},{4,12},{5,13},{6,14},{7,15},{8,0},{9,1},... | collective-permute-start | bytes 196616 | tf_op jit(solution)/shard_map/ppermute | solution.py:284
  104.9 1.0 copy-start.4
  105.9 22.7 %copy-start.1 = (bf16[1,64,8192]{2,1,0:T(8,128)(2,1)S(1)}, bf16[1,64,8192]{2,1,0:T(8,128)(2,1)}, u32[]{:S(2)}) copy-start(bf16[1,64,8192]{2,1,0:T(8,128)(2,1)} %gradient.5) | copy-start | bytes 3145732
  105.9 22.7 %copy-start.3 = (bf16[1,64,8192]{2,1,0:T(8,128)(2,1)S(1)}, bf16[1,64,8192]{2,1,0:T(8,128)(2,1)}, u32[]{:S(2)}) copy-start(bf16[1,64,8192]{2,1,0:T(8,128)(2,1)} %error.5) | copy-start | bytes 3145732
  105.9 16.9 %all-to-all-start.4 = ((f32[4,8,64,128]{3,2,1,0:T(8,128)}), f32[4,8,64,128]{3,2,1,0:T(8,128)S(1)}, u32[]{:S(2)}, u32[]{:S(2)}) async-start(f32[4,8,64,128]{3,2,1,0:T(8,128)} %copy-done.4), calls=%async_computation.4 | async-start | bytes 2097152 | tf_op jit(solution)/shard_map/all_to_all | solution.py:17
  122.8 8.1 %collective-permute-start.6 = (f32[4,8,64,128]{3,2,1,0:T(8,128)S(1)}, f32[4,8,64,128]{3,2,1,0:T(8,128)}, u32[]{:S(2)}, u32[]{:S(2)}) collective-permute-start(f32[4,8,64,128]{3,2,1,0:T(8,128)S(1)} %all-to-all-done.4.mine), channel_id=1, source_target_pairs={{0,64},{64,0},{128,192},{192,128},{256,320},{320,256},{384,448},{4... | collective-permute-start | bytes 3145736 | tf_op jit(solution)/shard_map/ppermute | solution.py:21

commit v7 on v6

--- a/solution.py
+++ b/solution.py
@@ -277,12 +277,13 @@
     ])
 
     keep, give = split_moment(core.reshape(1), gradient, error, own)
-    paired, q_block = lax.optimization_barrier((keep + swap_cores(give, replicas), q_block))
-    parts = exchange(paired, "replica", chip_groups)
+    give, q_block = lax.optimization_barrier((give, q_block))
 
     def along(value, apart):
         return lax.ppermute(value, "mp", [(j, j ^ (apart * replicas)) for j in range(shards)])
     pair = jnp.concatenate([q_block, along(q_block, 4)], axis=0)
+    paired, pair = lax.optimization_barrier((keep + swap_cores(give, replicas), pair))
+    parts = exchange(paired, "replica", chip_groups)
     pairs = [pair] + [along(pair, apart) for apart in (1, 2, 3)]
     mean, copies = product(outer.reshape(1), parts, pairs, replicas)
 

time: 135 us -> 133 us (0.985)
  blocking collectives: 57.9 us -> 53.9 us
  starting transfers between devices: 44 us -> 46 us
    all_to_all x2, starting transfers between devices: 7.7 us -> 13.9 us  [exchange(): return lax.all_to_all(value, axis, 0, 0, axis_index_groups=groups)]
    all_to_all x3, blocking collectives: 57.9 us -> 53.9 us  [exchange(): return lax.all_to_all(value, axis, 0, 0, axis_index_groups=groups)]
    ppermute x4, starting transfers between devices: 19.9 us -> 16.2 us  [along(): lax.ppermute(value, 'mp', [(j, j ^ apart * replicas) for j in range(shard...]
    ppermute x2, starting transfers between devices: 14.5 us -> 11.3 us  [swap_cores(): return lax.ppermute(value, 'replica', [(r, r ^ 1) for r in range(replicas)])]
    ppermute x1, starting transfers between devices: 1.92 us -> 4.59 us  [body(): lax.ppermute(q_prev.T[None], ('replica', 'mp'), [(r * shards + o * replic...]
    ppermute x1, waiting for transfers between devices: 1.82 us -> 0.01 us  [body(): lax.ppermute(q_prev.T[None], ('replica', 'mp'), [(r * shards + o * replic...]
    all_to_all x2, waiting for transfers between devices: 0.01 us -> 1.68 us  [exchange(): return lax.all_to_all(value, axis, 0, 0, axis_index_groups=groups)]
    unnamed x13 -> x10, local copies, waits for them, and re-layouts: 3.42 us -> 3.42 us
  transfers between devices with their start and end apart: 9 -> 9, of which waited for: 6 -> 5; matrix products, arithmetic and copies ran while one was open for 10% -> 9% of each run, Pallas kernels for 1% -> 2%
where the time goes in v7:
time: 133 us; the launch traced here: 132 us
  blocking collectives  53.9 us (41%)
  starting transfers between devices  46 us (35%)
  other arithmetic  13.3 us (10%)
  waiting for transfers between devices  7.76 us (6%)
  Pallas kernels  6.85 us (5%)
  local copies, waits for them, and re-layouts  3.49 us (3%)
    all_to_all x3, blocking collectives, exchange(): return lax.all_to_all(value, axis, 0, 0, axis_index_groups=groups)  53.9 us
    ppermute x4, starting transfers between devices, along(): lax.ppermute(value, 'mp', [(j, j ^ apart * replicas) for j in range(shard...  16.2 us
    all_to_all x2, starting transfers between devices, exchange(): return lax.all_to_all(value, axis, 0, 0, axis_index_groups=groups)  13.9 us
    ppermute x2, starting transfers between devices, swap_cores(): return lax.ppermute(value, 'replica', [(r, r ^ 1) for r in range(replicas)])  11.3 us
    another operation x3, other arithmetic, body(): lower = jnp.linalg.cholesky(gram)  6.52 us
    another operation x2, other arithmetic, body(): lax.linalg.triangular_solve(lower, jnp.eye(rank, dtype=jnp.float32), left...  5.55 us
    ppermute x4, waiting for transfers between devices, along(): lax.ppermute(value, 'mp', [(j, j ^ apart * replicas) for j in range(shard...  4.87 us
    ppermute x1, starting transfers between devices, body(): lax.ppermute(q_prev.T[None], ('replica', 'mp'), [(r * shards + o * replic...  4.59 us
  transfers between devices with their start and end apart: 9, of which 5 were waited for; matrix products, arithmetic and copies ran while one was open for 9% of the time, Pallas kernels for 2%

profile of v7, /device:TPU:1, one launch (start us, length us, event | category | flops | bytes accessed | tf_op | source)
XLA Modules:
  0.0 132.5 jit_solution(5968162476254423608)
XLA Ops:
  0.6 4.6 %collective-permute-start = (f32[1,64,128]{2,1,0:T(8,128)}, f32[1,64,128]{2,1,0:T(8,128)S(1)}, u32[]{:S(2)}, u32[]{:S(2)}) collective-permute-start(f32[1,64,128]{2,1,0:T(8,128)} %bitcast.25), channel_id=1, source_target_pairs={{0,0},{1,64},{2,128},{3,192},{4,256},{5,320},{6,384},{7,448},{8,8}... | collective-permute-start | bytes 98312 | tf_op jit(solution)/shard_map/ppermute | solution.py:274
  5.2 0.0 copy-start
  5.3 1.2 copy-done
  6.5 0.0 copy-start.2
  6.5 1.2 copy-done.2
  7.7 0.5 split_moment.1
  8.2 0.0 collective-permute-done
  8.3 5.6 %collective-permute-start.1 = (f32[4,64,1024]{2,1,0:T(8,128)S(1)}, f32[4,64,1024]{2,1,0:T(8,128)S(1)}, u32[]{:S(2)}, u32[]{:S(2)}) collective-permute-start(f32[4,64,1024]{2,1,0:T(8,128)S(1)} %get-tuple-element.24), channel_id=1, source_target_pairs={{0,64},{64,0},{128,192},{192,128},{256,320},{320,256},{384,448},{4... | collective-permute-start | bytes 3145736 | tf_op jit(solution)/shard_map/ppermute | solution.py:21
  13.8 7.0 %collective-permute-start.2 = (f32[1,64,128]{2,1,0:T(8,128)S(1)}, f32[1,64,128]{2,1,0:T(8,128)S(1)}, u32[]{:S(2)}, u32[]{:S(2)}) collective-permute-start(f32[1,64,128]{2,1,0:T(8,128)S(1)} %collective-permute-done), channel_id=1, source_target_pairs={{0,32},{1,33},{2,34},{3,35},{4,36},{5,37},{6,38},{7,39},{8,40},{9,... | collective-permute-start | bytes 98312 | tf_op jit(solution)/shard_map/ppermute | solution.py:283
  20.8 1.7 %collective-permute-done.2 = f32[1,64,128]{2,1,0:T(8,128)S(1)} collective-permute-done((f32[1,64,128]{2,1,0:T(8,128)S(1)}, f32[1,64,128]{2,1,0:T(8,128)S(1)}, u32[]{:S(2)}, u32[]{:S(2)}) %collective-permute-start.2) | collective-permute-done | bytes 32800 | tf_op jit(solution)/shard_map/ppermute | solution.py:283
  22.5 0.0 collective-permute-done.1
  22.5 1.2 add.29
  23.7 10.3 %all-to-all-start = ((f32[4,64,1024]{2,1,0:T(8,128)}), f32[4,64,1024]{2,1,0:T(8,128)S(1)}, u32[]{:S(2)}, u32[]{:S(2)}) async-start(f32[4,64,1024]{2,1,0:T(8,128)} %add.29), calls=%async_computation | async-start | bytes 2097152 | tf_op jit(solution)/shard_map/all_to_all | solution.py:17
  33.9 4.9 %collective-permute-start.5 = (f32[2,64,128]{2,1,0:T(8,128)S(1)}, f32[2,64,128]{2,1,0:T(8,128)S(1)}, u32[]{:S(2)}, u32[]{:S(2)}) collective-permute-start(f32[2,64,128]{2,1,0:T(8,128)S(1)} %pad_maximum_fusion.refs_0_), channel_id=1, source_target_pairs={{0,24},{1,25},{2,26},{3,27},{4,28},{5,29},{6,30},{7,31},{8,16},{9,... | collective-permute-start | bytes 196616 | tf_op jit(solution)/shard_map/ppermute | solution.py:283
  38.8 1.9 %collective-permute-start.4 = (f32[2,64,128]{2,1,0:T(8,128)S(1)}, f32[2,64,128]{2,1,0:T(8,128)S(1)}, u32[]{:S(2)}, u32[]{:S(2)}) collective-permute-start(f32[2,64,128]{2,1,0:T(8,128)S(1)} %pad_maximum_fusion.refs_0_), channel_id=1, source_target_pairs={{0,16},{1,17},{2,18},{3,19},{4,20},{5,21},{6,22},{7,23},{8,24},{9,... | collective-permute-start | bytes 196616 | tf_op jit(solution)/shard_map/ppermute | solution.py:283
  40.8 2.4 %collective-permute-start.3 = (f32[2,64,128]{2,1,0:T(8,128)S(1)}, f32[2,64,128]{2,1,0:T(8,128)S(1)}, u32[]{:S(2)}, u32[]{:S(2)}) collective-permute-start(f32[2,64,128]{2,1,0:T(8,128)S(1)} %pad_maximum_fusion.refs_0_), channel_id=1, source_target_pairs={{0,8},{1,9},{2,10},{3,11},{4,12},{5,13},{6,14},{7,15},{8,0},{9,1},... | collective-permute-start | bytes 196616 | tf_op jit(solution)/shard_map/ppermute | solution.py:283
  43.2 0.0 collective-permute-done.5.refs_3_
  43.2 2.5 %collective-permute-done.4.refs_2_ = f32[2,64,128]{2,1,0:T(8,128)S(1)} collective-permute-done((f32[2,64,128]{2,1,0:T(8,128)S(1)}, f32[2,64,128]{2,1,0:T(8,128)S(1)}, u32[]{:S(2)}, u32[]{:S(2)}) %collective-permute-start.4) | collective-permute-done | bytes 65568 | tf_op jit(solution)/shard_map/ppermute | solution.py:283
  45.7 0.7 collective-permute-done.3.refs_1_
  46.5 1.7 %all-to-all-done.parts = f32[4,64,1024]{2,1,0:T(8,128)S(1)} async-done(((f32[4,64,1024]{2,1,0:T(8,128)}), f32[4,64,1024]{2,1,0:T(8,128)S(1)}, u32[]{:S(2)}, u32[]{:S(2)}) %all-to-all-start) | async-done | bytes 1048608 | tf_op jit(solution)/shard_map/all_to_all | solution.py:17
  48.1 0.5 product.1
  48.6 10.1 %all_to_all.25.p_parts = f32[8,32,128]{2,1,0:T(8,128)S(1)} all-to-all(f32[8,32,128]{2,1,0:T(8,128)S(1)} %get-tuple-element.28), channel_id=1, replica_groups=mesh['replica'=8,'mp'=64] {'replica'}, dimensions={0} | all-to-all | bytes 262144 | tf_op jit(solution)/shard_map/all_to_all | solution.py:17
  58.7 0.6 pack.1
  59.3 25.5 %all_to_all.26 = f32[64,9,1,128]{3,2,1,0:T(1,128)S(1)} all-to-all(f32[64,9,1,128]{3,2,1,0:T(1,128)S(1)} %bitcast.24), channel_id=1, replica_groups=mesh['replica'=8,'mp'=64] {'mp'}, dimensions={0} | all-to-all | bytes 589824 | tf_op jit(solution)/shard_map/all_to_all | solution.py:17
  84.8 0.1 total.1
  84.8 18.4 %all_to_all.27 = f32[64,9,1,128]{3,2,1,0:T(1,128)S(1)} all-to-all(f32[64,9,1,128]{3,2,1,0:T(1,128)S(1)} %bitcast.23), channel_id=1, replica_groups=mesh['replica'=8,'mp'=64] {'mp'}, dimensions={0} | all-to-all | bytes 589824 | tf_op jit(solution)/shard_map/all_to_all | solution.py:17
  103.2 0.1 unpack.1
  103.3 0.0 copy-start.4
  103.3 1.0 copy-done.4
  104.3 0.0 copy-start.1
  104.3 0.0 copy-start.3
  104.3 3.6 %all-to-all-start.4 = ((f32[4,8,64,128]{3,2,1,0:T(8,128)}), f32[4,8,64,128]{3,2,1,0:T(8,128)S(1)}, u32[]{:S(2)}, u32[]{:S(2)}) async-start(f32[4,8,64,128]{3,2,1,0:T(8,128)} %copy-done.4), calls=%async_computation.4 | async-start | bytes 2097152 | tf_op jit(solution)/shard_map/all_to_all | solution.py:17
  107.9 0.1 copy.10
  108.0 5.8 %cholesky.17 = f32[64,64]{1,0:T(8,128)S(1)} custom-call(f32[64,64]{1,0:T(8,128)S(1)} %fusion.3), custom_call_target="Cholesky" | custom-call | tf_op jit(solution)/shard_map/jit(cholesky)/cholesky | solution.py:297
  113.9 0.6 compare_reduce_fusion
  114.5 0.7 fusion
  115.2 4.9 %custom-call.6 = f32[1,64,64]{1,2,0:T(8,128)S(1)} custom-call(f32[1,64,64]{2,1,0:T(8,128)S(1)} %fusion), custom_call_target="InvertDiagBlocksLowerTriangular" | custom-call | tf_op jit(solution)/shard_map/triangular_solve | solution.py:298
  120.1 0.2 fusion.1.inverse
  120.3 0.8 factors.1
  121.2 0.0 all-to-all-done.4.mine
  121.2 5.7 %collective-permute-start.6 = (f32[4,8,64,128]{3,2,1,0:T(8,128)S(1)}, f32[4,8,64,128]{3,2,1,0:T(8,128)}, u32[]{:S(2)}, u32[]{:S(2)}) collective-permute-start(f32[4,8,64,128]{3,2,1,0:T(8,128)S(1)} %all-to-all-done.4.mine), channel_id=1, source_target_pairs={{0,64},{64,0},{128,192},{192,128},{256,320},{320,256},{384,448},{4... | collective-permute-start | bytes 3145736 | tf_op jit(solution)/shard_map/ppermute | solution.py:21
  126.9 0.1 pad_add_fusion.place
  127.0 0.0 copy-done.1
  127.0 0.0 copy-done.3
  127.0 1.1 update_near.1.near
  128.1 1.2 collective-permute-done.6.theirs
  129.3 3.2 %update_far.1 = (bf16[1,64,8192]{2,1,0:T(8,128)(2,1)}, f32[64,128]{1,0:T(8,128)}) custom-call(s32[4]{0:T(128)S(1)} %pad_add_fusion.place, f32[64,128]{1,0:T(8,128)S(1)} %get-tuple-element.35.weights, f32[64,64]{1,0:T(8,128)S(1)} %fusion.1.inverse, f32[4,8,64,128]{3,2,1,0:T(8,128)S(1)} %all-to-all-done.4.mine, ...), custom_call_target="tpu_custom_call" | custom-call | flops 134217728 | bytes 3145728 | tf_op jit(solution)/shard_map/update_far/pallas_call | solution.py:246
  (3 shorter events, 0.0 us)
Async XLA Ops:
  0.6 7.6 %collective-permute-start = (f32[1,64,128]{2,1,0:T(8,128)}, f32[1,64,128]{2,1,0:T(8,128)S(1)}, u32[]{:S(2)}, u32[]{:S(2)}) collective-permute-start(f32[1,64,128]{2,1,0:T(8,128)} %bitcast.25), channel_id=1, source_target_pairs={{0,0},{1,64},{2,128},{3,192},{4,256},{5,320},{6,384},{7,448},{8,8}... | collective-permute-start | bytes 98312 | tf_op jit(solution)/shard_map/ppermute | solution.py:274
  5.2 1.2 copy-start
  6.5 1.2 copy-start.2
  8.3 14.2 %collective-permute-start.1 = (f32[4,64,1024]{2,1,0:T(8,128)S(1)}, f32[4,64,1024]{2,1,0:T(8,128)S(1)}, u32[]{:S(2)}, u32[]{:S(2)}) collective-permute-start(f32[4,64,1024]{2,1,0:T(8,128)S(1)} %get-tuple-element.24), channel_id=1, source_target_pairs={{0,64},{64,0},{128,192},{192,128},{256,320},{320,256},{384,448},{4... | collective-permute-start | bytes 3145736 | tf_op jit(solution)/shard_map/ppermute | solution.py:21
  13.8 8.6 %collective-permute-start.2 = (f32[1,64,128]{2,1,0:T(8,128)S(1)}, f32[1,64,128]{2,1,0:T(8,128)S(1)}, u32[]{:S(2)}, u32[]{:S(2)}) collective-permute-start(f32[1,64,128]{2,1,0:T(8,128)S(1)} %collective-permute-done), channel_id=1, source_target_pairs={{0,32},{1,33},{2,34},{3,35},{4,36},{5,37},{6,38},{7,39},{8,40},{9,... | collective-permute-start | bytes 98312 | tf_op jit(solution)/shard_map/ppermute | solution.py:283
  23.7 24.5 %all-to-all-start = ((f32[4,64,1024]{2,1,0:T(8,128)}), f32[4,64,1024]{2,1,0:T(8,128)S(1)}, u32[]{:S(2)}, u32[]{:S(2)}) async-start(f32[4,64,1024]{2,1,0:T(8,128)} %add.29), calls=%async_computation | async-start | bytes 2097152 | tf_op jit(solution)/shard_map/all_to_all | solution.py:17
  33.9 9.3 %collective-permute-start.5 = (f32[2,64,128]{2,1,0:T(8,128)S(1)}, f32[2,64,128]{2,1,0:T(8,128)S(1)}, u32[]{:S(2)}, u32[]{:S(2)}) collective-permute-start(f32[2,64,128]{2,1,0:T(8,128)S(1)} %pad_maximum_fusion.refs_0_), channel_id=1, source_target_pairs={{0,24},{1,25},{2,26},{3,27},{4,28},{5,29},{6,30},{7,31},{8,16},{9,... | collective-permute-start | bytes 196616 | tf_op jit(solution)/shard_map/ppermute | solution.py:283
  38.8 6.9 %collective-permute-start.4 = (f32[2,64,128]{2,1,0:T(8,128)S(1)}, f32[2,64,128]{2,1,0:T(8,128)S(1)}, u32[]{:S(2)}, u32[]{:S(2)}) collective-permute-start(f32[2,64,128]{2,1,0:T(8,128)S(1)} %pad_maximum_fusion.refs_0_), channel_id=1, source_target_pairs={{0,16},{1,17},{2,18},{3,19},{4,20},{5,21},{6,22},{7,23},{8,24},{9,... | collective-permute-start | bytes 196616 | tf_op jit(solution)/shard_map/ppermute | solution.py:283
  40.8 5.7 %collective-permute-start.3 = (f32[2,64,128]{2,1,0:T(8,128)S(1)}, f32[2,64,128]{2,1,0:T(8,128)S(1)}, u32[]{:S(2)}, u32[]{:S(2)}) collective-permute-start(f32[2,64,128]{2,1,0:T(8,128)S(1)} %pad_maximum_fusion.refs_0_), channel_id=1, source_target_pairs={{0,8},{1,9},{2,10},{3,11},{4,12},{5,13},{6,14},{7,15},{8,0},{9,1},... | collective-permute-start | bytes 196616 | tf_op jit(solution)/shard_map/ppermute | solution.py:283
  103.3 1.0 copy-start.4
  104.3 22.7 %copy-start.1 = (bf16[1,64,8192]{2,1,0:T(8,128)(2,1)S(1)}, bf16[1,64,8192]{2,1,0:T(8,128)(2,1)}, u32[]{:S(2)}) copy-start(bf16[1,64,8192]{2,1,0:T(8,128)(2,1)} %gradient.5) | copy-start | bytes 3145732
  104.3 22.7 %copy-start.3 = (bf16[1,64,8192]{2,1,0:T(8,128)(2,1)S(1)}, bf16[1,64,8192]{2,1,0:T(8,128)(2,1)}, u32[]{:S(2)}) copy-start(bf16[1,64,8192]{2,1,0:T(8,128)(2,1)} %error.5) | copy-start | bytes 3145732
  104.3 16.9 %all-to-all-start.4 = ((f32[4,8,64,128]{3,2,1,0:T(8,128)}), f32[4,8,64,128]{3,2,1,0:T(8,128)S(1)}, u32[]{:S(2)}, u32[]{:S(2)}) async-start(f32[4,8,64,128]{3,2,1,0:T(8,128)} %copy-done.4), calls=%async_computation.4 | async-start | bytes 2097152 | tf_op jit(solution)/shard_map/all_to_all | solution.py:17
  121.2 8.1 %collective-permute-start.6 = (f32[4,8,64,128]{3,2,1,0:T(8,128)S(1)}, f32[4,8,64,128]{3,2,1,0:T(8,128)}, u32[]{:S(2)}, u32[]{:S(2)}) collective-permute-start(f32[4,8,64,128]{3,2,1,0:T(8,128)S(1)} %all-to-all-done.4.mine), channel_id=1, source_target_pairs={{0,64},{64,0},{128,192},{192,128},{256,320},{320,256},{384,448},{4... | collective-permute-start | bytes 3145736 | tf_op jit(solution)/shard_map/ppermute | solution.py:21

commit v8 on v7

--- a/solution.py
+++ b/solution.py
@@ -60,7 +60,7 @@
     blocks = []
     for a in range(q_list.shape[0]):
         apart = outer_ref[0] ^ a
-        blocks.append(q_list[((apart & 3) << 1) | (apart >> 2)])
+        blocks.append(q_list[apart])
     q_own = jnp.concatenate(blocks, axis=1)
     p = lax.dot_general(mean[...], q_own, (((1,), (1,)), ((), ())), precision=HIGHEST,
                         preferred_element_type=jnp.float32)
@@ -197,43 +197,54 @@
         for i in range(2)]
 
 
-def near_kernel(place, weights, mine, gradient, error, out):
-    chips, groups, _, _ = mine.shape
-    factor = halves(weights[...], 0)
-    for a in range(groups):
-        for x in range(0, chips, 2):
-            out[x, a], out[x + 1, a] = remainder(factor, mine, x, a, place[0], gradient, error)
-
-
-def update_near(place, weights, mine, gradient, error):
-    _, rows, cols = gradient.shape
-    chips, groups, rank, _ = mine.shape
-    return pl.pallas_call(
-        near_kernel,
-        in_specs=[SCALARS] + [VECTORS] * 4,
-        out_shape=jax.ShapeDtypeStruct((chips, groups, rows, BLOCK), gradient.dtype),
-        cost_estimate=pl.CostEstimate(
-            flops=4 * rows * cols * rank, bytes_accessed=4 * rows * cols, transcendentals=0),
-        compiler_params=PARAMS,
-        name="update_near",
-    )(place, weights, mine, gradient, error)
-
-
-def far_kernel(place, weights, inverse, mine, theirs, near, gradient, error, out, right, bands, done):
-    chips, groups, _, _ = mine.shape
-    core, block, chip, parity = (place[i] for i in range(4))
-    factor = halves(weights[...], 0)
+def half_kernel(factor, s, core, gradient, error, out, blocks, done):
+    chips, groups, _, _ = s.shape
     copies = []
     for a in range(groups):
         for x in range(0, chips, 2):
-            far = remainder(factor, theirs, x, a, 1 - core, gradient, error)
-            for i in range(2):
-                for value, owner in ((near[x + i, a], core), (far[i], 1 - core)):
-                    start = pl.multiple_of((CORES * (x + i) + owner) * BLOCK, BLOCK)
-                    bands[a, :, pl.ds(start, BLOCK)] = value
-        width = bands.shape[2]
-        copies.append(pltpu.make_async_copy(bands.at[a], out.at[0, :, a * width:(a + 1) * width], done.at[a]))
-        copies[a].start()
+            blocks[a, x], blocks[a, x + 1] = remainder(factor, s, x, a, core, gradient, error)
+            for i in (x, x + 1):
+                start = pl.multiple_of((CORES * (a * chips + i) + core) * BLOCK, BLOCK)
+                copies.append(pltpu.make_async_copy(
+                    blocks.at[a, i], out.at[0, :, pl.ds(start, BLOCK)], done.at[a, i]))
+                copies[-1].start()
+    return copies
+
+
+def near_kernel(place, weights, mine, gradient, error, out, blocks, done):
+    factor = halves(weights[...], 0)
+    for copy in half_kernel(factor, mine, place[0], gradient, error, out, blocks, done):
+        copy.wait()
+
+
+def half_scratch(s, gradient):
+    chips, groups, _, _ = s.shape
+    return [pltpu.VMEM((groups, chips, gradient.shape[1], BLOCK), gradient.dtype),
+            pltpu.SemaphoreType.DMA((groups, chips))]
+
+
+def half_cost(s, gradient):
+    _, rows, cols = gradient.shape
+    return pl.CostEstimate(flops=4 * rows * cols * s.shape[2], bytes_accessed=4 * rows * cols, transcendentals=0)
+
+
+def update_near(place, weights, mine, gradient, error):
+    return pl.pallas_call(
+        near_kernel,
+        in_specs=[SCALARS] + [VECTORS] * 4,
+        out_specs=pl.BlockSpec(memory_space=pl.ANY),
+        out_shape=jax.ShapeDtypeStruct(gradient.shape, gradient.dtype),
+        scratch_shapes=half_scratch(mine, gradient),
+        cost_estimate=half_cost(mine, gradient),
+        compiler_params=PARAMS,
+        name="update_near",
+    )(place, weights, mine, gradient, error)
+
+
+def far_kernel(place, weights, inverse, mine, theirs, gradient, error, near, out, right, blocks, done):
+    core, block, chip, parity = (place[i] for i in range(4))
+    factor = halves(weights[...], 0)
+    copies = half_kernel(factor, theirs, 1 - core, gradient, error, out, blocks, done)
     s = jnp.where(core == parity, mine[chip, block], theirs[chip, block])
     right[...] = jnp.dot(inverse[...], s, precision=HIGHEST, preferred_element_type=jnp.float32)
     for copy in copies:
@@ -241,21 +252,19 @@
 
 
 def update_far(place, weights, inverse, mine, theirs, near, gradient, error):
-    _, rows, cols = gradient.shape
-    chips, groups, rank, _ = mine.shape
+    rank = mine.shape[2]
     return pl.pallas_call(
         far_kernel,
-        in_specs=[SCALARS] + [VECTORS] * 7,
+        in_specs=[SCALARS] + [VECTORS] * 6 + [pl.BlockSpec(memory_space=pl.ANY)],
         out_specs=[pl.BlockSpec(memory_space=pl.ANY), VECTORS],
         out_shape=[jax.ShapeDtypeStruct(gradient.shape, gradient.dtype),
                    jax.ShapeDtypeStruct((rank, BLOCK), jnp.float32)],
-        scratch_shapes=[pltpu.VMEM((groups, rows, cols // groups), gradient.dtype),
-                        pltpu.SemaphoreType.DMA((groups,))],
-        cost_estimate=pl.CostEstimate(
-            flops=4 * rows * cols * rank, bytes_accessed=6 * rows * cols, transcendentals=0),
+        input_output_aliases={7: 0},
+        scratch_shapes=half_scratch(theirs, gradient),
+        cost_estimate=half_cost(theirs, gradient),
         compiler_params=PARAMS,
         name="update_far",
-    )(place, weights, inverse, mine, theirs, near, gradient, error)
+    )(place, weights, inverse, mine, theirs, gradient, error, near)
 
 
 def body(gradient, error, q_prev):
@@ -281,10 +290,10 @@
 
     def along(value, apart):
         return lax.ppermute(value, "mp", [(j, j ^ (apart * replicas)) for j in range(shards)])
-    pair = jnp.concatenate([q_block, along(q_block, 4)], axis=0)
+    pair = jnp.concatenate([q_block, along(q_block, 1)], axis=0)
     paired, pair = lax.optimization_barrier((keep + swap_cores(give, replicas), pair))
     parts = exchange(paired, "replica", chip_groups)
-    pairs = [pair] + [along(pair, apart) for apart in (1, 2, 3)]
+    pairs = [pair] + [along(pair, apart) for apart in (2, 4, 6)]
     mean, copies = product(outer.reshape(1), parts, pairs, replicas)
 
     p_mean, tiles = pack(exchange(copies, "replica"), mean, shards)

time: 133 us -> 132 us (level)
  starting transfers between devices: 46 us -> 44.5 us
    all_to_all x2, starting transfers between devices: 13.9 us -> 11.3 us  [exchange(): return lax.all_to_all(value, axis, 0, 0, axis_index_groups=groups)]
    all_to_all x2, waiting for transfers between devices: 1.68 us -> 0.01 us  [exchange(): return lax.all_to_all(value, axis, 0, 0, axis_index_groups=groups)]
    ppermute x4, waiting for transfers between devices: 4.87 us -> 6.46 us  [along(): lax.ppermute(value, 'mp', [(j, j ^ apart * replicas) for j in range(shard...]
  transfers between devices with their start and end apart: 9 -> 9, of which waited for: 5 -> 3; matrix products, arithmetic and copies ran while one was open for 9% -> 9% of each run, Pallas kernels for 2% -> 3%
where the time goes in v8:
time: 132 us
  blocking collectives  54.6 us (41%)
  starting transfers between devices  44.5 us (34%)
  other arithmetic  13.3 us (10%)
  Pallas kernels  7.86 us (6%)
  waiting for transfers between devices  6.76 us (5%)
  local copies, waits for them, and re-layouts  3.49 us (3%)
    all_to_all x3, blocking collectives, exchange(): return lax.all_to_all(value, axis, 0, 0, axis_index_groups=groups)  54.6 us
    ppermute x4, starting transfers between devices, along(): lax.ppermute(value, 'mp', [(j, j ^ apart * replicas) for j in range(shard...  17.4 us
    ppermute x2, starting transfers between devices, swap_cores(): return lax.ppermute(value, 'replica', [(r, r ^ 1) for r in range(replicas)])  11.3 us
    all_to_all x2, starting transfers between devices, exchange(): return lax.all_to_all(value, axis, 0, 0, axis_index_groups=groups)  11.3 us
    another operation x3, other arithmetic, body(): lower = jnp.linalg.cholesky(gram)  6.52 us
    ppermute x4, waiting for transfers between devices, along(): lax.ppermute(value, 'mp', [(j, j ^ apart * replicas) for j in range(shard...  6.46 us
    another operation x2, other arithmetic, body(): lax.linalg.triangular_solve(lower, jnp.eye(rank, dtype=jnp.float32), left...  5.55 us
    ppermute x1, starting transfers between devices, body(): lax.ppermute(q_prev.T[None], ('replica', 'mp'), [(r * shards + o * replic...  4.59 us
  transfers between devices with their start and end apart: 9, of which 3 were waited for; matrix products, arithmetic and copies ran while one was open for 9% of the time, Pallas kernels for 3%

profile of v8, /device:TPU:1, one launch (start us, length us, event | category | flops | bytes accessed | tf_op | source)
XLA Modules:
  0.0 131.7 jit_solution(11448685600506172426)
XLA Ops:
  0.6 4.6 %collective-permute-start = (f32[1,64,128]{2,1,0:T(8,128)}, f32[1,64,128]{2,1,0:T(8,128)S(1)}, u32[]{:S(2)}, u32[]{:S(2)}) collective-permute-start(f32[1,64,128]{2,1,0:T(8,128)} %bitcast.25), channel_id=1, source_target_pairs={{0,0},{1,64},{2,128},{3,192},{4,256},{5,320},{6,384},{7,448},{8,8}... | collective-permute-start | bytes 98312 | tf_op jit(solution)/shard_map/ppermute | solution.py:283
  5.2 0.0 copy-start
  5.3 1.2 copy-done
  6.5 0.0 copy-start.2
  6.5 1.2 copy-done.2
  7.7 0.5 split_moment.1
  8.2 0.0 collective-permute-done
  8.3 5.6 %collective-permute-start.1 = (f32[4,64,1024]{2,1,0:T(8,128)S(1)}, f32[4,64,1024]{2,1,0:T(8,128)S(1)}, u32[]{:S(2)}, u32[]{:S(2)}) collective-permute-start(f32[4,64,1024]{2,1,0:T(8,128)S(1)} %get-tuple-element.24), channel_id=1, source_target_pairs={{0,64},{64,0},{128,192},{192,128},{256,320},{320,256},{384,448},{4... | collective-permute-start | bytes 3145736 | tf_op jit(solution)/shard_map/ppermute | solution.py:21
  13.8 1.9 %collective-permute-start.2 = (f32[1,64,128]{2,1,0:T(8,128)S(1)}, f32[1,64,128]{2,1,0:T(8,128)S(1)}, u32[]{:S(2)}, u32[]{:S(2)}) collective-permute-start(f32[1,64,128]{2,1,0:T(8,128)S(1)} %collective-permute-done), channel_id=1, source_target_pairs={{0,8},{1,9},{2,10},{3,11},{4,12},{5,13},{6,14},{7,15},{8,0},{9,1},... | collective-permute-start | bytes 98312 | tf_op jit(solution)/shard_map/ppermute | solution.py:292
  15.8 2.7 %collective-permute-done.2 = f32[1,64,128]{2,1,0:T(8,128)S(1)} collective-permute-done((f32[1,64,128]{2,1,0:T(8,128)S(1)}, f32[1,64,128]{2,1,0:T(8,128)S(1)}, u32[]{:S(2)}, u32[]{:S(2)}) %collective-permute-start.2) | collective-permute-done | bytes 32800 | tf_op jit(solution)/shard_map/ppermute | solution.py:292
  18.5 0.0 collective-permute-done.1
  18.5 1.2 add.29
  19.7 7.6 %all-to-all-start = ((f32[4,64,1024]{2,1,0:T(8,128)}), f32[4,64,1024]{2,1,0:T(8,128)S(1)}, u32[]{:S(2)}, u32[]{:S(2)}) async-start(f32[4,64,1024]{2,1,0:T(8,128)} %add.29), calls=%async_computation | async-start | bytes 2097152 | tf_op jit(solution)/shard_map/all_to_all | solution.py:17
  27.3 9.6 %collective-permute-start.5 = (f32[2,64,128]{2,1,0:T(8,128)S(1)}, f32[2,64,128]{2,1,0:T(8,128)S(1)}, u32[]{:S(2)}, u32[]{:S(2)}) collective-permute-start(f32[2,64,128]{2,1,0:T(8,128)S(1)} %pad_maximum_fusion.refs_0_), channel_id=1, source_target_pairs={{0,48},{1,49},{2,50},{3,51},{4,52},{5,53},{6,54},{7,55},{8,56},{9,... | collective-permute-start | bytes 196616 | tf_op jit(solution)/shard_map/ppermute | solution.py:292
  36.9 1.9 %collective-permute-start.4 = (f32[2,64,128]{2,1,0:T(8,128)S(1)}, f32[2,64,128]{2,1,0:T(8,128)S(1)}, u32[]{:S(2)}, u32[]{:S(2)}) collective-permute-start(f32[2,64,128]{2,1,0:T(8,128)S(1)} %pad_maximum_fusion.refs_0_), channel_id=1, source_target_pairs={{0,32},{1,33},{2,34},{3,35},{4,36},{5,37},{6,38},{7,39},{8,40},{9,... | collective-permute-start | bytes 196616 | tf_op jit(solution)/shard_map/ppermute | solution.py:292
  38.8 4.0 %collective-permute-start.3 = (f32[2,64,128]{2,1,0:T(8,128)S(1)}, f32[2,64,128]{2,1,0:T(8,128)S(1)}, u32[]{:S(2)}, u32[]{:S(2)}) collective-permute-start(f32[2,64,128]{2,1,0:T(8,128)S(1)} %pad_maximum_fusion.refs_0_), channel_id=1, source_target_pairs={{0,16},{1,17},{2,18},{3,19},{4,20},{5,21},{6,22},{7,23},{8,24},{9,... | collective-permute-start | bytes 196616 | tf_op jit(solution)/shard_map/ppermute | solution.py:292
  42.8 0.0 collective-permute-done.5.refs_3_
  42.8 3.7 %collective-permute-done.4.refs_2_ = f32[2,64,128]{2,1,0:T(8,128)S(1)} collective-permute-done((f32[2,64,128]{2,1,0:T(8,128)S(1)}, f32[2,64,128]{2,1,0:T(8,128)S(1)}, u32[]{:S(2)}, u32[]{:S(2)}) %collective-permute-start.4) | collective-permute-done | bytes 65568 | tf_op jit(solution)/shard_map/ppermute | solution.py:292
  46.5 0.0 collective-permute-done.3.refs_1_
  46.5 0.0 all-to-all-done.parts
  46.5 0.5 product.1
  47.0 13.2 %all_to_all.25.p_parts = f32[8,32,128]{2,1,0:T(8,128)S(1)} all-to-all(f32[8,32,128]{2,1,0:T(8,128)S(1)} %get-tuple-element.28), channel_id=1, replica_groups=mesh['replica'=8,'mp'=64] {'replica'}, dimensions={0} | all-to-all | bytes 262144 | tf_op jit(solution)/shard_map/all_to_all | solution.py:17
  60.2 0.6 pack.1
  60.8 23.0 %all_to_all.26 = f32[64,9,1,128]{3,2,1,0:T(1,128)S(1)} all-to-all(f32[64,9,1,128]{3,2,1,0:T(1,128)S(1)} %bitcast.24), channel_id=1, replica_groups=mesh['replica'=8,'mp'=64] {'mp'}, dimensions={0} | all-to-all | bytes 589824 | tf_op jit(solution)/shard_map/all_to_all | solution.py:17
  83.9 0.1 total.1
  83.9 18.4 %all_to_all.27 = f32[64,9,1,128]{3,2,1,0:T(1,128)S(1)} all-to-all(f32[64,9,1,128]{3,2,1,0:T(1,128)S(1)} %bitcast.23), channel_id=1, replica_groups=mesh['replica'=8,'mp'=64] {'mp'}, dimensions={0} | all-to-all | bytes 589824 | tf_op jit(solution)/shard_map/all_to_all | solution.py:17
  102.3 0.1 unpack.1
  102.4 0.0 copy-start.4
  102.4 1.0 copy-done.4
  103.4 0.0 copy-start.1
  103.4 0.0 copy-start.3
  103.4 3.6 %all-to-all-start.4 = ((f32[4,8,64,128]{3,2,1,0:T(8,128)}), f32[4,8,64,128]{3,2,1,0:T(8,128)S(1)}, u32[]{:S(2)}, u32[]{:S(2)}) async-start(f32[4,8,64,128]{3,2,1,0:T(8,128)} %copy-done.4), calls=%async_computation.4 | async-start | bytes 2097152 | tf_op jit(solution)/shard_map/all_to_all | solution.py:17
  107.0 0.1 copy.11
  107.1 5.8 %cholesky.17 = f32[64,64]{1,0:T(8,128)S(1)} custom-call(f32[64,64]{1,0:T(8,128)S(1)} %fusion.3), custom_call_target="Cholesky" | custom-call | tf_op jit(solution)/shard_map/jit(cholesky)/cholesky | solution.py:306
  113.0 0.6 compare_reduce_fusion
  113.6 0.7 fusion
  114.3 4.9 %custom-call.6 = f32[1,64,64]{1,2,0:T(8,128)S(1)} custom-call(f32[1,64,64]{2,1,0:T(8,128)S(1)} %fusion), custom_call_target="InvertDiagBlocksLowerTriangular" | custom-call | tf_op jit(solution)/shard_map/triangular_solve | solution.py:307
  119.2 0.2 fusion.1.inverse
  119.4 0.8 factors.1
  120.3 0.0 all-to-all-done.4.mine
  120.3 5.7 %collective-permute-start.6 = (f32[4,8,64,128]{3,2,1,0:T(8,128)S(1)}, f32[4,8,64,128]{3,2,1,0:T(8,128)}, u32[]{:S(2)}, u32[]{:S(2)}) collective-permute-start(f32[4,8,64,128]{3,2,1,0:T(8,128)S(1)} %all-to-all-done.4.mine), channel_id=1, source_target_pairs={{0,64},{64,0},{128,192},{192,128},{256,320},{320,256},{384,448},{4... | collective-permute-start | bytes 3145736 | tf_op jit(solution)/shard_map/ppermute | solution.py:21
  126.0 0.1 pad_add_fusion.place
  126.1 0.0 copy-done.1
  126.1 0.0 copy-done.3
  126.1 2.0 %update_near.1.near = bf16[1,64,8192]{2,1,0:T(8,128)(2,1)} custom-call(s32[4]{0:T(128)S(1)} %pad_add_fusion.place, f32[64,128]{1,0:T(8,128)S(1)} %get-tuple-element.35.weights, f32[4,8,64,128]{3,2,1,0:T(8,128)S(1)} %all-to-all-done.4.mine, bf16[1,64,8192]{2,1,0:T(8,128)(2,1)S(1)} %copy-done.1, bf16[1,64,8192]{2,1,0:T(8,128)(2,1)S(1)} %copy-done.3), custom_call_target="tpu_custom_call" | custom-call | flops 134217728 | bytes 2097152 | tf_op jit(solution)/shard_map/update_near/pallas_call | solution.py:232
  128.1 0.3 collective-permute-done.6.theirs
  128.4 3.3 %update_far.1 = (bf16[1,64,8192]{2,1,0:T(8,128)(2,1)}, f32[64,128]{1,0:T(8,128)}) custom-call(s32[4]{0:T(128)S(1)} %pad_add_fusion.place, f32[64,128]{1,0:T(8,128)S(1)} %get-tuple-element.35.weights, f32[64,64]{1,0:T(8,128)S(1)} %fusion.1.inverse, f32[4,8,64,128]{3,2,1,0:T(8,128)S(1)} %all-to-all-done.4.mine, ...), custom_call_target="tpu_custom_call", output_to_operand_aliasing={{0}: (7, {})} | custom-call | flops 134217728 | bytes 2097152 | tf_op jit(solution)/shard_map/update_far/pallas_call | solution.py:256
  (3 shorter events, 0.0 us)
Async XLA Ops:
  0.6 7.6 %collective-permute-start = (f32[1,64,128]{2,1,0:T(8,128)}, f32[1,64,128]{2,1,0:T(8,128)S(1)}, u32[]{:S(2)}, u32[]{:S(2)}) collective-permute-start(f32[1,64,128]{2,1,0:T(8,128)} %bitcast.25), channel_id=1, source_target_pairs={{0,0},{1,64},{2,128},{3,192},{4,256},{5,320},{6,384},{7,448},{8,8}... | collective-permute-start | bytes 98312 | tf_op jit(solution)/shard_map/ppermute | solution.py:283
  5.2 1.2 copy-start
  6.5 1.2 copy-start.2
  8.3 10.3 %collective-permute-start.1 = (f32[4,64,1024]{2,1,0:T(8,128)S(1)}, f32[4,64,1024]{2,1,0:T(8,128)S(1)}, u32[]{:S(2)}, u32[]{:S(2)}) collective-permute-start(f32[4,64,1024]{2,1,0:T(8,128)S(1)} %get-tuple-element.24), channel_id=1, source_target_pairs={{0,64},{64,0},{128,192},{192,128},{256,320},{320,256},{384,448},{4... | collective-permute-start | bytes 3145736 | tf_op jit(solution)/shard_map/ppermute | solution.py:21
  13.8 4.7 %collective-permute-start.2 = (f32[1,64,128]{2,1,0:T(8,128)S(1)}, f32[1,64,128]{2,1,0:T(8,128)S(1)}, u32[]{:S(2)}, u32[]{:S(2)}) collective-permute-start(f32[1,64,128]{2,1,0:T(8,128)S(1)} %collective-permute-done), channel_id=1, source_target_pairs={{0,8},{1,9},{2,10},{3,11},{4,12},{5,13},{6,14},{7,15},{8,0},{9,1},... | collective-permute-start | bytes 98312 | tf_op jit(solution)/shard_map/ppermute | solution.py:292
  19.7 26.9 %all-to-all-start = ((f32[4,64,1024]{2,1,0:T(8,128)}), f32[4,64,1024]{2,1,0:T(8,128)S(1)}, u32[]{:S(2)}, u32[]{:S(2)}) async-start(f32[4,64,1024]{2,1,0:T(8,128)} %add.29), calls=%async_computation | async-start | bytes 2097152 | tf_op jit(solution)/shard_map/all_to_all | solution.py:17
  27.3 15.5 %collective-permute-start.5 = (f32[2,64,128]{2,1,0:T(8,128)S(1)}, f32[2,64,128]{2,1,0:T(8,128)S(1)}, u32[]{:S(2)}, u32[]{:S(2)}) collective-permute-start(f32[2,64,128]{2,1,0:T(8,128)S(1)} %pad_maximum_fusion.refs_0_), channel_id=1, source_target_pairs={{0,48},{1,49},{2,50},{3,51},{4,52},{5,53},{6,54},{7,55},{8,56},{9,... | collective-permute-start | bytes 196616 | tf_op jit(solution)/shard_map/ppermute | solution.py:292
  36.9 9.7 %collective-permute-start.4 = (f32[2,64,128]{2,1,0:T(8,128)S(1)}, f32[2,64,128]{2,1,0:T(8,128)S(1)}, u32[]{:S(2)}, u32[]{:S(2)}) collective-permute-start(f32[2,64,128]{2,1,0:T(8,128)S(1)} %pad_maximum_fusion.refs_0_), channel_id=1, source_target_pairs={{0,32},{1,33},{2,34},{3,35},{4,36},{5,37},{6,38},{7,39},{8,40},{9,... | collective-permute-start | bytes 196616 | tf_op jit(solution)/shard_map/ppermute | solution.py:292
  38.8 7.7 %collective-permute-start.3 = (f32[2,64,128]{2,1,0:T(8,128)S(1)}, f32[2,64,128]{2,1,0:T(8,128)S(1)}, u32[]{:S(2)}, u32[]{:S(2)}) collective-permute-start(f32[2,64,128]{2,1,0:T(8,128)S(1)} %pad_maximum_fusion.refs_0_), channel_id=1, source_target_pairs={{0,16},{1,17},{2,18},{3,19},{4,20},{5,21},{6,22},{7,23},{8,24},{9,... | collective-permute-start | bytes 196616 | tf_op jit(solution)/shard_map/ppermute | solution.py:292
  102.4 1.0 copy-start.4
  103.4 22.7 %copy-start.1 = (bf16[1,64,8192]{2,1,0:T(8,128)(2,1)S(1)}, bf16[1,64,8192]{2,1,0:T(8,128)(2,1)}, u32[]{:S(2)}) copy-start(bf16[1,64,8192]{2,1,0:T(8,128)(2,1)} %gradient.5) | copy-start | bytes 3145732
  103.4 22.7 %copy-start.3 = (bf16[1,64,8192]{2,1,0:T(8,128)(2,1)S(1)}, bf16[1,64,8192]{2,1,0:T(8,128)(2,1)}, u32[]{:S(2)}) copy-start(bf16[1,64,8192]{2,1,0:T(8,128)(2,1)} %error.5) | copy-start | bytes 3145732
  103.4 16.9 %all-to-all-start.4 = ((f32[4,8,64,128]{3,2,1,0:T(8,128)}), f32[4,8,64,128]{3,2,1,0:T(8,128)S(1)}, u32[]{:S(2)}, u32[]{:S(2)}) async-start(f32[4,8,64,128]{3,2,1,0:T(8,128)} %copy-done.4), calls=%async_computation.4 | async-start | bytes 2097152 | tf_op jit(solution)/shard_map/all_to_all | solution.py:17
  120.3 8.1 %collective-permute-start.6 = (f32[4,8,64,128]{3,2,1,0:T(8,128)S(1)}, f32[4,8,64,128]{3,2,1,0:T(8,128)}, u32[]{:S(2)}, u32[]{:S(2)}) collective-permute-start(f32[4,8,64,128]{3,2,1,0:T(8,128)S(1)} %all-to-all-done.4.mine), channel_id=1, source_target_pairs={{0,64},{64,0},{128,192},{192,128},{256,320},{320,256},{384,448},{4... | collective-permute-start | bytes 3145736 | tf_op jit(solution)/shard_map/ppermute | solution.py:21

commit v9 on v8

--- a/solution.py
+++ b/solution.py
@@ -241,13 +241,15 @@
     )(place, weights, mine, gradient, error)
 
 
-def far_kernel(place, weights, inverse, mine, theirs, gradient, error, near, out, right, blocks, done):
+def far_kernel(place, weights, inverse, mine, theirs, gradient, error, near, out, right, blocks, done, held, sent):
     core, block, chip, parity = (place[i] for i in range(4))
+    s = jnp.where(core == parity, mine[chip, block], theirs[chip, block])
+    held[...] = jnp.dot(inverse[...], s, precision=HIGHEST, preferred_element_type=jnp.float32)
+    send = pltpu.make_async_copy(held, right, sent)
+    send.start()
     factor = halves(weights[...], 0)
     copies = half_kernel(factor, theirs, 1 - core, gradient, error, out, blocks, done)
-    s = jnp.where(core == parity, mine[chip, block], theirs[chip, block])
-    right[...] = jnp.dot(inverse[...], s, precision=HIGHEST, preferred_element_type=jnp.float32)
-    for copy in copies:
+    for copy in copies + [send]:
         copy.wait()
 
 
@@ -256,11 +258,12 @@
     return pl.pallas_call(
         far_kernel,
         in_specs=[SCALARS] + [VECTORS] * 6 + [pl.BlockSpec(memory_space=pl.ANY)],
-        out_specs=[pl.BlockSpec(memory_space=pl.ANY), VECTORS],
+        out_specs=[pl.BlockSpec(memory_space=pl.ANY)] * 2,
         out_shape=[jax.ShapeDtypeStruct(gradient.shape, gradient.dtype),
                    jax.ShapeDtypeStruct((rank, BLOCK), jnp.float32)],
         input_output_aliases={7: 0},
-        scratch_shapes=half_scratch(theirs, gradient),
+        scratch_shapes=half_scratch(theirs, gradient) + [
+            pltpu.VMEM((rank, BLOCK), jnp.float32), pltpu.SemaphoreType.DMA],
         cost_estimate=half_cost(theirs, gradient),
         compiler_params=PARAMS,
         name="update_far",

time: 132 us -> 132 us (level)
  transfers between devices with their start and end apart: 9 -> 9, of which waited for: 3 -> 3; matrix products, arithmetic and copies ran while one was open for 9% -> 10% of each run, Pallas kernels for 3% -> 3%
where the time goes in v9:
time: 132 us; the launch traced here: 131 us
  blocking collectives  54.6 us (41%)
  starting transfers between devices  44.5 us (34%)
  other arithmetic  13.3 us (10%)
  Pallas kernels  7.21 us (5%)
  waiting for transfers between devices  6.76 us (5%)
  local copies, waits for them, and re-layouts  3.49 us (3%)
    all_to_all x3, blocking collectives, exchange(): return lax.all_to_all(value, axis, 0, 0, axis_index_groups=groups)  54.6 us
    ppermute x4, starting transfers between devices, along(): lax.ppermute(value, 'mp', [(j, j ^ apart * replicas) for j in range(shard...  17.4 us
    ppermute x2, starting transfers between devices, swap_cores(): return lax.ppermute(value, 'replica', [(r, r ^ 1) for r in range(replicas)])  11.3 us
    all_to_all x2, starting transfers between devices, exchange(): return lax.all_to_all(value, axis, 0, 0, axis_index_groups=groups)  11.3 us
    another operation x3, other arithmetic, body(): lower = jnp.linalg.cholesky(gram)  6.52 us
    ppermute x4, waiting for transfers between devices, along(): lax.ppermute(value, 'mp', [(j, j ^ apart * replicas) for j in range(shard...  6.46 us
    another operation x2, other arithmetic, body(): lax.linalg.triangular_solve(lower, jnp.eye(rank, dtype=jnp.float32), left...  5.55 us
    ppermute x1, starting transfers between devices, body(): lax.ppermute(q_prev.T[None], ('replica', 'mp'), [(r * shards + o * replic...  4.59 us
  transfers between devices with their start and end apart: 9, of which 3 were waited for; matrix products, arithmetic and copies ran while one was open for 10% of the time, Pallas kernels for 3%

profile of v9, /device:TPU:1, one launch (start us, length us, event | category | flops | bytes accessed | tf_op | source)
XLA Modules:
  0.0 131.0 jit_solution(8488477704943411267)
XLA Ops:
  0.6 4.6 %collective-permute-start = (f32[1,64,128]{2,1,0:T(8,128)}, f32[1,64,128]{2,1,0:T(8,128)S(1)}, u32[]{:S(2)}, u32[]{:S(2)}) collective-permute-start(f32[1,64,128]{2,1,0:T(8,128)} %bitcast.25), channel_id=1, source_target_pairs={{0,0},{1,64},{2,128},{3,192},{4,256},{5,320},{6,384},{7,448},{8,8}... | collective-permute-start | bytes 98312 | tf_op jit(solution)/shard_map/ppermute | solution.py:286
  5.2 0.0 copy-start
  5.3 1.2 copy-done
  6.5 0.0 copy-start.2
  6.5 1.2 copy-done.2
  7.7 0.5 split_moment.1
  8.2 0.0 collective-permute-done
  8.3 5.6 %collective-permute-start.1 = (f32[4,64,1024]{2,1,0:T(8,128)S(1)}, f32[4,64,1024]{2,1,0:T(8,128)S(1)}, u32[]{:S(2)}, u32[]{:S(2)}) collective-permute-start(f32[4,64,1024]{2,1,0:T(8,128)S(1)} %get-tuple-element.24), channel_id=1, source_target_pairs={{0,64},{64,0},{128,192},{192,128},{256,320},{320,256},{384,448},{4... | collective-permute-start | bytes 3145736 | tf_op jit(solution)/shard_map/ppermute | solution.py:21
  13.8 1.9 %collective-permute-start.2 = (f32[1,64,128]{2,1,0:T(8,128)S(1)}, f32[1,64,128]{2,1,0:T(8,128)S(1)}, u32[]{:S(2)}, u32[]{:S(2)}) collective-permute-start(f32[1,64,128]{2,1,0:T(8,128)S(1)} %collective-permute-done), channel_id=1, source_target_pairs={{0,8},{1,9},{2,10},{3,11},{4,12},{5,13},{6,14},{7,15},{8,0},{9,1},... | collective-permute-start | bytes 98312 | tf_op jit(solution)/shard_map/ppermute | solution.py:295
  15.8 2.7 %collective-permute-done.2 = f32[1,64,128]{2,1,0:T(8,128)S(1)} collective-permute-done((f32[1,64,128]{2,1,0:T(8,128)S(1)}, f32[1,64,128]{2,1,0:T(8,128)S(1)}, u32[]{:S(2)}, u32[]{:S(2)}) %collective-permute-start.2) | collective-permute-done | bytes 32800 | tf_op jit(solution)/shard_map/ppermute | solution.py:295
  18.5 0.0 collective-permute-done.1
  18.5 1.2 add.29
  19.7 7.6 %all-to-all-start = ((f32[4,64,1024]{2,1,0:T(8,128)}), f32[4,64,1024]{2,1,0:T(8,128)S(1)}, u32[]{:S(2)}, u32[]{:S(2)}) async-start(f32[4,64,1024]{2,1,0:T(8,128)} %add.29), calls=%async_computation | async-start | bytes 2097152 | tf_op jit(solution)/shard_map/all_to_all | solution.py:17
  27.3 9.6 %collective-permute-start.5 = (f32[2,64,128]{2,1,0:T(8,128)S(1)}, f32[2,64,128]{2,1,0:T(8,128)S(1)}, u32[]{:S(2)}, u32[]{:S(2)}) collective-permute-start(f32[2,64,128]{2,1,0:T(8,128)S(1)} %pad_maximum_fusion.refs_0_), channel_id=1, source_target_pairs={{0,48},{1,49},{2,50},{3,51},{4,52},{5,53},{6,54},{7,55},{8,56},{9,... | collective-permute-start | bytes 196616 | tf_op jit(solution)/shard_map/ppermute | solution.py:295
  36.9 1.9 %collective-permute-start.4 = (f32[2,64,128]{2,1,0:T(8,128)S(1)}, f32[2,64,128]{2,1,0:T(8,128)S(1)}, u32[]{:S(2)}, u32[]{:S(2)}) collective-permute-start(f32[2,64,128]{2,1,0:T(8,128)S(1)} %pad_maximum_fusion.refs_0_), channel_id=1, source_target_pairs={{0,32},{1,33},{2,34},{3,35},{4,36},{5,37},{6,38},{7,39},{8,40},{9,... | collective-permute-start | bytes 196616 | tf_op jit(solution)/shard_map/ppermute | solution.py:295
  38.8 4.0 %collective-permute-start.3 = (f32[2,64,128]{2,1,0:T(8,128)S(1)}, f32[2,64,128]{2,1,0:T(8,128)S(1)}, u32[]{:S(2)}, u32[]{:S(2)}) collective-permute-start(f32[2,64,128]{2,1,0:T(8,128)S(1)} %pad_maximum_fusion.refs_0_), channel_id=1, source_target_pairs={{0,16},{1,17},{2,18},{3,19},{4,20},{5,21},{6,22},{7,23},{8,24},{9,... | collective-permute-start | bytes 196616 | tf_op jit(solution)/shard_map/ppermute | solution.py:295
  42.8 0.0 collective-permute-done.5.refs_3_
  42.8 3.7 %collective-permute-done.4.refs_2_ = f32[2,64,128]{2,1,0:T(8,128)S(1)} collective-permute-done((f32[2,64,128]{2,1,0:T(8,128)S(1)}, f32[2,64,128]{2,1,0:T(8,128)S(1)}, u32[]{:S(2)}, u32[]{:S(2)}) %collective-permute-start.4) | collective-permute-done | bytes 65568 | tf_op jit(solution)/shard_map/ppermute | solution.py:295
  46.5 0.0 collective-permute-done.3.refs_1_
  46.5 0.0 all-to-all-done.parts
  46.5 0.5 product.1
  47.0 13.2 %all_to_all.25.p_parts = f32[8,32,128]{2,1,0:T(8,128)S(1)} all-to-all(f32[8,32,128]{2,1,0:T(8,128)S(1)} %get-tuple-element.28), channel_id=1, replica_groups=mesh['replica'=8,'mp'=64] {'replica'}, dimensions={0} | all-to-all | bytes 262144 | tf_op jit(solution)/shard_map/all_to_all | solution.py:17
  60.2 0.6 pack.1
  60.8 23.0 %all_to_all.26 = f32[64,9,1,128]{3,2,1,0:T(1,128)S(1)} all-to-all(f32[64,9,1,128]{3,2,1,0:T(1,128)S(1)} %bitcast.24), channel_id=1, replica_groups=mesh['replica'=8,'mp'=64] {'mp'}, dimensions={0} | all-to-all | bytes 589824 | tf_op jit(solution)/shard_map/all_to_all | solution.py:17
  83.9 0.1 total.1
  83.9 18.4 %all_to_all.27 = f32[64,9,1,128]{3,2,1,0:T(1,128)S(1)} all-to-all(f32[64,9,1,128]{3,2,1,0:T(1,128)S(1)} %bitcast.23), channel_id=1, replica_groups=mesh['replica'=8,'mp'=64] {'mp'}, dimensions={0} | all-to-all | bytes 589824 | tf_op jit(solution)/shard_map/all_to_all | solution.py:17
  102.3 0.1 unpack.1
  102.4 0.0 copy-start.4
  102.4 1.0 copy-done.4
  103.4 0.0 copy-start.1
  103.4 0.0 copy-start.3
  103.4 3.6 %all-to-all-start.4 = ((f32[4,8,64,128]{3,2,1,0:T(8,128)}), f32[4,8,64,128]{3,2,1,0:T(8,128)S(1)}, u32[]{:S(2)}, u32[]{:S(2)}) async-start(f32[4,8,64,128]{3,2,1,0:T(8,128)} %copy-done.4), calls=%async_computation.4 | async-start | bytes 2097152 | tf_op jit(solution)/shard_map/all_to_all | solution.py:17
  107.0 0.1 copy.11
  107.1 5.8 %cholesky.17 = f32[64,64]{1,0:T(8,128)S(1)} custom-call(f32[64,64]{1,0:T(8,128)S(1)} %fusion.3), custom_call_target="Cholesky" | custom-call | tf_op jit(solution)/shard_map/jit(cholesky)/cholesky | solution.py:309
  113.0 0.6 compare_reduce_fusion
  113.6 0.7 fusion
  114.3 4.9 %custom-call.6 = f32[1,64,64]{1,2,0:T(8,128)S(1)} custom-call(f32[1,64,64]{2,1,0:T(8,128)S(1)} %fusion), custom_call_target="InvertDiagBlocksLowerTriangular" | custom-call | tf_op jit(solution)/shard_map/triangular_solve | solution.py:310
  119.2 0.2 fusion.1.inverse
  119.4 0.8 factors.1
  120.3 0.0 all-to-all-done.4.mine
  120.3 5.7 %collective-permute-start.6 = (f32[4,8,64,128]{3,2,1,0:T(8,128)S(1)}, f32[4,8,64,128]{3,2,1,0:T(8,128)}, u32[]{:S(2)}, u32[]{:S(2)}) collective-permute-start(f32[4,8,64,128]{3,2,1,0:T(8,128)S(1)} %all-to-all-done.4.mine), channel_id=1, source_target_pairs={{0,64},{64,0},{128,192},{192,128},{256,320},{320,256},{384,448},{4... | collective-permute-start | bytes 3145736 | tf_op jit(solution)/shard_map/ppermute | solution.py:21
  126.0 0.1 pad_add_fusion.place
  126.1 0.0 copy-done.1
  126.1 0.0 copy-done.3
  126.1 2.0 %update_near.1.near = bf16[1,64,8192]{2,1,0:T(8,128)(2,1)} custom-call(s32[4]{0:T(128)S(1)} %pad_add_fusion.place, f32[64,128]{1,0:T(8,128)S(1)} %get-tuple-element.35.weights, f32[4,8,64,128]{3,2,1,0:T(8,128)S(1)} %all-to-all-done.4.mine, bf16[1,64,8192]{2,1,0:T(8,128)(2,1)S(1)} %copy-done.1, bf16[1,64,8192]{2,1,0:T(8,128)(2,1)S(1)} %copy-done.3), custom_call_target="tpu_custom_call" | custom-call | flops 134217728 | bytes 2097152 | tf_op jit(solution)/shard_map/update_near/pallas_call | solution.py:232
  128.1 0.3 collective-permute-done.6.theirs
  128.4 2.6 %update_far.1 = (bf16[1,64,8192]{2,1,0:T(8,128)(2,1)}, f32[64,128]{1,0:T(8,128)}) custom-call(s32[4]{0:T(128)S(1)} %pad_add_fusion.place, f32[64,128]{1,0:T(8,128)S(1)} %get-tuple-element.35.weights, f32[64,64]{1,0:T(8,128)S(1)} %fusion.1.inverse, f32[4,8,64,128]{3,2,1,0:T(8,128)S(1)} %all-to-all-done.4.mine, ...), custom_call_target="tpu_custom_call", output_to_operand_aliasing={{0}: (7, {})} | custom-call | flops 134217728 | bytes 2097152 | tf_op jit(solution)/shard_map/update_far/pallas_call | solution.py:258
  (3 shorter events, 0.0 us)
Async XLA Ops:
  0.6 7.6 %collective-permute-start = (f32[1,64,128]{2,1,0:T(8,128)}, f32[1,64,128]{2,1,0:T(8,128)S(1)}, u32[]{:S(2)}, u32[]{:S(2)}) collective-permute-start(f32[1,64,128]{2,1,0:T(8,128)} %bitcast.25), channel_id=1, source_target_pairs={{0,0},{1,64},{2,128},{3,192},{4,256},{5,320},{6,384},{7,448},{8,8}... | collective-permute-start | bytes 98312 | tf_op jit(solution)/shard_map/ppermute | solution.py:286
  5.2 1.2 copy-start
  6.5 1.2 copy-start.2
  8.3 10.3 %collective-permute-start.1 = (f32[4,64,1024]{2,1,0:T(8,128)S(1)}, f32[4,64,1024]{2,1,0:T(8,128)S(1)}, u32[]{:S(2)}, u32[]{:S(2)}) collective-permute-start(f32[4,64,1024]{2,1,0:T(8,128)S(1)} %get-tuple-element.24), channel_id=1, source_target_pairs={{0,64},{64,0},{128,192},{192,128},{256,320},{320,256},{384,448},{4... | collective-permute-start | bytes 3145736 | tf_op jit(solution)/shard_map/ppermute | solution.py:21
  13.8 4.7 %collective-permute-start.2 = (f32[1,64,128]{2,1,0:T(8,128)S(1)}, f32[1,64,128]{2,1,0:T(8,128)S(1)}, u32[]{:S(2)}, u32[]{:S(2)}) collective-permute-start(f32[1,64,128]{2,1,0:T(8,128)S(1)} %collective-permute-done), channel_id=1, source_target_pairs={{0,8},{1,9},{2,10},{3,11},{4,12},{5,13},{6,14},{7,15},{8,0},{9,1},... | collective-permute-start | bytes 98312 | tf_op jit(solution)/shard_map/ppermute | solution.py:295
  19.7 26.9 %all-to-all-start = ((f32[4,64,1024]{2,1,0:T(8,128)}), f32[4,64,1024]{2,1,0:T(8,128)S(1)}, u32[]{:S(2)}, u32[]{:S(2)}) async-start(f32[4,64,1024]{2,1,0:T(8,128)} %add.29), calls=%async_computation | async-start | bytes 2097152 | tf_op jit(solution)/shard_map/all_to_all | solution.py:17
  27.3 15.5 %collective-permute-start.5 = (f32[2,64,128]{2,1,0:T(8,128)S(1)}, f32[2,64,128]{2,1,0:T(8,128)S(1)}, u32[]{:S(2)}, u32[]{:S(2)}) collective-permute-start(f32[2,64,128]{2,1,0:T(8,128)S(1)} %pad_maximum_fusion.refs_0_), channel_id=1, source_target_pairs={{0,48},{1,49},{2,50},{3,51},{4,52},{5,53},{6,54},{7,55},{8,56},{9,... | collective-permute-start | bytes 196616 | tf_op jit(solution)/shard_map/ppermute | solution.py:295
  36.9 9.7 %collective-permute-start.4 = (f32[2,64,128]{2,1,0:T(8,128)S(1)}, f32[2,64,128]{2,1,0:T(8,128)S(1)}, u32[]{:S(2)}, u32[]{:S(2)}) collective-permute-start(f32[2,64,128]{2,1,0:T(8,128)S(1)} %pad_maximum_fusion.refs_0_), channel_id=1, source_target_pairs={{0,32},{1,33},{2,34},{3,35},{4,36},{5,37},{6,38},{7,39},{8,40},{9,... | collective-permute-start | bytes 196616 | tf_op jit(solution)/shard_map/ppermute | solution.py:295
  38.8 7.7 %collective-permute-start.3 = (f32[2,64,128]{2,1,0:T(8,128)S(1)}, f32[2,64,128]{2,1,0:T(8,128)S(1)}, u32[]{:S(2)}, u32[]{:S(2)}) collective-permute-start(f32[2,64,128]{2,1,0:T(8,128)S(1)} %pad_maximum_fusion.refs_0_), channel_id=1, source_target_pairs={{0,16},{1,17},{2,18},{3,19},{4,20},{5,21},{6,22},{7,23},{8,24},{9,... | collective-permute-start | bytes 196616 | tf_op jit(solution)/shard_map/ppermute | solution.py:295
  102.4 1.0 copy-start.4
  103.4 22.7 %copy-start.1 = (bf16[1,64,8192]{2,1,0:T(8,128)(2,1)S(1)}, bf16[1,64,8192]{2,1,0:T(8,128)(2,1)}, u32[]{:S(2)}) copy-start(bf16[1,64,8192]{2,1,0:T(8,128)(2,1)} %gradient.5) | copy-start | bytes 3145732
  103.4 22.7 %copy-start.3 = (bf16[1,64,8192]{2,1,0:T(8,128)(2,1)S(1)}, bf16[1,64,8192]{2,1,0:T(8,128)(2,1)}, u32[]{:S(2)}) copy-start(bf16[1,64,8192]{2,1,0:T(8,128)(2,1)} %error.5) | copy-start | bytes 3145732
  103.4 16.9 %all-to-all-start.4 = ((f32[4,8,64,128]{3,2,1,0:T(8,128)}), f32[4,8,64,128]{3,2,1,0:T(8,128)S(1)}, u32[]{:S(2)}, u32[]{:S(2)}) async-start(f32[4,8,64,128]{3,2,1,0:T(8,128)} %copy-done.4), calls=%async_computation.4 | async-start | bytes 2097152 | tf_op jit(solution)/shard_map/all_to_all | solution.py:17
  120.3 8.1 %collective-permute-start.6 = (f32[4,8,64,128]{3,2,1,0:T(8,128)S(1)}, f32[4,8,64,128]{3,2,1,0:T(8,128)}, u32[]{:S(2)}, u32[]{:S(2)}) collective-permute-start(f32[4,8,64,128]{3,2,1,0:T(8,128)S(1)} %all-to-all-done.4.mine), channel_id=1, source_target_pairs={{0,64},{64,0},{128,192},{192,128},{256,320},{320,256},{384,448},{4... | collective-permute-start | bytes 3145736 | tf_op jit(solution)/shard_map/ppermute | solution.py:21

commit v10 on v9

--- a/solution.py
+++ b/solution.py
@@ -293,9 +293,9 @@
 
     def along(value, apart):
         return lax.ppermute(value, "mp", [(j, j ^ (apart * replicas)) for j in range(shards)])
+    paired, q_block = lax.optimization_barrier((keep + swap_cores(give, replicas), q_block))
+    parts = exchange(paired, "replica", chip_groups)
     pair = jnp.concatenate([q_block, along(q_block, 1)], axis=0)
-    paired, pair = lax.optimization_barrier((keep + swap_cores(give, replicas), pair))
-    parts = exchange(paired, "replica", chip_groups)
     pairs = [pair] + [along(pair, apart) for apart in (2, 4, 6)]
     mean, copies = product(outer.reshape(1), parts, pairs, replicas)
 

time: 132 us -> 134 us (1.015)
  starting transfers between devices: 44.5 us -> 46 us
    ppermute x4, starting transfers between devices: 17.4 us -> 19.9 us  [along(): lax.ppermute(value, 'mp', [(j, j ^ apart * replicas) for j in range(shard...]
    ppermute x2, waiting for transfers between devices: 0.29 us -> 2.55 us  [swap_cores(): return lax.ppermute(value, 'replica', [(r, r ^ 1) for r in range(replicas)])]
    unnamed x10 -> x11, local copies, waits for them, and re-layouts: 3.42 us -> 3.42 us
  transfers between devices with their start and end apart: 9 -> 9, of which waited for: 3 -> 4; matrix products, arithmetic and copies ran while one was open for 10% -> 9% of each run, Pallas kernels for 3% -> 3%
where the time goes in v10:
time: 134 us
  blocking collectives  54.7 us (41%)
  starting transfers between devices  46 us (34%)
  other arithmetic  13.3 us (10%)
  waiting for transfers between devices  7.88 us (6%)
  Pallas kernels  7.21 us (5%)
  local copies, waits for them, and re-layouts  3.5 us (3%)
    all_to_all x3, blocking collectives, exchange(): return lax.all_to_all(value, axis, 0, 0, axis_index_groups=groups)  54.7 us
    ppermute x4, starting transfers between devices, along(): lax.ppermute(value, 'mp', [(j, j ^ apart * replicas) for j in range(shard...  19.9 us
    ppermute x2, starting transfers between devices, swap_cores(): return lax.ppermute(value, 'replica', [(r, r ^ 1) for r in range(replicas)])  11.3 us
    all_to_all x2, starting transfers between devices, exchange(): return lax.all_to_all(value, axis, 0, 0, axis_index_groups=groups)  10.2 us
    another operation x3, other arithmetic, body(): lower = jnp.linalg.cholesky(gram)  6.52 us
    another operation x2, other arithmetic, body(): lax.linalg.triangular_solve(lower, jnp.eye(rank, dtype=jnp.float32), left...  5.55 us
    ppermute x4, waiting for transfers between devices, along(): lax.ppermute(value, 'mp', [(j, j ^ apart * replicas) for j in range(shard...  5.32 us
    ppermute x1, starting transfers between devices, body(): lax.ppermute(q_prev.T[None], ('replica', 'mp'), [(r * shards + o * replic...  4.59 us
  transfers between devices with their start and end apart: 9, of which 4 were waited for; matrix products, arithmetic and copies ran while one was open for 9% of the time, Pallas kernels for 3%

profile of v10, /device:TPU:1, one launch (start us, length us, event | category | flops | bytes accessed | tf_op | source)
XLA Modules:
  0.0 133.6 jit_solution(5904449701644025938)
XLA Ops:
  0.6 4.6 %collective-permute-start = (f32[1,64,128]{2,1,0:T(8,128)}, f32[1,64,128]{2,1,0:T(8,128)S(1)}, u32[]{:S(2)}, u32[]{:S(2)}) collective-permute-start(f32[1,64,128]{2,1,0:T(8,128)} %bitcast.25), channel_id=1, source_target_pairs={{0,0},{1,64},{2,128},{3,192},{4,256},{5,320},{6,384},{7,448},{8,8}... | collective-permute-start | bytes 98312 | tf_op jit(solution)/shard_map/ppermute | solution.py:286
  5.2 0.0 copy-start
  5.3 1.2 copy-done
  6.5 0.0 copy-start.2
  6.5 1.2 copy-done.2
  7.7 0.5 split_moment.1
  8.2 0.0 collective-permute-done
  8.3 5.6 %collective-permute-start.1 = (f32[4,64,1024]{2,1,0:T(8,128)S(1)}, f32[4,64,1024]{2,1,0:T(8,128)S(1)}, u32[]{:S(2)}, u32[]{:S(2)}) collective-permute-start(f32[4,64,1024]{2,1,0:T(8,128)S(1)} %get-tuple-element.24), channel_id=1, source_target_pairs={{0,64},{64,0},{128,192},{192,128},{256,320},{320,256},{384,448},{4... | collective-permute-start | bytes 3145736 | tf_op jit(solution)/shard_map/ppermute | solution.py:21
  13.8 2.3 %collective-permute-done.1 = f32[4,64,1024]{2,1,0:T(8,128)S(1)} collective-permute-done((f32[4,64,1024]{2,1,0:T(8,128)S(1)}, f32[4,64,1024]{2,1,0:T(8,128)S(1)}, u32[]{:S(2)}, u32[]{:S(2)}) %collective-permute-start.1) | collective-permute-done | bytes 1048608 | tf_op jit(solution)/shard_map/ppermute | solution.py:21
  16.1 1.2 add.29
  17.3 6.5 %all-to-all-start = ((f32[4,64,1024]{2,1,0:T(8,128)}), f32[4,64,1024]{2,1,0:T(8,128)S(1)}, u32[]{:S(2)}, u32[]{:S(2)}) async-start(f32[4,64,1024]{2,1,0:T(8,128)} %add.29), calls=%async_computation | async-start | bytes 2097152 | tf_op jit(solution)/shard_map/all_to_all | solution.py:17
  23.8 4.0 %collective-permute-start.2 = (f32[1,64,128]{2,1,0:T(8,128)S(1)}, f32[1,64,128]{2,1,0:T(8,128)S(1)}, u32[]{:S(2)}, u32[]{:S(2)}) collective-permute-start(f32[1,64,128]{2,1,0:T(8,128)S(1)} %collective-permute-done), channel_id=1, source_target_pairs={{0,8},{1,9},{2,10},{3,11},{4,12},{5,13},{6,14},{7,15},{8,0},{9,1},... | collective-permute-start | bytes 98312 | tf_op jit(solution)/shard_map/ppermute | solution.py:295
  27.8 1.6 %collective-permute-done.2 = f32[1,64,128]{2,1,0:T(8,128)S(1)} collective-permute-done((f32[1,64,128]{2,1,0:T(8,128)S(1)}, f32[1,64,128]{2,1,0:T(8,128)S(1)}, u32[]{:S(2)}, u32[]{:S(2)}) %collective-permute-start.2) | collective-permute-done | bytes 32800 | tf_op jit(solution)/shard_map/ppermute | solution.py:295
  29.4 10.0 %collective-permute-start.5 = (f32[2,64,128]{2,1,0:T(8,128)S(1)}, f32[2,64,128]{2,1,0:T(8,128)S(1)}, u32[]{:S(2)}, u32[]{:S(2)}) collective-permute-start(f32[2,64,128]{2,1,0:T(8,128)S(1)} %constant_dynamic-update-slice_fusion.refs_0_), channel_id=1, source_target_pairs={{0,48},{1,49},{2,50},{3,51},{4,52},{5,53},{6,54},{7,55},{8,56},{9,... | collective-permute-start | bytes 196616 | tf_op jit(solution)/shard_map/ppermute | solution.py:295
  39.4 1.9 %collective-permute-start.4 = (f32[2,64,128]{2,1,0:T(8,128)S(1)}, f32[2,64,128]{2,1,0:T(8,128)S(1)}, u32[]{:S(2)}, u32[]{:S(2)}) collective-permute-start(f32[2,64,128]{2,1,0:T(8,128)S(1)} %constant_dynamic-update-slice_fusion.refs_0_), channel_id=1, source_target_pairs={{0,32},{1,33},{2,34},{3,35},{4,36},{5,37},{6,38},{7,39},{8,40},{9,... | collective-permute-start | bytes 196616 | tf_op jit(solution)/shard_map/ppermute | solution.py:295
  41.3 4.0 %collective-permute-start.3 = (f32[2,64,128]{2,1,0:T(8,128)S(1)}, f32[2,64,128]{2,1,0:T(8,128)S(1)}, u32[]{:S(2)}, u32[]{:S(2)}) collective-permute-start(f32[2,64,128]{2,1,0:T(8,128)S(1)} %constant_dynamic-update-slice_fusion.refs_0_), channel_id=1, source_target_pairs={{0,16},{1,17},{2,18},{3,19},{4,20},{5,21},{6,22},{7,23},{8,24},{9,... | collective-permute-start | bytes 196616 | tf_op jit(solution)/shard_map/ppermute | solution.py:295
  45.3 0.0 collective-permute-done.5.refs_3_
  45.4 3.7 %collective-permute-done.4.refs_2_ = f32[2,64,128]{2,1,0:T(8,128)S(1)} collective-permute-done((f32[2,64,128]{2,1,0:T(8,128)S(1)}, f32[2,64,128]{2,1,0:T(8,128)S(1)}, u32[]{:S(2)}, u32[]{:S(2)}) %collective-permute-start.4) | collective-permute-done | bytes 65568 | tf_op jit(solution)/shard_map/ppermute | solution.py:295
  49.1 0.0 collective-permute-done.3.refs_1_
  49.1 0.0 all-to-all-done.parts
  49.1 0.5 product.1
  49.6 13.2 %all_to_all.25.p_parts = f32[8,32,128]{2,1,0:T(8,128)S(1)} all-to-all(f32[8,32,128]{2,1,0:T(8,128)S(1)} %get-tuple-element.28), channel_id=1, replica_groups=mesh['replica'=8,'mp'=64] {'replica'}, dimensions={0} | all-to-all | bytes 262144 | tf_op jit(solution)/shard_map/all_to_all | solution.py:17
  62.8 0.6 pack.1
  63.3 23.1 %all_to_all.26 = f32[64,9,1,128]{3,2,1,0:T(1,128)S(1)} all-to-all(f32[64,9,1,128]{3,2,1,0:T(1,128)S(1)} %bitcast.24), channel_id=1, replica_groups=mesh['replica'=8,'mp'=64] {'mp'}, dimensions={0} | all-to-all | bytes 589824 | tf_op jit(solution)/shard_map/all_to_all | solution.py:17
  86.5 0.1 total.1
  86.5 18.4 %all_to_all.27 = f32[64,9,1,128]{3,2,1,0:T(1,128)S(1)} all-to-all(f32[64,9,1,128]{3,2,1,0:T(1,128)S(1)} %bitcast.23), channel_id=1, replica_groups=mesh['replica'=8,'mp'=64] {'mp'}, dimensions={0} | all-to-all | bytes 589824 | tf_op jit(solution)/shard_map/all_to_all | solution.py:17
  104.9 0.1 unpack.1
  105.0 0.0 copy-start.4
  105.0 1.0 copy-done.4
  106.0 0.0 copy-start.1
  106.0 0.0 copy-start.3
  106.0 3.6 %all-to-all-start.4 = ((f32[4,8,64,128]{3,2,1,0:T(8,128)}), f32[4,8,64,128]{3,2,1,0:T(8,128)S(1)}, u32[]{:S(2)}, u32[]{:S(2)}) async-start(f32[4,8,64,128]{3,2,1,0:T(8,128)} %copy-done.4), calls=%async_computation.4 | async-start | bytes 2097152 | tf_op jit(solution)/shard_map/all_to_all | solution.py:17
  109.6 0.1 copy.11
  109.7 5.8 %cholesky.17 = f32[64,64]{1,0:T(8,128)S(1)} custom-call(f32[64,64]{1,0:T(8,128)S(1)} %fusion.3), custom_call_target="Cholesky" | custom-call | tf_op jit(solution)/shard_map/jit(cholesky)/cholesky | solution.py:309
  115.6 0.6 compare_reduce_fusion
  116.2 0.7 fusion
  116.9 4.9 %custom-call.6 = f32[1,64,64]{1,2,0:T(8,128)S(1)} custom-call(f32[1,64,64]{2,1,0:T(8,128)S(1)} %fusion), custom_call_target="InvertDiagBlocksLowerTriangular" | custom-call | tf_op jit(solution)/shard_map/triangular_solve | solution.py:310
  121.8 0.2 fusion.1.inverse
  122.0 0.8 factors.1
  122.9 0.0 all-to-all-done.4.mine
  122.9 5.7 %collective-permute-start.6 = (f32[4,8,64,128]{3,2,1,0:T(8,128)S(1)}, f32[4,8,64,128]{3,2,1,0:T(8,128)}, u32[]{:S(2)}, u32[]{:S(2)}) collective-permute-start(f32[4,8,64,128]{3,2,1,0:T(8,128)S(1)} %all-to-all-done.4.mine), channel_id=1, source_target_pairs={{0,64},{64,0},{128,192},{192,128},{256,320},{320,256},{384,448},{4... | collective-permute-start | bytes 3145736 | tf_op jit(solution)/shard_map/ppermute | solution.py:21
  128.6 0.1 pad_add_fusion.place
  128.7 0.0 copy-done.1
  128.7 0.0 copy-done.3
  128.7 2.0 %update_near.1.near = bf16[1,64,8192]{2,1,0:T(8,128)(2,1)} custom-call(s32[4]{0:T(128)S(1)} %pad_add_fusion.place, f32[64,128]{1,0:T(8,128)S(1)} %get-tuple-element.35.weights, f32[4,8,64,128]{3,2,1,0:T(8,128)S(1)} %all-to-all-done.4.mine, bf16[1,64,8192]{2,1,0:T(8,128)(2,1)S(1)} %copy-done.1, bf16[1,64,8192]{2,1,0:T(8,128)(2,1)S(1)} %copy-done.3), custom_call_target="tpu_custom_call" | custom-call | flops 134217728 | bytes 2097152 | tf_op jit(solution)/shard_map/update_near/pallas_call | solution.py:232
  130.7 0.3 collective-permute-done.6.theirs
  131.0 2.6 %update_far.1 = (bf16[1,64,8192]{2,1,0:T(8,128)(2,1)}, f32[64,128]{1,0:T(8,128)}) custom-call(s32[4]{0:T(128)S(1)} %pad_add_fusion.place, f32[64,128]{1,0:T(8,128)S(1)} %get-tuple-element.35.weights, f32[64,64]{1,0:T(8,128)S(1)} %fusion.1.inverse, f32[4,8,64,128]{3,2,1,0:T(8,128)S(1)} %all-to-all-done.4.mine, ...), custom_call_target="tpu_custom_call", output_to_operand_aliasing={{0}: (7, {})} | custom-call | flops 134217728 | bytes 2097152 | tf_op jit(solution)/shard_map/update_far/pallas_call | solution.py:258
  (4 shorter events, 0.0 us)
Async XLA Ops:
  0.6 7.6 %collective-permute-start = (f32[1,64,128]{2,1,0:T(8,128)}, f32[1,64,128]{2,1,0:T(8,128)S(1)}, u32[]{:S(2)}, u32[]{:S(2)}) collective-permute-start(f32[1,64,128]{2,1,0:T(8,128)} %bitcast.25), channel_id=1, source_target_pairs={{0,0},{1,64},{2,128},{3,192},{4,256},{5,320},{6,384},{7,448},{8,8}... | collective-permute-start | bytes 98312 | tf_op jit(solution)/shard_map/ppermute | solution.py:286
  5.2 1.2 copy-start
  6.5 1.2 copy-start.2
  8.3 7.9 %collective-permute-start.1 = (f32[4,64,1024]{2,1,0:T(8,128)S(1)}, f32[4,64,1024]{2,1,0:T(8,128)S(1)}, u32[]{:S(2)}, u32[]{:S(2)}) collective-permute-start(f32[4,64,1024]{2,1,0:T(8,128)S(1)} %get-tuple-element.24), channel_id=1, source_target_pairs={{0,64},{64,0},{128,192},{192,128},{256,320},{320,256},{384,448},{4... | collective-permute-start | bytes 3145736 | tf_op jit(solution)/shard_map/ppermute | solution.py:21
  17.3 31.8 %all-to-all-start = ((f32[4,64,1024]{2,1,0:T(8,128)}), f32[4,64,1024]{2,1,0:T(8,128)S(1)}, u32[]{:S(2)}, u32[]{:S(2)}) async-start(f32[4,64,1024]{2,1,0:T(8,128)} %add.29), calls=%async_computation | async-start | bytes 2097152 | tf_op jit(solution)/shard_map/all_to_all | solution.py:17
  23.8 5.6 %collective-permute-start.2 = (f32[1,64,128]{2,1,0:T(8,128)S(1)}, f32[1,64,128]{2,1,0:T(8,128)S(1)}, u32[]{:S(2)}, u32[]{:S(2)}) collective-permute-start(f32[1,64,128]{2,1,0:T(8,128)S(1)} %collective-permute-done), channel_id=1, source_target_pairs={{0,8},{1,9},{2,10},{3,11},{4,12},{5,13},{6,14},{7,15},{8,0},{9,1},... | collective-permute-start | bytes 98312 | tf_op jit(solution)/shard_map/ppermute | solution.py:295
  29.4 16.0 %collective-permute-start.5 = (f32[2,64,128]{2,1,0:T(8,128)S(1)}, f32[2,64,128]{2,1,0:T(8,128)S(1)}, u32[]{:S(2)}, u32[]{:S(2)}) collective-permute-start(f32[2,64,128]{2,1,0:T(8,128)S(1)} %constant_dynamic-update-slice_fusion.refs_0_), channel_id=1, source_target_pairs={{0,48},{1,49},{2,50},{3,51},{4,52},{5,53},{6,54},{7,55},{8,56},{9,... | collective-permute-start | bytes 196616 | tf_op jit(solution)/shard_map/ppermute | solution.py:295
  39.4 9.7 %collective-permute-start.4 = (f32[2,64,128]{2,1,0:T(8,128)S(1)}, f32[2,64,128]{2,1,0:T(8,128)S(1)}, u32[]{:S(2)}, u32[]{:S(2)}) collective-permute-start(f32[2,64,128]{2,1,0:T(8,128)S(1)} %constant_dynamic-update-slice_fusion.refs_0_), channel_id=1, source_target_pairs={{0,32},{1,33},{2,34},{3,35},{4,36},{5,37},{6,38},{7,39},{8,40},{9,... | collective-permute-start | bytes 196616 | tf_op jit(solution)/shard_map/ppermute | solution.py:295
  41.3 7.8 %collective-permute-start.3 = (f32[2,64,128]{2,1,0:T(8,128)S(1)}, f32[2,64,128]{2,1,0:T(8,128)S(1)}, u32[]{:S(2)}, u32[]{:S(2)}) collective-permute-start(f32[2,64,128]{2,1,0:T(8,128)S(1)} %constant_dynamic-update-slice_fusion.refs_0_), channel_id=1, source_target_pairs={{0,16},{1,17},{2,18},{3,19},{4,20},{5,21},{6,22},{7,23},{8,24},{9,... | collective-permute-start | bytes 196616 | tf_op jit(solution)/shard_map/ppermute | solution.py:295
  105.0 1.0 copy-start.4
  106.0 22.7 %copy-start.1 = (bf16[1,64,8192]{2,1,0:T(8,128)(2,1)S(1)}, bf16[1,64,8192]{2,1,0:T(8,128)(2,1)}, u32[]{:S(2)}) copy-start(bf16[1,64,8192]{2,1,0:T(8,128)(2,1)} %gradient.5) | copy-start | bytes 3145732
  106.0 22.7 %copy-start.3 = (bf16[1,64,8192]{2,1,0:T(8,128)(2,1)S(1)}, bf16[1,64,8192]{2,1,0:T(8,128)(2,1)}, u32[]{:S(2)}) copy-start(bf16[1,64,8192]{2,1,0:T(8,128)(2,1)} %error.5) | copy-start | bytes 3145732
  106.0 16.9 %all-to-all-start.4 = ((f32[4,8,64,128]{3,2,1,0:T(8,128)}), f32[4,8,64,128]{3,2,1,0:T(8,128)S(1)}, u32[]{:S(2)}, u32[]{:S(2)}) async-start(f32[4,8,64,128]{3,2,1,0:T(8,128)} %copy-done.4), calls=%async_computation.4 | async-start | bytes 2097152 | tf_op jit(solution)/shard_map/all_to_all | solution.py:17
  122.9 8.1 %collective-permute-start.6 = (f32[4,8,64,128]{3,2,1,0:T(8,128)S(1)}, f32[4,8,64,128]{3,2,1,0:T(8,128)}, u32[]{:S(2)}, u32[]{:S(2)}) collective-permute-start(f32[4,8,64,128]{3,2,1,0:T(8,128)S(1)} %all-to-all-done.4.mine), channel_id=1, source_target_pairs={{0,64},{64,0},{128,192},{192,128},{256,320},{320,256},{384,448},{4... | collective-permute-start | bytes 3145736 | tf_op jit(solution)/shard_map/ppermute | solution.py:21
